TPU v7x, 32 devices: a whole 2x2x4 slice. The times are simulated.
32 devices in a mesh: ep: 8 (over z, y), tp: 4 (over x, core).
Axes of the slice: x: 2, y: 2, z: 4, core: 2. Of those that a mesh axis runs over, the one named last changes fastest.
Arguments:
- inputs: bfloat16 [8192, 2048], P(('ep', 'tp')), may hold values from -6 to 6
- cotangent: bfloat16 [8192, 2048], P(('ep', 'tp')), may hold values from -6 to 6
- arrangement: int32 [8192], replicated, may hold values from 0 to 8191, as said below
- seq_lengths: int32 [8], replicated, may hold values from 1 to 4096, 8192 in all
- routes: int32 [8192, 8], P(('ep', 'tp')), may hold values from 0 to 31, all different within a row; in each aligned block of 256 rows (0 to 255, 256 to 511, ...) at most 128 rows name the same one
- gate_values: float32 [8192, 8], P(('ep', 'tp')), may hold values from 0.05 to 0.25
- input_gain: float32 [2048], replicated, may hold values from 0.25 to 1.75
- query_proj: bfloat16 [2048, 4096], P(None, 'tp'), may hold values from -0.125 to 0.125
- key_projected: bfloat16 [2048, 512], P(None, 'tp'), may hold values from -0.125 to 0.125
- value_projected: bfloat16 [2048, 512], P(None, 'tp'), may hold values from -0.125 to 0.125
- query_gain: float32 [128], replicated, may hold values from 0.25 to 1.75
- key_gain: float32 [128], replicated, may hold values from 0.25 to 1.75
- output_proj: bfloat16 [4096, 2048], P('tp'), may hold values from -1.5 to 1.5
- expert_gain: float32 [2048], replicated, may hold values from 0.25 to 1.75
- gate_weight: bfloat16 [32, 2048, 768], P(('ep', 'tp')), may hold values from -0.125 to 0.125
- up_weight: bfloat16 [32, 2048, 768], P(('ep', 'tp')), may hold values from -0.125 to 0.125
- down_weight: bfloat16 [32, 768, 2048], P(('ep', 'tp')), may hold values from -0.875 to 0.875
Outputs:
- layer_out: bfloat16 [8192, 2048], P(('ep', 'tp'))
- grad_inputs: float32 [8192, 2048], P(('ep', 'tp'))
- grad_query: float32 [2048, 4096], P('ep', 'tp')
- grad_key: float32 [2048, 512], P('ep', 'tp')
- grad_value: float32 [2048, 512], P('ep', 'tp')
- grad_output: float32 [4096, 2048], P('tp', 'ep')
- grad_input_gain: float32 [2048], replicated
- grad_query_gain: float32 [128], replicated
- grad_key_gain: float32 [128], replicated
- grad_expert_gain: float32 [2048], replicated
- grad_gate: float32 [32, 2048, 768], P(('ep', 'tp'))
- grad_up: float32 [32, 2048, 768], P(('ep', 'tp'))
- grad_down: float32 [32, 768, 2048], P(('ep', 'tp'))
Inputs may be any that keep to these rules, and one draw needn't show every extreme that they name: arrangement holds every given index once. Place t = e * 1024 + j * 256 + s * 32 + b, with b < 32, holds one of the given tokens s * 1024 + j * 256 to s * 1024 + j * 256 + 255. `routes`: within each aligned block of 256 places, no expert is named by more than 128 rows, a bound that some block reaches.
All inputs are finite; a program needn't handle non-finite values.
Results may differ from a plain program's by a relative error of at most 0.025.
Values may be sent and summed in bfloat16 or wider, within the bound.
A program may use at most 384 MiB of HBM per device.

v0:
```python
import jax
import jax.numpy as jnp
from jax import lax
from jax.sharding import PartitionSpec as P

TOP = 8


EPSILON = 1e-06
ROPE_BASE = 1000000.0
NEGATIVE = -1e30
KEY_SPAN = 512
QUERY_BLOCK = 128


def rms_scale(values, gain):
    inverse = lax.rsqrt(jnp.mean(values * values, axis=-1, keepdims=True) + EPSILON)
    return values * inverse * gain


def rotate_half(values):
    half = values.shape[-1] // 2
    return jnp.concatenate([-values[..., half:], values[..., :half]], axis=-1)


def rope_apply(values, cosine, sine):
    return values * cosine + rotate_half(values) * sine


def head_prep(raw_values, gain, cosine, sine):
    return rope_apply(rms_scale(raw_values, gain), cosine, sine)


def rope_tables(positions, head_dim):
    freqs = ROPE_BASE ** (-jnp.arange(0, head_dim, 2, dtype=jnp.float32) / head_dim)
    angles = positions.astype(jnp.float32)[:, None] * freqs[None, :]
    angles = jnp.concatenate([angles, angles], axis=-1)
    return (jnp.cos(angles), jnp.sin(angles))


def seq_info(given, seq_lengths):
    ends = jnp.cumsum(seq_lengths)
    starts = ends - seq_lengths
    seq_ids = jnp.sum((given[:, None] >= ends[None, :]).astype(jnp.int32), axis=1)
    match = seq_ids[:, None] == jnp.arange(seq_lengths.shape[0], dtype=jnp.int32)[None, :]
    firsts = jnp.sum(jnp.where(match, starts[None, :], 0), axis=1)
    return (seq_ids, given - firsts)


def span_mask(query_seq, query_given, key_seq, offset):
    seq_part = lax.dynamic_slice_in_dim(key_seq, offset, KEY_SPAN, 0)
    given_part = offset + jnp.arange(KEY_SPAN, dtype=jnp.int32)
    allowed = (query_seq[:, None] == seq_part[None, :]) & (
        given_part[None, :] <= query_given[:, None]
    )
    return allowed[:, None, :]


def span_range(query_first, query_given, start_offset):
    lowest = query_first[start_offset] // KEY_SPAN
    highest = query_given[start_offset + QUERY_BLOCK - 1] // KEY_SPAN
    return (lowest, highest + 1)


def attend_forward(
    query_matrix, key_all, value_all, query_seq, query_given, query_first, key_seq, score_scale
):
    query_count = query_matrix.shape[0]
    head_count = query_matrix.shape[1]
    head_dim = query_matrix.shape[2]
    blocks = query_count // QUERY_BLOCK

    def block_fn(carry, block_index):
        start_offset = block_index * QUERY_BLOCK
        query_slice = lax.dynamic_slice_in_dim(query_matrix, start_offset, QUERY_BLOCK, 0)
        seq_part = lax.dynamic_slice_in_dim(query_seq, start_offset, QUERY_BLOCK, 0)
        given_part = lax.dynamic_slice_in_dim(query_given, start_offset, QUERY_BLOCK, 0)
        lowest, highest = span_range(query_first, query_given, start_offset)

        def advance(span_index, state):
            running_max, running_sum, running_out = state
            offset = span_index * KEY_SPAN
            key_part = lax.dynamic_slice_in_dim(key_all, offset, KEY_SPAN, 0)
            value_part = lax.dynamic_slice_in_dim(value_all, offset, KEY_SPAN, 0)
            allowed = span_mask(seq_part, given_part, key_seq, offset)
            scores = (
                jnp.einsum("qhd,kd->qhk", query_slice, key_part, preferred_element_type=jnp.float32)
                * score_scale
            )
            new_max = jnp.maximum(
                running_max, jnp.max(jnp.where(allowed, scores, NEGATIVE), axis=-1)
            )
            weights = jnp.where(allowed, jnp.exp(scores - new_max[..., None]), 0.0)
            shrink = jnp.exp(running_max - new_max)
            running_sum = running_sum * shrink + jnp.sum(weights, axis=-1)
            running_out = running_out * shrink[..., None] + jnp.einsum(
                "qhk,kd->qhd",
                weights.astype(jnp.bfloat16),
                value_part,
                preferred_element_type=jnp.float32,
            )
            return (new_max, running_sum, running_out)

        start_state = (
            jnp.full((QUERY_BLOCK, head_count), NEGATIVE, jnp.float32),
            jnp.zeros((QUERY_BLOCK, head_count), jnp.float32),
            jnp.zeros((QUERY_BLOCK, head_count, head_dim), jnp.float32),
        )
        running_max, running_sum, running_out = lax.fori_loop(lowest, highest, advance, start_state)
        return (carry, (running_out / running_sum[..., None], running_max + jnp.log(running_sum)))

    ignored, results = lax.scan(
        block_fn, jnp.zeros((), jnp.int32), jnp.arange(blocks, dtype=jnp.int32)
    )
    outs, log_sums = results
    return (
        outs.reshape(query_count, head_count, head_dim),
        log_sums.reshape(query_count, head_count),
    )


def attend_backward(
    query_matrix,
    key_all,
    value_all,
    query_seq,
    query_given,
    query_first,
    key_seq,
    score_scale,
    out_grad,
    log_sum,
    delta,
):
    query_count = query_matrix.shape[0]
    blocks = query_count // QUERY_BLOCK
    key_total = key_all.shape[0]
    head_dim = key_all.shape[1]

    def block_fn(kv_buffer, block_index):
        start_offset = block_index * QUERY_BLOCK
        query_slice = lax.dynamic_slice_in_dim(query_matrix, start_offset, QUERY_BLOCK, 0)
        seq_part = lax.dynamic_slice_in_dim(query_seq, start_offset, QUERY_BLOCK, 0)
        given_part = lax.dynamic_slice_in_dim(query_given, start_offset, QUERY_BLOCK, 0)
        grad_part = lax.dynamic_slice_in_dim(out_grad, start_offset, QUERY_BLOCK, 0)
        lse_part = lax.dynamic_slice_in_dim(log_sum, start_offset, QUERY_BLOCK, 0)
        delta_part = lax.dynamic_slice_in_dim(delta, start_offset, QUERY_BLOCK, 0)
        lowest, highest = span_range(query_first, query_given, start_offset)

        def advance(span_index, state):
            query_acc, kv_acc = state
            offset = span_index * KEY_SPAN
            key_part = lax.dynamic_slice_in_dim(key_all, offset, KEY_SPAN, 0)
            value_part = lax.dynamic_slice_in_dim(value_all, offset, KEY_SPAN, 0)
            allowed = span_mask(seq_part, given_part, key_seq, offset)
            scores = (
                jnp.einsum("qhd,kd->qhk", query_slice, key_part, preferred_element_type=jnp.float32)
                * score_scale
            )
            probs = jnp.where(allowed, jnp.exp(scores - lse_part[..., None]), 0.0)
            value_grad = jnp.einsum(
                "qhk,qhd->kd",
                probs.astype(jnp.bfloat16),
                grad_part,
                preferred_element_type=jnp.float32,
            )
            prob_grad = jnp.einsum(
                "qhd,kd->qhk", grad_part, value_part, preferred_element_type=jnp.float32
            )
            score_grad = (probs * (prob_grad - delta_part[..., None])).astype(jnp.bfloat16)
            query_acc = query_acc + jnp.einsum(
                "qhk,kd->qhd", score_grad, key_part, preferred_element_type=jnp.float32
            )
            key_grad = (
                jnp.einsum(
                    "qhk,qhd->kd", score_grad, query_slice, preferred_element_type=jnp.float32
                )
                * score_scale
            )
            current = lax.dynamic_slice_in_dim(kv_acc, offset, KEY_SPAN, 0)
            kv_acc = lax.dynamic_update_slice_in_dim(
                kv_acc, current + jnp.concatenate([key_grad, value_grad], axis=1), offset, 0
            )
            return (query_acc, kv_acc)

        start_acc = jnp.zeros(query_slice.shape, jnp.float32)
        query_acc, kv_buffer = lax.fori_loop(lowest, highest, advance, (start_acc, kv_buffer))
        return (kv_buffer, query_acc * score_scale)

    start_buffer = jnp.zeros((key_total, 2 * head_dim), jnp.float32)
    kv_buffer, query_blocks = lax.scan(block_fn, start_buffer, jnp.arange(blocks, dtype=jnp.int32))
    return (query_blocks.reshape(query_matrix.shape), kv_buffer)


def on_device(
    inputs,
    cotangent,
    arrangement,
    seq_lengths,
    routes,
    gate_values,
    input_gain,
    query_proj,
    key_projected,
    value_projected,
    query_gain,
    key_gain,
    output_proj,
    expert_gain,
    gate_weight,
    up_weight,
    down_weight,
):
    ep_size = lax.axis_size("ep")
    tp_size = lax.axis_size("tp")
    ep_index = lax.axis_index("ep")
    tp_index = lax.axis_index("tp")
    own_rows = inputs.shape[0]
    width = inputs.shape[1]
    group_rows = own_rows * tp_size
    row_block = own_rows // ep_size
    head_dim = query_gain.shape[0]
    head_count = query_proj.shape[1] // head_dim
    query_cols = head_count * head_dim
    expert_count = ep_size * tp_size
    capacity = 2 * own_rows * TOP // expert_count
    score_scale = head_dim ** (-0.5)
    token_total = arrangement.shape[0]
    table = arrangement.reshape(ep_size, tp_size, ep_size, row_block)
    table = lax.dynamic_index_in_dim(table, tp_index, 1, keepdims=False)
    table = lax.dynamic_index_in_dim(table, ep_index, 1, keepdims=False)
    send_index = table - (ep_index * group_rows + tp_index * own_rows)
    arrived = (
        lax.all_to_all(inputs[send_index], "ep", split_axis=0, concat_axis=0, tiled=True),
        lax.all_to_all(cotangent[send_index], "ep", split_axis=0, concat_axis=0, tiled=True),
    )
    own_inputs = arrived[0].reshape(own_rows, width)
    own_cot = arrived[1].reshape(own_rows, width).astype(jnp.float32)
    query_given = lax.dynamic_slice_in_dim(arrangement, ep_index * group_rows, group_rows, 0)
    query_seq, query_pos = seq_info(query_given, seq_lengths)
    all_given = jnp.arange(token_total, dtype=jnp.int32)
    key_seq, key_pos = seq_info(all_given, seq_lengths)
    key_order = jnp.zeros((token_total,), jnp.int32).at[arrangement].set(all_given)
    cosine, sine = rope_tables(query_pos, head_dim)
    query_order = jnp.argsort(query_given)
    query_back = (
        jnp.zeros((group_rows,), jnp.int32)
        .at[query_order]
        .set(jnp.arange(group_rows, dtype=jnp.int32))
    )
    sorted_given = query_given[query_order]
    sorted_seq = query_seq[query_order]
    sorted_first = (query_given - query_pos)[query_order]
    slot_expert = routes.reshape(-1)
    hits = (slot_expert[:, None] == jnp.arange(expert_count, dtype=jnp.int32)[None, :]).astype(
        jnp.int32
    )
    slot_rank = jnp.sum((jnp.cumsum(hits, axis=0) - 1) * hits, axis=1)
    slot_gates = gate_values.reshape(-1)[:, None]

    def front_pass(own_x):
        group_x = lax.all_gather(own_x, "tp", axis=0, tiled=True)
        normed_input = rms_scale(group_x.astype(jnp.float32), input_gain).astype(jnp.bfloat16)
        query_raw = jnp.dot(normed_input, query_proj, preferred_element_type=jnp.float32).reshape(
            group_rows, head_count, head_dim
        )
        key_unrotated = jnp.dot(normed_input, key_projected, preferred_element_type=jnp.float32)
        value_row_block = jnp.dot(
            normed_input, value_projected, preferred_element_type=jnp.float32
        ).astype(jnp.bfloat16)
        query_rows = head_prep(query_raw, query_gain, cosine[:, None, :], sine[:, None, :]).astype(
            jnp.bfloat16
        )
        key_rows = head_prep(key_unrotated, key_gain, cosine, sine).astype(jnp.bfloat16)
        key_place, value_place = (
            lax.all_gather(key_rows, "ep", axis=0, tiled=True),
            lax.all_gather(value_row_block, "ep", axis=0, tiled=True),
        )
        key_all = key_place[key_order]
        value_all = value_place[key_order]
        query_sorted = query_rows[query_order]
        out_sorted, log_sum = attend_forward(
            query_sorted,
            key_all,
            value_all,
            sorted_seq,
            sorted_given,
            sorted_first,
            key_seq,
            score_scale,
        )
        out_exact = out_sorted[query_back]
        out_rows = out_exact.astype(jnp.bfloat16).reshape(group_rows, query_cols)
        branch = lax.psum_scatter(
            jnp.dot(out_rows, output_proj, preferred_element_type=jnp.float32).astype(jnp.bfloat16),
            "tp",
            scatter_dimension=0,
            tiled=True,
        ).astype(jnp.float32)
        hidden = own_x.astype(jnp.float32) + branch
        normed_mid = rms_scale(hidden, expert_gain).astype(jnp.bfloat16)
        sending = (
            jnp.zeros((expert_count, capacity, width), jnp.bfloat16)
            .at[slot_expert, slot_rank]
            .set(jnp.repeat(normed_mid, TOP, axis=0))
        )
        received = lax.all_to_all(sending, ("ep", "tp"), split_axis=0, concat_axis=0, tiled=True)
        return (
            normed_input,
            query_raw,
            key_unrotated,
            query_sorted,
            key_all,
            value_all,
            out_exact,
            out_rows,
            log_sum,
            hidden,
            received,
        )

    forward_state = front_pass(own_inputs)
    hidden_first = forward_state[9]
    expert_first = forward_state[10].reshape(-1, width)
    gate_first = jnp.dot(expert_first, gate_weight[0], preferred_element_type=jnp.float32)
    up_first = jnp.dot(expert_first, up_weight[0], preferred_element_type=jnp.float32)
    inner_first = (gate_first * jax.nn.sigmoid(gate_first) * up_first).astype(jnp.bfloat16)
    expert_out = (
        jnp.dot(inner_first, down_weight[0], preferred_element_type=jnp.float32)
        .astype(jnp.bfloat16)
        .reshape(expert_count, capacity, width)
    )
    returned = lax.all_to_all(expert_out, ("ep", "tp"), split_axis=0, concat_axis=0, tiled=True)
    picked = returned[slot_expert, slot_rank].astype(jnp.float32) * slot_gates
    layer_rows = hidden_first + jnp.sum(picked.reshape(own_rows, TOP, width), axis=1)
    again = front_pass(own_inputs)
    (
        normed_input,
        query_raw,
        key_unrotated,
        query_sorted,
        key_all,
        value_all,
        out_exact,
        out_rows,
        log_sum,
        hidden,
        received,
    ) = again
    cot_slots = (slot_gates * jnp.repeat(own_cot, TOP, axis=0)).astype(jnp.bfloat16)
    grad_sending = (
        jnp.zeros((expert_count, capacity, width), jnp.bfloat16)
        .at[slot_expert, slot_rank]
        .set(cot_slots)
    )
    grad_received = lax.all_to_all(
        grad_sending, ("ep", "tp"), split_axis=0, concat_axis=0, tiled=True
    ).reshape(-1, width)
    expert_in = received.reshape(-1, width)
    gate_part = jnp.dot(expert_in, gate_weight[0], preferred_element_type=jnp.float32)
    up_part = jnp.dot(expert_in, up_weight[0], preferred_element_type=jnp.float32)
    gate_sig = jax.nn.sigmoid(gate_part)
    activated = gate_part * gate_sig
    inner = (activated * up_part).astype(jnp.bfloat16)
    contract_rows = (((0,), (0,)), ((), ()))
    contract_cols = (((1,), (1,)), ((), ()))
    grad_down = lax.dot_general(
        inner, grad_received, contract_rows, preferred_element_type=jnp.float32
    )
    inner_grad = lax.dot_general(
        grad_received, down_weight[0], contract_cols, preferred_element_type=jnp.float32
    )
    gate_grad = (inner_grad * up_part * gate_sig * (1.0 + gate_part * (1.0 - gate_sig))).astype(
        jnp.bfloat16
    )
    up_grad = (inner_grad * activated).astype(jnp.bfloat16)
    grad_gate = lax.dot_general(
        expert_in, gate_grad, contract_rows, preferred_element_type=jnp.float32
    )
    grad_up = lax.dot_general(expert_in, up_grad, contract_rows, preferred_element_type=jnp.float32)
    slot_grads = lax.dot_general(
        gate_grad, gate_weight[0], contract_cols, preferred_element_type=jnp.float32
    )
    slot_grads = slot_grads + lax.dot_general(
        up_grad, up_weight[0], contract_cols, preferred_element_type=jnp.float32
    )
    slot_grads = slot_grads.astype(jnp.bfloat16).reshape(expert_count, capacity, width)
    grad_back = lax.all_to_all(slot_grads, ("ep", "tp"), split_axis=0, concat_axis=0, tiled=True)
    mid_grad = jnp.sum(
        grad_back[slot_expert, slot_rank].astype(jnp.float32).reshape(own_rows, TOP, width), axis=1
    )
    mid_scale = lax.rsqrt(jnp.mean(hidden * hidden, axis=-1, keepdims=True) + EPSILON)
    mid_hat = hidden * mid_scale
    grad_expert_gain = jnp.sum(mid_grad * mid_hat, axis=0)
    mid_scaled = mid_grad * expert_gain
    hidden_grad = own_cot + mid_scale * (
        mid_scaled - mid_hat * jnp.mean(mid_scaled * mid_hat, axis=-1, keepdims=True)
    )
    branch_grad = lax.all_gather(hidden_grad.astype(jnp.bfloat16), "tp", axis=0, tiled=True)
    out_grad = lax.dot_general(
        branch_grad, output_proj, contract_cols, preferred_element_type=jnp.float32
    )
    out_grad = out_grad.astype(jnp.bfloat16).reshape(group_rows, head_count, head_dim)
    delta = jnp.sum(out_grad.astype(jnp.float32) * out_exact, axis=-1)
    query_grad_sorted, kv_given = attend_backward(
        query_sorted,
        key_all,
        value_all,
        sorted_seq,
        sorted_given,
        sorted_first,
        key_seq,
        score_scale,
        out_grad[query_order],
        log_sum,
        delta[query_order],
    )
    query_grad = query_grad_sorted[query_back]
    key_value_own = lax.psum_scatter(
        kv_given[arrangement].astype(jnp.bfloat16), "ep", scatter_dimension=0, tiled=True
    ).astype(jnp.float32)
    key_grad = key_value_own[:, :head_dim]
    value_grad = key_value_own[:, head_dim:]
    query_values, query_pull = jax.vjp(
        lambda raw_values, gain: head_prep(raw_values, gain, cosine[:, None, :], sine[:, None, :]),
        query_raw,
        query_gain,
    )
    raw_query_grad, grad_query_gain = query_pull(query_grad)
    key_values, key_pull = jax.vjp(
        lambda raw_values, gain: head_prep(raw_values, gain, cosine, sine), key_unrotated, key_gain
    )
    raw_key_grad, grad_key_gain = key_pull(key_grad)
    combined = jnp.concatenate(
        [
            raw_query_grad.astype(jnp.bfloat16).reshape(group_rows, query_cols),
            raw_key_grad.astype(jnp.bfloat16),
            value_grad.astype(jnp.bfloat16),
        ],
        axis=1,
    )
    stacked_proj = jnp.concatenate([query_proj, key_projected, value_projected], axis=1)
    normed_grad = lax.psum_scatter(
        lax.dot_general(
            combined, stacked_proj, contract_cols, preferred_element_type=jnp.float32
        ).astype(jnp.bfloat16),
        "tp",
        scatter_dimension=0,
        tiled=True,
    ).astype(jnp.float32)
    own_float = own_inputs.astype(jnp.float32)
    in_scale = lax.rsqrt(jnp.mean(own_float * own_float, axis=-1, keepdims=True) + EPSILON)
    in_hat = own_float * in_scale
    grad_input_gain = jnp.sum(normed_grad * in_hat, axis=0)
    in_scaled = normed_grad * input_gain
    input_rows_grad = hidden_grad + in_scale * (
        in_scaled - in_hat * jnp.mean(in_scaled * in_hat, axis=-1, keepdims=True)
    )
    first_part = lax.dot_general(
        normed_input, combined, contract_rows, preferred_element_type=jnp.float32
    )
    second_part = lax.dot_general(
        branch_grad, out_rows, contract_rows, preferred_element_type=jnp.float32
    )
    weight_rows = lax.psum_scatter(
        jnp.concatenate([first_part, second_part], axis=1).astype(jnp.bfloat16),
        "ep",
        scatter_dimension=0,
        tiled=True,
    ).astype(jnp.float32)
    grad_query = weight_rows[:, :query_cols]
    grad_key = weight_rows[:, query_cols : query_cols + head_dim]
    grad_value = weight_rows[:, query_cols + head_dim : query_cols + 2 * head_dim]
    grad_output = jnp.transpose(weight_rows[:, query_cols + 2 * head_dim :])
    gains = lax.psum(
        (grad_input_gain, grad_expert_gain, grad_query_gain, grad_key_gain), ("ep", "tp")
    )
    leaving = (
        lax.all_to_all(
            layer_rows.reshape(ep_size, row_block, width).astype(jnp.bfloat16),
            "ep",
            split_axis=0,
            concat_axis=0,
            tiled=True,
        ).astype(jnp.float32),
        lax.all_to_all(
            input_rows_grad.reshape(ep_size, row_block, width).astype(jnp.bfloat16),
            "ep",
            split_axis=0,
            concat_axis=0,
            tiled=True,
        ).astype(jnp.float32),
    )
    flat_index = send_index.reshape(-1)
    layer_out = (
        jnp.zeros((own_rows, width), jnp.float32)
        .at[flat_index]
        .set(leaving[0].reshape(-1, width))
        .astype(jnp.bfloat16)
    )
    grad_inputs = (
        jnp.zeros((own_rows, width), jnp.float32).at[flat_index].set(leaving[1].reshape(-1, width))
    )
    return (
        layer_out,
        grad_inputs,
        grad_query,
        grad_key,
        grad_value,
        grad_output,
        gains[0],
        gains[2],
        gains[3],
        gains[1],
        grad_gate[None],
        grad_up[None],
        grad_down[None],
    )


def solution(mesh):
    return jax.shard_map(
        on_device,
        mesh=mesh,
        in_specs=(
            P(("ep", "tp"), None),
            P(("ep", "tp"), None),
            P(),
            P(),
            P(("ep", "tp"), None),
            P(("ep", "tp"), None),
            P(),
            P(None, "tp"),
            P(None, "tp"),
            P(None, "tp"),
            P(),
            P(),
            P("tp", None),
            P(),
            P(("ep", "tp"), None, None),
            P(("ep", "tp"), None, None),
            P(("ep", "tp"), None, None),
        ),
        out_specs=(
            P(("ep", "tp"), None),
            P(("ep", "tp"), None),
            P("ep", "tp"),
            P("ep", "tp"),
            P("ep", "tp"),
            P("tp", "ep"),
            P(),
            P(),
            P(),
            P(),
            P(("ep", "tp"), None, None),
            P(("ep", "tp"), None, None),
            P(("ep", "tp"), None, None),
        ),
        check_vma=False,
    )
```

profile of v0, /device:TPU:0, one launch (start us, length us, event | category | flops | bytes accessed | tf_op | source)
XLA Modules:
  0.0 3807.6 jit_solution(10268472925383949238)
XLA Ops:
  259.3 285.6 %while.177 = (s32[]{:T(128)}, f32[8,128,8,128]{3,2,1,0:T(8,128)}, f32[8,128,8]{1,2,0:T(8,128)}, s32[8]{0:T(128)S(1)}, s32[1024]{0:T(1024)S(1)}, /*index=5*/s32[1...) while((s32[]{:T(128)}, f32[8,128,8,128]{3,2,1,0:T(8,128)}, ...), condition=%wide.region_29.30_spmd, body=%wide.region_24.29_spmd.sunk | while | flops 274796064 | bytes 15571008 | solution.py:112
  446.1 37.0 while.181
  495.7 46.2 %while.181 = (s32[]{:T(128)}, f32[128,8]{0,1:T(8,128)S(1)}, f32[128,8]{0,1:T(8,128)S(1)}, f32[128,8,128]{2,0,1:T(8,128)}, s32[]{:T(128)}, /*index=5*/s32[128]{0:...) while((s32[]{:T(128)}, f32[128,8]{0,1:T(8,128)S(1)}, ...), condition=%wide.region_28.28_spmd, body=%wide.region_25.27_spmd.sunk | while | flops 274663936 | bytes 12397827 | solution.py:109
  678.5 347.0 %all-to-all-done.6 = bf16[32,128,2048]{2,1,0:T(8,128)(2,1)} async-done(((bf16[32,128,2048]{2,1,0:T(8,128)(2,1)}), bf16[32,128,2048]{2,1,0:T(8,128)(2,1)}, u32[]{:S(2)}, u32[]{:S(2)}) %all-to-all-start.6) | async-done | bytes 16777248 | tf_op jit(solution)/shard_map/all_to_all | solution.py:307
  1069.1 333.5 %all-to-all-done.5 = bf16[32,128,2048]{2,1,0:T(8,128)(2,1)} async-done(((bf16[32,128,2048]{2,1,0:T(8,128)(2,1)}), bf16[32,128,2048]{2,1,0:T(8,128)(2,1)}, u32[]{:S(2)}, u32[]{:S(2)}) %all-to-all-start.5) | async-done | bytes 16777248 | tf_op jit(solution)/shard_map/all_to_all | solution.py:356
  1483.3 319.4 %while.175 = (s32[]{:T(128)}, bf16[8,128,8,128]{3,2,1,0:T(8,128)(2,1)}, s32[8]{0:T(128)S(1)}, s32[1024]{0:T(1024)}, s32[1024]{0:T(1024)S(1)}, /*index=5*/s32[102...) while((s32[]{:T(128)}, ...), condition=%wide.region_14.15_spmd, body=%wide.region_9.14_spmd.sunk | while | flops 274926112 | bytes 14772276 | solution.py:112
  1691.0 42.8 %while.180 = (s32[]{:T(128)}, f32[128,8]{0,1:T(8,128)S(1)}, f32[128,8]{0,1:T(8,128)S(1)}, f32[128,8,128]{2,0,1:T(8,128)}, s32[]{:T(128)}, /*index=5*/s32[128]{0:...) while((s32[]{:T(128)}, f32[128,8]{0,1:T(8,128)S(1)}, ...), condition=%wide.region_13.13_spmd, body=%wide.region_10.12_spmd.sunk | while | flops 274663936 | bytes 12397827 | solution.py:109
  1747.0 53.6 %while.180 = (s32[]{:T(128)}, f32[128,8]{0,1:T(8,128)S(1)}, f32[128,8]{0,1:T(8,128)S(1)}, f32[128,8,128]{2,0,1:T(8,128)}, s32[]{:T(128)}, /*index=5*/s32[128]{0:...) while((s32[]{:T(128)}, f32[128,8]{0,1:T(8,128)S(1)}, ...), condition=%wide.region_13.13_spmd, body=%wide.region_10.12_spmd.sunk | while | flops 274663936 | bytes 12397827 | solution.py:109
  1821.2 34.7 all-to-all-done.7
  1856.0 50.8 %gather_fusion.11 = bf16[2048,2048]{1,0:T(8,128)(2,1)} fusion(bf16[32,128,2048]{2,1,0:T(8,128)(2,1)} %all-to-all-done.7, s32[2048]{0:T(1024)S(1)} %bitcast.326), kind=kCustom, calls=%fused_computation.11 | custom fusion | bytes 16793600 | tf_op jit(solution)/shard_map/gather | solution.py:390
  1997.2 474.5 %while.179 = (s32[]{:T(128)}, f32[8192,256]{0,1:T(8,128)}, f32[8,128,8,128]{3,2,1,0:T(8,128)}, s32[8]{0:T(128)S(1)}, s32[1024]{0:T(1024)}, /*index=5*/s32[1024]{...) while((s32[]{:T(128)}, f32[8192,256]{0,1:T(8,128)}, ...), condition=%wide.region_41.42_spmd, body=%wide.region_38.41_spmd.sunk | while | flops 675545664 | bytes 24156300 | solution.py:191
  2045.4 34.1 while.182
  2180.7 34.1 while.182
  2231.5 51.1 %while.182 = (s32[]{:T(128)}, f32[128,8,128]{2,0,1:T(8,128)}, f32[8192,256]{0,1:T(8,128)}, s32[]{:T(128)}, s32[128]{0:T(128)S(1)}, /*index=5*/s32[8192]{0:T(1024...) while((s32[]{:T(128)}, f32[128,8,128]{2,0,1:T(8,128)}, ...), condition=%wide.region_40.40_spmd, body=%wide.region_39.39_spmd.sunk | while | flops 675414528 | bytes 19418424 | solution.py:187
  2299.3 68.2 %while.182 = (s32[]{:T(128)}, f32[128,8,128]{2,0,1:T(8,128)}, f32[8192,256]{0,1:T(8,128)}, s32[]{:T(128)}, s32[128]{0:T(128)S(1)}, /*index=5*/s32[8192]{0:T(1024...) while((s32[]{:T(128)}, f32[128,8,128]{2,0,1:T(8,128)}, ...), condition=%wide.region_40.40_spmd, body=%wide.region_39.39_spmd.sunk | while | flops 675414528 | bytes 19418424 | solution.py:187
  2384.2 85.2 %while.182 = (s32[]{:T(128)}, f32[128,8,128]{2,0,1:T(8,128)}, f32[8192,256]{0,1:T(8,128)}, s32[]{:T(128)}, s32[128]{0:T(128)S(1)}, /*index=5*/s32[8192]{0:T(1024...) while((s32[]{:T(128)}, f32[128,8,128]{2,0,1:T(8,128)}, ...), condition=%wide.region_40.40_spmd, body=%wide.region_39.39_spmd.sunk | while | flops 675414528 | bytes 19418424 | solution.py:187
  2478.9 33.7 gather_fusion.15
  2556.2 51.4 %reduce-scatter.10.cloned.1.call-done = bf16[1024,256]{0,1:T(8,128)(2,1)} async-done(((bf16[8192,256]{0,1:T(8,128)(2,1)}), bf16[1024,256]{0,1:T(8,128)(2,1)}) %reduce-scatter.10.cloned.1.call-update) | async-done | bytes 524304 | tf_op jit(solution)/shard_map/reduce_scatter | solution.py:419
  2635.1 42.8 %reduce-scatter.12.cloned.1.call-done = bf16[256,2048]{1,0:T(8,128)(2,1)} async-done(((bf16[1024,2048]{1,0:T(8,128)(2,1)}), bf16[256,2048]{1,0:T(8,128)(2,1)}) %reduce-scatter.12.cloned.1.call-update) | async-done | bytes 1048592 | tf_op jit(solution)/shard_map/reduce_scatter | solution.py:443
  2707.6 368.1 %all_to_all.46 = bf16[32,128,2048]{2,1,0:T(8,128)(2,1)S(1)} all-to-all(bf16[32,128,2048]{2,1,0:T(8,128)(2,1)} %bitcast.330), channel_id=1, replica_groups=mesh['ep'=8,'tp'=4] {'ep','tp'}, dimensions={0} | all-to-all | bytes 33554432 | tf_op jit(solution)/shard_map/all_to_all | solution.py:307
  3098.0 36.5 convolution_convert_fusion
  3190.3 428.8 %all-to-all-done.2 = bf16[32,128,2048]{2,1,0:T(8,128)(2,1)} async-done(((bf16[32,128,2048]{2,1,0:T(8,128)(2,1)}), bf16[32,128,2048]{2,1,0:T(8,128)(2,1)}, u32[]{:S(2)}, u32[]{:S(2)}) %all-to-all-start.2) | async-done | bytes 16777248 | tf_op jit(solution)/shard_map/all_to_all | solution.py:333
  3644.5 50.5 %gather_fusion.8 = bf16[2048,2048]{1,0:T(8,128)(2,1)} fusion(bf16[32,128,2048]{2,1,0:T(8,128)(2,1)} %all-to-all-done.2, s32[2048]{0:T(1024)S(1)} %bitcast.327), kind=kCustom, calls=%fused_computation.8 | custom fusion | bytes 16793600 | tf_op jit(solution)/shard_map/gather | solution.py:334
  3738.3 41.9 %all-reduce.4 = (f32[2048]{0:T(1024)}, f32[128]{0:T(128)}, f32[128]{0:T(128)}, f32[2048]{0:T(1024)}) all-reduce(f32[2048]{0:T(1024)S(1)} %copy-done.52, f32[128]{0:T(128)S(1)} %copy-done.75, f32[128]{0:T(128)S(1)} %copy-done.76, f32[2048]{0:T(1024)S(1)} %copy-done.51), channel_id=1, replica_groups=mesh['ep'=8,'tp'=4] {'ep','tp'}, use_global_device_ids=true, to_apply=%region_50.51 | all-reduce | flops 4352 | bytes 34816 | tf_op jit(solution)/shard_map/psum | solution.py:475
  (2273 shorter events, 2109.5 us)
Async XLA Ops:
  7.2 1043.5 %copy-start = (bf16[1,2048,768]{2,1,0:T(8,128)(2,1)S(1)}, bf16[1,2048,768]{2,1,0:T(8,128)(2,1)}, u32[]{:S(2)}) copy-start(bf16[1,2048,768]{2,1,0:T(8,128)(2,1)} %param.44) | copy-start | bytes 9437188
  7.2 74.6 %all-gather.5.cloned.1.call-start = ((), (), s32[]{:S(2)}) async-start(), calls=%async_computation.14 | async-start | bytes 5242880 | tf_op jit(solution)/shard_map/all_gather | solution.py:262
  14.8 70.2 %copy-start.49 = (f32[2048]{0:T(1024)S(1)}, f32[2048]{0:T(1024)}, u32[]{:S(2)}) copy-start(f32[2048]{0:T(1024)} %param.35) | copy-start | bytes 24580
  48.1 145.0 %all-gather.7.cloned.1.call-start = ((), (), s32[]{:S(2)}) async-start(), calls=%async_computation.15 | async-start | bytes 2359296 | tf_op jit(solution)/shard_map/all_gather | solution.py:276
  85.2 68.8 %copy-start.68 = (f32[1024]{0:T(1024)}, f32[1024]{0:T(1024)S(1)}, u32[]{:S(2)}) copy-start(f32[1024]{0:T(1024)S(1)} %add_rsqrt_fusion.1) | copy-start | bytes 12292
  91.6 135.5 %all-gather.9.cloned.1.call-start = ((), (), s32[]{:S(2)}) async-start(), calls=%async_computation.16 | async-start | bytes 2359296 | tf_op jit(solution)/shard_map/all_gather | solution.py:277
  100.4 520.3 %reduce-scatter.8.cloned.1.call-start = ((), (), s32[]{:S(2)}) async-start(), calls=%async_computation.18 | async-start | bytes 5242880 | tf_op jit(solution)/shard_map/reduce_scatter | solution.py:294
  100.5 80.3 %copy-start.35 = (s32[1024]{0:T(1024)}, s32[1024]{0:T(1024)S(1)}, u32[]{:S(2)}) copy-start(s32[1024]{0:T(1024)S(1)} %get-tuple-element.1436) | copy-start | bytes 12292
  149.9 394.9 %copy-start.46 = (s32[1024]{0:T(1024)}, s32[1024]{0:T(1024)S(1)}, u32[]{:S(2)}) copy-start(s32[1024]{0:T(1024)S(1)} %fusion.134) | copy-start | bytes 12292
  580.7 67.4 %all-to-all-start.4 = ((bf16[8,32,2048]{2,1,0:T(8,128)(2,1)}), bf16[8,32,2048]{2,1,0:T(8,128)(2,1)}, u32[]{:S(2)}, u32[]{:S(2)}) async-start(bf16[8,32,2048]{2,1,0:T(8,128)(2,1)} %bitcast.341), calls=%async_computation.5 | async-start | bytes 2097152 | tf_op jit(solution)/shard_map/all_to_all | solution.py:235
  648.1 377.4 %all-to-all-start.6 = ((bf16[32,128,2048]{2,1,0:T(8,128)(2,1)}), bf16[32,128,2048]{2,1,0:T(8,128)(2,1)}, u32[]{:S(2)}, u32[]{:S(2)}) async-start(bf16[32,128,2048]{2,1,0:T(8,128)(2,1)} %bitcast.329), calls=%async_computation.8 | async-start | bytes 33554432 | tf_op jit(solution)/shard_map/all_to_all | solution.py:307
  1025.5 377.0 %all-to-all-start.5 = ((bf16[32,128,2048]{2,1,0:T(8,128)(2,1)}), bf16[32,128,2048]{2,1,0:T(8,128)(2,1)}, u32[]{:S(2)}, u32[]{:S(2)}) async-start(bf16[32,128,2048]{2,1,0:T(8,128)(2,1)} %bitcast.331), calls=%async_computation.7 | async-start | bytes 33554432 | tf_op jit(solution)/shard_map/all_to_all | solution.py:356
  1479.2 376.8 %all-to-all-start.7 = ((bf16[32,128,2048]{2,1,0:T(8,128)(2,1)}), bf16[32,128,2048]{2,1,0:T(8,128)(2,1)}, u32[]{:S(2)}, u32[]{:S(2)}) async-start(bf16[32,128,2048]{2,1,0:T(8,128)(2,1)} %bitcast.332), calls=%async_computation.9 | async-start | bytes 33554432 | tf_op jit(solution)/shard_map/all_to_all | solution.py:388
  1483.2 434.9 %reduce-scatter.6.cloned.1.call-start = ((), (), s32[]{:S(2)}) async-start(), calls=%async_computation.17 | async-start | bytes 5242880 | tf_op jit(solution)/shard_map/reduce_scatter | solution.py:294
  1483.3 319.4 %copy-start.47 = (s32[1024]{0:T(1024)S(1)}, s32[1024]{0:T(1024)}, u32[]{:S(2)}) copy-start(s32[1024]{0:T(1024)} %copy-done.46) | copy-start | bytes 12292
  1821.2 135.6 %all-gather.11.cloned.1.call-start = ((), (), s32[]{:S(2)}) async-start(), calls=%async_computation.19 | async-start | bytes 5242880 | tf_op jit(solution)/shard_map/all_gather | solution.py:399
  1926.3 681.3 %reduce-scatter.10.cloned.1.call-start = ((), (), s32[]{:S(2)}) async-start(), calls=%async_computation.20 | async-start | bytes 4718592 | tf_op jit(solution)/shard_map/reduce_scatter | solution.py:419
  2519.0 158.9 %reduce-scatter.12.cloned.1.call-start = ((), (), s32[]{:S(2)}) async-start(), calls=%async_computation.21 | async-start | bytes 5242880 | tf_op jit(solution)/shard_map/reduce_scatter | solution.py:443
  2554.3 63.0 %copy-start.58 = (f32[1024]{0:T(1024)S(1)}, f32[1024]{0:T(1024)}, u32[]{:S(2)}) copy-start(f32[1024]{0:T(1024)} %copy-done.57) | copy-start | bytes 12292
  2707.6 373.8 %copy-start.80 = (bf16[1,2048,768]{2,1,0:T(8,128)(2,1)S(1)}, bf16[1,2048,768]{2,1,0:T(8,128)(2,1)}, u32[]{:S(2)}) copy-start(bf16[1,2048,768]{2,1,0:T(8,128)(2,1)} %param.43) | copy-start | bytes 9437188
  3134.5 484.7 %all-to-all-start.2 = ((bf16[32,128,2048]{2,1,0:T(8,128)(2,1)}), bf16[32,128,2048]{2,1,0:T(8,128)(2,1)}, u32[]{:S(2)}, u32[]{:S(2)}) async-start(bf16[32,128,2048]{2,1,0:T(8,128)(2,1)} %bitcast.333), calls=%async_computation.3 | async-start | bytes 33554432 | tf_op jit(solution)/shard_map/all_to_all | solution.py:333
  3138.9 645.4 %reduce-scatter.14.cloned.1.call-start = ((), (), s32[]{:S(2)}) async-start(), calls=%async_computation.22 | async-start | bytes 10616832 | tf_op jit(solution)/shard_map/reduce_scatter | solution.py:465
  3619.2 92.0 %all-to-all-start.8 = ((bf16[8,32,2048]{2,1,0:T(8,128)(2,1)}), bf16[8,32,2048]{2,1,0:T(8,128)(2,1)}, u32[]{:S(2)}, u32[]{:S(2)}) async-start(bf16[8,32,2048]{2,1,0:T(8,128)(2,1)} %bitcast.340), calls=%async_computation.12 | async-start | bytes 2097152 | tf_op jit(solution)/shard_map/all_to_all | solution.py:486
  3711.1 82.7 %all-to-all-start.3 = ((bf16[8,32,2048]{2,1,0:T(8,128)(2,1)}), bf16[8,32,2048]{2,1,0:T(8,128)(2,1)}, u32[]{:S(2)}, u32[]{:S(2)}) async-start(bf16[8,32,2048]{2,1,0:T(8,128)(2,1)} %bitcast.342), calls=%async_computation.4 | async-start | bytes 2097152 | tf_op jit(solution)/shard_map/all_to_all | solution.py:479
  (347 other events, 1671.7 us)
Sparse Core Ops, SparseCore 0:
  48.3 33.4 all-gather.4
  91.7 49.2 all-gather.6
  143.2 47.7 all-gather.8
  576.1 44.5 reduce-scatter.7
  1821.3 45.6 reduce-scatter.5
  1926.4 30.3 all-gather.10
  2519.1 88.4 reduce-scatter.9
  2633.6 44.2 reduce-scatter.11
  3165.9 371.8 reduce-scatter.13
where the time goes:
time: 3840 us; the launch traced here: 3810 us
  waiting for transfers between devices  1320 us (34%)
  matrix products  767 us (20%)
  local copies, waits for them, and re-layouts  722 us (19%)
  blocking collectives  443 us (12%)
  other arithmetic  358 us (9%)
  loops' own time  151 us (4%)
    all_to_all x1, waiting for transfers between devices, on_device(): lax.all_to_all(expert_out, ('ep', 'tp'), split_axis=0, concat_axis=0, til...  429 us
    all_to_all x1, blocking collectives, front_pass(): lax.all_to_all(sending, ('ep', 'tp'), split_axis=0, concat_axis=0, tiled=...  368 us
    all_to_all x1, waiting for transfers between devices, front_pass(): lax.all_to_all(sending, ('ep', 'tp'), split_axis=0, concat_axis=0, tiled=...  347 us
    all_to_all x1, waiting for transfers between devices, on_device(): lax.all_to_all(grad_sending, ('ep', 'tp'), split_axis=0, concat_axis=0, t...  333 us
    dot_general x120, matrix products, advance(): jnp.einsum('qhd,kd->qhk', query_slice, key_part, preferred_element_type=j...  173 us
    dot_general x80, matrix products, advance(): jnp.einsum('qhk,kd->qhd', weights.astype(jnp.bfloat16), value_part, prefe...  134 us
    another operation x2, loops' own time, attend_forward(): lax.scan(block_fn, jnp.zeros((), jnp.int32), jnp.arange(blocks, dtype=jnp...  94.8 us
    dynamic_update_slice x40, other arithmetic, advance(): lax.dynamic_update_slice_in_dim(kv_acc, current + jnp.concatenate([key_gr...  85.4 us
  transfers between devices with their start and end apart: 16, of which 9 were waited for; matrix products, arithmetic and copies ran while one was open for 20% of the time, Pallas kernels for 0%

commit v1 on v0

v1 whole, which is shorter than its diff:
```python
import math

import jax
import jax.numpy as jnp
from jax import lax
from jax.experimental import pallas as pl
from jax.experimental.pallas import tpu as pltpu
from jax.sharding import PartitionSpec as P

TOP = 8
EPSILON = 1e-06
ROPE_BASE = 1000000.0
KEY_SPAN = 512
QUERY_TOKENS = 32
HEAD = 128
ROW_TILE = 256
MIB = 1 << 20
LOG2E = math.log2(math.e)
ROWS_BY_ROWS = (((0,), (0,)), ((), ()))
COLS_BY_COLS = (((1,), (1,)), ((), ()))


def dot(left, right):
    return jnp.dot(left, right, preferred_element_type=jnp.float32)


def dot_with(left, right, dims):
    return lax.dot_general(left, right, dims, preferred_element_type=jnp.float32)


def cost(flops, moved, transcendentals=0):
    return pl.CostEstimate(
        flops=int(flops), bytes_accessed=int(moved), transcendentals=int(transcendentals)
    )


def params(mib):
    return pltpu.CompilerParams(
        dimension_semantics=("arbitrary",), vmem_limit_bytes=mib * MIB
    )


def whole(shape, single=True):
    rank = len(shape)
    if single:
        return pl.BlockSpec(shape, lambda *ids: (0,) * rank, pipeline_mode=pl.Buffered(1))
    return pl.BlockSpec(shape, lambda *ids: (0,) * rank)


def rows_of(shape):
    rank = len(shape)
    return pl.BlockSpec(shape, lambda i, *ids: (i,) + (0,) * (rank - 1))


def rope_tables(positions, head_dim):
    freqs = ROPE_BASE ** (-jnp.arange(0, head_dim, 2, dtype=jnp.float32) / head_dim)
    angles = positions.astype(jnp.float32)[:, None] * freqs[None, :]
    cosine, sine = jnp.cos(angles), jnp.sin(angles)
    return (
        jnp.concatenate([cosine, cosine], axis=-1),
        jnp.concatenate([-sine, sine], axis=-1),
    )


def seq_starts(given, seq_lengths):
    ends = jnp.cumsum(seq_lengths)
    passed = given[:, None] >= ends[None, :]
    return jnp.sum(jnp.where(passed, seq_lengths[None, :], 0), axis=1)


def inverse_root(values):
    return lax.rsqrt(jnp.mean(values * values, axis=-1, keepdims=True) + EPSILON)


def front_kernel(
    x_ref, gain_ref, wq_ref, wk_ref, wv_ref, qg_ref, kg_ref, cos_ref, sin_ref,
    normed_ref, qraw_ref, q_ref, kraw_ref, kv_ref,
):
    x = x_ref[...].astype(jnp.float32)
    normed = (x * inverse_root(x) * gain_ref[...]).astype(jnp.bfloat16)
    normed_ref[...] = normed
    cosine, sine = cos_ref[...], sin_ref[...]

    def prepare(raw, gain):
        values = raw * inverse_root(raw) * gain
        return (values * cosine + pltpu.roll(values, HEAD // 2, 1) * sine).astype(jnp.bfloat16)

    raw = dot(normed, wq_ref[...])
    qraw_ref[...] = raw
    for head in range(raw.shape[1] // HEAD):
        part = slice(head * HEAD, (head + 1) * HEAD)
        q_ref[:, part] = prepare(raw[:, part], qg_ref[...])
    raw = dot(normed, wk_ref[...])
    kraw_ref[...] = raw
    kv_ref[:, :HEAD] = prepare(raw, kg_ref[...])
    kv_ref[:, HEAD:] = dot(normed, wv_ref[...]).astype(jnp.bfloat16)


def front(group_x, input_gain, wq, wk, wv, query_gain, key_gain, cosine, sine):
    rows, width = group_x.shape
    cols = wq.shape[1]
    tile = min(ROW_TILE, rows)
    out = [
        ((rows, width), jnp.bfloat16),
        ((rows, cols), jnp.float32),
        ((rows, cols), jnp.bfloat16),
        ((rows, HEAD), jnp.float32),
        ((rows, 2 * HEAD), jnp.bfloat16),
    ]
    return pl.pallas_call(
        front_kernel,
        grid=(rows // tile,),
        in_specs=[
            rows_of((tile, width)),
            whole((1, width)),
            whole(wq.shape),
            whole(wk.shape),
            whole(wv.shape),
            whole((1, HEAD)),
            whole((1, HEAD)),
            rows_of((tile, HEAD)),
            rows_of((tile, HEAD)),
        ],
        out_specs=[rows_of((tile, shape[1])) for shape, kind in out],
        out_shape=[jax.ShapeDtypeStruct(shape, kind) for shape, kind in out],
        compiler_params=params(40),
        cost_estimate=cost(2 * rows * width * (cols + 2 * HEAD), 20 * MIB),
        name="front",
    )(
        group_x,
        input_gain[None],
        wq,
        wk,
        wv,
        query_gain[None],
        key_gain[None],
        cosine,
        sine,
    )


def stack_heads(block):
    heads = block.shape[1] // HEAD
    return jnp.concatenate(
        [block[:, head * HEAD : (head + 1) * HEAD] for head in range(heads)], axis=0
    )


def attend_forward_kernel(
    bounds_ref, q_ref, ask_ref, key_given_ref, kv_ref, exact_ref, out_ref, lse_ref, acc, tot
):
    step = pl.program_id(0)
    tokens, cols = q_ref.shape
    heads = cols // HEAD
    query = stack_heads(q_ref[...])
    ask = ask_ref[...]
    last = jnp.concatenate([ask[:, 0:1]] * heads, axis=0)
    first = jnp.concatenate([ask[:, 1:2]] * heads, axis=0)
    acc[...] = jnp.zeros_like(acc)
    tot[...] = jnp.zeros_like(tot)

    def visit(span, masked):
        offset = pl.multiple_of(span * KEY_SPAN, KEY_SPAN)
        keys = kv_ref[pl.ds(offset, KEY_SPAN), :HEAD]
        values = kv_ref[pl.ds(offset, KEY_SPAN), HEAD:]
        scores = dot_with(query, keys, COLS_BY_COLS)
        weights = jnp.exp2(scores * (HEAD**-0.5 * LOG2E))
        if masked:
            key_given = key_given_ref[:, pl.ds(offset, KEY_SPAN)]
            weights = jnp.where((key_given <= last) & (key_given >= first), weights, 0.0)
        part = weights[:, :HEAD]
        for chunk in range(1, KEY_SPAN // HEAD):
            part = part + weights[:, chunk * HEAD : (chunk + 1) * HEAD]
        tot[...] += part
        acc[...] += dot(weights.astype(jnp.bfloat16), values)

    lowest, open_low = bounds_ref[0, step], bounds_ref[1, step]
    open_high, highest = bounds_ref[2, step], bounds_ref[3, step]

    @pl.loop(lowest, open_low)
    def _(span):
        visit(span, True)

    @pl.loop(open_low, open_high)
    def _(span):
        visit(span, False)

    @pl.loop(open_high, highest)
    def _(span):
        visit(span, True)

    total = tot[...]
    exact = acc[...] / jnp.sum(total, axis=1, keepdims=True)
    for head in range(heads):
        rows = exact[head * tokens : (head + 1) * tokens]
        exact_ref[:, head * HEAD : (head + 1) * HEAD] = rows
        out_ref[:, head * HEAD : (head + 1) * HEAD] = rows.astype(jnp.bfloat16)
    lse_ref[0] = jnp.log2(jnp.sum(total.T, axis=0, keepdims=True))


def attend_forward(bounds, query, ask, key_given, kv, pairs):
    rows, cols = query.shape
    heads = cols // HEAD
    steps = rows // QUERY_TOKENS
    stacked = heads * QUERY_TOKENS
    return pl.pallas_call(
        attend_forward_kernel,
        grid_spec=pltpu.PrefetchScalarGridSpec(
            num_scalar_prefetch=1,
            grid=(steps,),
            in_specs=[
                rows_of((QUERY_TOKENS, cols)),
                rows_of((QUERY_TOKENS, 2)),
                whole(key_given.shape),
                whole(kv.shape),
            ],
            out_specs=[
                rows_of((QUERY_TOKENS, cols)),
                rows_of((QUERY_TOKENS, cols)),
                rows_of((1, 1, stacked)),
            ],
            scratch_shapes=[
                pltpu.VMEM((stacked, HEAD), jnp.float32),
                pltpu.VMEM((stacked, HEAD), jnp.float32),
            ],
        ),
        out_shape=[
            jax.ShapeDtypeStruct((rows, cols), jnp.float32),
            jax.ShapeDtypeStruct((rows, cols), jnp.bfloat16),
            jax.ShapeDtypeStruct((steps, 1, stacked), jnp.float32),
        ],
        compiler_params=params(48),
        cost_estimate=cost(8 * pairs * HEAD, 16 * MIB, pairs),
        name="attend_forward",
    )(bounds, query, ask, key_given, kv)


def attend_backward_kernel(
    bounds_ref, q_ref, grad_ref, exact_ref, lse_ref, ask_ref, key_given_ref, kv_ref,
    dq_ref, dkv_ref, acc,
):
    step = pl.program_id(0)
    tokens, cols = q_ref.shape
    heads = cols // HEAD

    @pl.when(step == 0)
    def _():
        dkv_ref[...] = jnp.zeros_like(dkv_ref)

    query = stack_heads(q_ref[...])
    grad = stack_heads(grad_ref[...])
    product = grad.astype(jnp.float32) * stack_heads(exact_ref[...])
    delta = jnp.sum(product.T, axis=0, keepdims=True)
    lse = lse_ref[0]
    last, first = ask_ref[0, 0:1, :], ask_ref[0, 1:2, :]
    acc[...] = jnp.zeros_like(acc)

    def visit(span, masked):
        offset = pl.multiple_of(span * KEY_SPAN, KEY_SPAN)
        place = pl.ds(offset, KEY_SPAN)
        keys = kv_ref[place, :HEAD]
        values = kv_ref[place, HEAD:]
        scores = dot_with(keys, query, COLS_BY_COLS)
        probs = jnp.exp2(scores * (HEAD**-0.5 * LOG2E) - lse)
        if masked:
            key_given = key_given_ref[place, :]
            probs = jnp.where((key_given <= last) & (key_given >= first), probs, 0.0)
        prob_grad = dot_with(values, grad, COLS_BY_COLS)
        score_grad = (probs * (prob_grad - delta)).astype(jnp.bfloat16)
        dkv_ref[place, HEAD:] += dot(probs.astype(jnp.bfloat16), grad)
        dkv_ref[place, :HEAD] += dot(score_grad, query) * (HEAD**-0.5)
        acc[...] += dot_with(score_grad, keys, ROWS_BY_ROWS)

    lowest, open_low = bounds_ref[0, step], bounds_ref[1, step]
    open_high, highest = bounds_ref[2, step], bounds_ref[3, step]

    @pl.loop(lowest, open_low)
    def _(span):
        visit(span, True)

    @pl.loop(open_low, open_high)
    def _(span):
        visit(span, False)

    @pl.loop(open_high, highest)
    def _(span):
        visit(span, True)

    for head in range(heads):
        dq_ref[:, head * HEAD : (head + 1) * HEAD] = acc[
            head * tokens : (head + 1) * tokens
        ] * (HEAD**-0.5)


def attend_backward(bounds, query, grad, exact, lse, ask_rows, key_column, kv, pairs):
    rows, cols = query.shape
    heads = cols // HEAD
    steps = rows // QUERY_TOKENS
    stacked = heads * QUERY_TOKENS
    return pl.pallas_call(
        attend_backward_kernel,
        grid_spec=pltpu.PrefetchScalarGridSpec(
            num_scalar_prefetch=1,
            grid=(steps,),
            in_specs=[
                rows_of((QUERY_TOKENS, cols)),
                rows_of((QUERY_TOKENS, cols)),
                rows_of((QUERY_TOKENS, cols)),
                rows_of((1, 1, stacked)),
                rows_of((1, 2, stacked)),
                whole(key_column.shape),
                whole(kv.shape),
            ],
            out_specs=[rows_of((QUERY_TOKENS, cols)), whole(kv.shape)],
            scratch_shapes=[pltpu.VMEM((stacked, HEAD), jnp.float32)],
        ),
        out_shape=[
            jax.ShapeDtypeStruct((rows, cols), jnp.float32),
            jax.ShapeDtypeStruct(kv.shape, jnp.float32),
        ],
        compiler_params=params(56),
        cost_estimate=cost(20 * pairs * HEAD, 32 * MIB, pairs),
        name="attend_backward",
    )(bounds, query, grad, exact, lse, ask_rows, key_column, kv)


def selection(meta, expert, capacity):
    tokens = meta.shape[1]
    weight = jnp.sum(jnp.where(meta[:TOP] == expert, meta[TOP:], 0.0), axis=0, keepdims=True)
    member = jnp.where(weight > 0.0, 1.0, 0.0)
    earlier = lax.broadcasted_iota(jnp.int32, (tokens, tokens), 0)
    later = lax.broadcasted_iota(jnp.int32, (tokens, tokens), 1)
    before = jnp.where(earlier < later, 1.0, 0.0).astype(jnp.bfloat16)
    rank = dot(jnp.broadcast_to(member, (16, tokens)).astype(jnp.bfloat16), before)[0:1]
    rank = jnp.where(weight > 0.0, rank, -1.0).astype(jnp.int32)
    hit = lax.broadcasted_iota(jnp.int32, (capacity, tokens), 0) == rank
    gate = jnp.sum(jnp.where(hit, weight, 0.0), axis=1, keepdims=True)
    return jnp.where(hit, 1.0, 0.0).astype(jnp.bfloat16), gate


def expert_kernel(
    expert_ref, meta_ref, x_ref, c_ref, wg_ref, wu_ref, wd_ref,
    mid_ref, xs_ref, cs_ref, inner_ref, gg_ref, ug_ref,
):
    blocks, _, tokens = meta_ref.shape
    capacity = xs_ref.shape[0] // blocks
    expert = expert_ref[0].astype(jnp.float32)
    picks = []
    for block in range(blocks):
        rows = slice(block * tokens, (block + 1) * tokens)
        slots = slice(block * capacity, (block + 1) * capacity)
        pick, gate = selection(meta_ref[block], expert, capacity)
        picks.append(pick)
        xs_ref[slots] = dot(pick, x_ref[rows]).astype(jnp.bfloat16)
        cs_ref[slots] = (dot(pick, c_ref[rows]) * gate).astype(jnp.bfloat16)
    gate_part = dot(xs_ref[...], wg_ref[0])
    up_part = dot(xs_ref[...], wu_ref[0])
    inner_grad = dot_with(cs_ref[...], wd_ref[0], COLS_BY_COLS)
    gate_sig = jax.nn.sigmoid(gate_part)
    activated = gate_part * gate_sig
    inner_ref[...] = (activated * up_part).astype(jnp.bfloat16)
    gate_grad = (inner_grad * up_part * gate_sig * (1.0 + gate_part * (1.0 - gate_sig))).astype(
        jnp.bfloat16
    )
    up_grad = (inner_grad * activated).astype(jnp.bfloat16)
    gg_ref[...] = gate_grad
    ug_ref[...] = up_grad
    slot_grad = dot_with(gate_grad, wg_ref[0], COLS_BY_COLS)
    slot_grad = (slot_grad + dot_with(up_grad, wu_ref[0], COLS_BY_COLS)).astype(jnp.bfloat16)
    for block in range(blocks):
        rows = slice(block * tokens, (block + 1) * tokens)
        slots = slice(block * capacity, (block + 1) * capacity)
        mid_ref[rows] = dot_with(picks[block], slot_grad[slots], ROWS_BY_ROWS).astype(
            jnp.bfloat16
        )


def expert_pass(expert, meta, x_all, c_all, gate_w, up_w, down_w, capacity):
    blocks, lines, tokens = meta.shape
    width, hidden = gate_w.shape[1:]
    per = max(1, 512 // tokens)
    total = blocks * capacity
    slots = per * capacity
    shapes = [(blocks * tokens, width)] + [(total, width)] * 2 + [(total, hidden)] * 3
    return pl.pallas_call(
        expert_kernel,
        grid_spec=pltpu.PrefetchScalarGridSpec(
            num_scalar_prefetch=1,
            grid=(blocks // per,),
            in_specs=[
                rows_of((per, lines, tokens)),
                rows_of((per * tokens, width)),
                rows_of((per * tokens, width)),
                whole(gate_w.shape),
                whole(up_w.shape),
                whole(down_w.shape),
            ],
            out_specs=[rows_of((per * tokens, width))]
            + [rows_of((slots, width))] * 2
            + [rows_of((slots, hidden))] * 3,
        ),
        out_shape=[jax.ShapeDtypeStruct(shape, jnp.bfloat16) for shape in shapes],
        compiler_params=params(56),
        cost_estimate=cost(10 * total * width * hidden, 150 * MIB, total * hidden),
        name="expert_pass",
    )(expert, meta, x_all, c_all, gate_w, up_w, down_w)


def down_kernel(expert_ref, meta_ref, inner_ref, wd_ref, out_ref):
    blocks, _, tokens = meta_ref.shape
    capacity = inner_ref.shape[0] // blocks
    expert = expert_ref[0].astype(jnp.float32)
    result = dot(inner_ref[...], wd_ref[0]).astype(jnp.bfloat16).astype(jnp.float32)
    for block in range(blocks):
        pick, gate = selection(meta_ref[block], expert, capacity)
        slots = slice(block * capacity, (block + 1) * capacity)
        scaled = (result[slots] * gate).astype(jnp.bfloat16)
        out_ref[block * tokens : (block + 1) * tokens] = dot_with(
            pick, scaled, ROWS_BY_ROWS
        ).astype(jnp.bfloat16)


def down_pass(expert, meta, inner, down_w):
    blocks, lines, tokens = meta.shape
    total, hidden = inner.shape
    width = down_w.shape[2]
    per = max(1, 512 // tokens)
    slots = per * (total // blocks)
    return pl.pallas_call(
        down_kernel,
        grid_spec=pltpu.PrefetchScalarGridSpec(
            num_scalar_prefetch=1,
            grid=(blocks // per,),
            in_specs=[
                rows_of((per, lines, tokens)),
                rows_of((slots, hidden)),
                whole(down_w.shape),
            ],
            out_specs=rows_of((per * tokens, width)),
        ),
        out_shape=jax.ShapeDtypeStruct((blocks * tokens, width), jnp.bfloat16),
        compiler_params=params(40),
        cost_estimate=cost(2 * total * width * hidden, 40 * MIB),
        name="down_pass",
    )(expert, meta, inner, down_w)


def head_back_kernel(raw_ref, grad_ref, gain_ref, cos_ref, sin_ref, out_ref, gain_grad_ref):
    @pl.when(pl.program_id(0) == 0)
    def _():
        gain_grad_ref[...] = jnp.zeros_like(gain_grad_ref)

    cosine, sine, gain = cos_ref[...], sin_ref[...], gain_ref[...]
    for head in range(raw_ref.shape[1] // HEAD):
        part = slice(head * HEAD, (head + 1) * HEAD)
        raw = raw_ref[:, part]
        grad = grad_ref[:, part].astype(jnp.float32)
        back = grad * cosine - pltpu.roll(grad, HEAD // 2, 1) * sine
        inverse = inverse_root(raw)
        hat = raw * inverse
        gain_grad_ref[...] += jnp.sum(back * hat, axis=0, keepdims=True)
        scaled = back * gain
        out_ref[:, part] = (
            inverse * (scaled - hat * jnp.mean(scaled * hat, axis=-1, keepdims=True))
        ).astype(jnp.bfloat16)


def head_back(raw, grad, gain, cosine, sine):
    rows, cols = raw.shape
    tile = min(ROW_TILE, rows)
    return pl.pallas_call(
        head_back_kernel,
        grid=(rows // tile,),
        in_specs=[
            rows_of((tile, cols)),
            rows_of((tile, cols)),
            whole((1, HEAD)),
            rows_of((tile, HEAD)),
            rows_of((tile, HEAD)),
        ],
        out_specs=[rows_of((tile, cols)), whole((1, HEAD))],
        out_shape=[
            jax.ShapeDtypeStruct((rows, cols), jnp.bfloat16),
            jax.ShapeDtypeStruct((1, HEAD), jnp.float32),
        ],
        compiler_params=params(24),
        cost_estimate=cost(rows * cols * 20, rows * cols * 10),
        name="head_back",
    )(raw, grad, gain[None], cosine, sine)


def on_device(
    inputs,
    cotangent,
    arrangement,
    seq_lengths,
    routes,
    gate_values,
    input_gain,
    query_proj,
    key_projected,
    value_projected,
    query_gain,
    key_gain,
    output_proj,
    expert_gain,
    gate_weight,
    up_weight,
    down_weight,
):
    ep_size = lax.axis_size("ep")
    tp_size = lax.axis_size("tp")
    ep_index = lax.axis_index("ep")
    tp_index = lax.axis_index("tp")
    everyone = ("ep", "tp")
    own_rows, width = inputs.shape
    group_rows = own_rows * tp_size
    row_block = own_rows // ep_size
    token_total = arrangement.shape[0]
    expert_count = ep_size * tp_size
    capacity = 2 * own_rows * TOP // expert_count
    heads = query_proj.shape[1] // HEAD
    expert = (ep_index * tp_size + tp_index).astype(jnp.int32)[None]

    table = arrangement.reshape(ep_size, tp_size, ep_size, row_block)
    leaving_from = lax.dynamic_index_in_dim(table, tp_index, 1, keepdims=False)
    leaving_from = lax.dynamic_index_in_dim(leaving_from, ep_index, 1, keepdims=False)
    send_index = leaving_from - (ep_index * group_rows + tp_index * own_rows)
    mover = (
        send_index.reshape(-1)[:, None] == jnp.arange(own_rows, dtype=jnp.int32)[None, :]
    ).astype(jnp.bfloat16)

    def to_places(rows):
        moved = dot(mover, rows).astype(jnp.bfloat16).reshape(ep_size, row_block, width)
        return lax.all_to_all(moved, "ep", split_axis=0, concat_axis=0, tiled=True).reshape(
            own_rows, width
        )

    def to_given(rows):
        moved = lax.all_to_all(
            rows.astype(jnp.bfloat16).reshape(ep_size, row_block, width),
            "ep",
            split_axis=0,
            concat_axis=0,
            tiled=True,
        ).reshape(own_rows, width)
        return dot_with(mover, moved, ROWS_BY_ROWS)

    def group_sorted(rows):
        gathered = lax.all_gather(rows, "tp", axis=0, tiled=True)
        gathered = gathered.reshape(tp_size, ep_size, row_block, rows.shape[1])
        return jnp.swapaxes(gathered, 0, 1).reshape(group_rows, rows.shape[1])

    def scatter_group(rows):
        placed = rows.reshape(ep_size, tp_size, row_block, rows.shape[1])
        placed = jnp.swapaxes(placed, 0, 1).reshape(group_rows, rows.shape[1])
        return lax.psum_scatter(placed, "tp", scatter_dimension=0, tiled=True)

    own_inputs = to_places(inputs)
    own_cot = to_places(cotangent)
    meta_own = jnp.concatenate([routes.astype(jnp.float32).T, gate_values.T], axis=0)
    meta = lax.all_gather(meta_own, everyone, axis=0, tiled=False)
    cot_all = lax.all_gather(own_cot, everyone, axis=0, tiled=True)

    query_given = lax.dynamic_index_in_dim(table, ep_index, 0, keepdims=False)
    query_given = jnp.swapaxes(query_given, 0, 1).reshape(group_rows)
    query_first = seq_starts(query_given, seq_lengths)
    cosine, sine = rope_tables(query_given - query_first, HEAD)
    key_given = jnp.transpose(table, (2, 1, 0, 3)).reshape(token_total)
    by_step = (-1, QUERY_TOKENS)
    given_steps, first_steps = query_given.reshape(by_step), query_first.reshape(by_step)
    lowest = jnp.min(first_steps, axis=1) // KEY_SPAN
    highest = jnp.max(given_steps, axis=1) // KEY_SPAN + 1
    open_low = (jnp.max(first_steps, axis=1) + KEY_SPAN - 1) // KEY_SPAN
    open_low = jnp.minimum(open_low, highest)
    open_high = jnp.clip((jnp.min(given_steps, axis=1) + 1) // KEY_SPAN, open_low, highest)
    bounds = jnp.stack([lowest, open_low, open_high, highest]).astype(jnp.int32)
    ask = jnp.stack([query_given, query_first], axis=1)
    ask_rows = jnp.stack(
        [jnp.tile(given_steps, (1, heads)), jnp.tile(first_steps, (1, heads))], axis=1
    )

    group_x = group_sorted(own_inputs)
    normed_in, query_raw, query_rows, key_raw, kv_rows = front(
        group_x, input_gain, query_proj, key_projected, value_projected,
        query_gain, key_gain, cosine, sine,
    )
    kv_places = lax.all_gather(kv_rows, "ep", axis=0, tiled=True)
    kv_all = jnp.transpose(
        kv_places.reshape(ep_size, ep_size, tp_size, row_block, 2 * HEAD), (1, 2, 0, 3, 4)
    ).reshape(token_total, 2 * HEAD)
    pairs = group_rows * heads * 1536
    exact, out_rows, lse = attend_forward(
        bounds, query_rows, ask, key_given[None], kv_all, pairs
    )
    branch = scatter_group(dot(out_rows, output_proj).astype(jnp.bfloat16))
    hidden = own_inputs.astype(jnp.float32) + branch.astype(jnp.float32)
    mid_scale = inverse_root(hidden)
    normed_mid = (hidden * mid_scale * expert_gain).astype(jnp.bfloat16)

    mid_all = lax.all_gather(normed_mid, everyone, axis=0, tiled=True)
    mid_partial, expert_in, slot_cot, inner, gate_grad, up_grad = expert_pass(
        expert, meta, mid_all, cot_all, gate_weight, up_weight, down_weight, capacity
    )
    mid_grad = lax.psum_scatter(mid_partial, everyone, scatter_dimension=0, tiled=True).astype(
        jnp.float32
    )
    out_partial = down_pass(expert, meta, inner, down_weight)
    grad_down = dot_with(inner, slot_cot, ROWS_BY_ROWS)
    grad_gate = dot_with(expert_in, gate_grad, ROWS_BY_ROWS)
    grad_up = dot_with(expert_in, up_grad, ROWS_BY_ROWS)
    mixed = lax.psum_scatter(out_partial, everyone, scatter_dimension=0, tiled=True).astype(
        jnp.float32
    )
    layer_out = to_given(hidden + mixed).astype(jnp.bfloat16)

    mid_hat = hidden * mid_scale
    grad_expert_gain = jnp.sum(mid_grad * mid_hat, axis=0)
    mid_scaled = mid_grad * expert_gain
    hidden_grad = own_cot.astype(jnp.float32) + mid_scale * (
        mid_scaled - mid_hat * jnp.mean(mid_scaled * mid_hat, axis=-1, keepdims=True)
    )
    branch_grad = group_sorted(hidden_grad.astype(jnp.bfloat16))
    out_grad = dot_with(branch_grad, output_proj, COLS_BY_COLS).astype(jnp.bfloat16)
    query_grad, kv_grad = attend_backward(
        bounds, query_rows, out_grad, exact, lse, ask_rows, key_given[:, None], kv_all, pairs
    )
    kv_grad = jnp.transpose(
        kv_grad.astype(jnp.bfloat16).reshape(ep_size, tp_size, ep_size, row_block, 2 * HEAD),
        (2, 0, 1, 3, 4),
    ).reshape(token_total, 2 * HEAD)
    kv_own = lax.psum_scatter(kv_grad, "ep", scatter_dimension=0, tiled=True)
    value_grad = kv_own[:, HEAD:]
    raw_query_grad, grad_query_gain = head_back(query_raw, query_grad, query_gain, cosine, sine)
    raw_key_grad, grad_key_gain = head_back(key_raw, kv_own[:, :HEAD], key_gain, cosine, sine)
    normed_grad = (
        dot_with(raw_query_grad, query_proj, COLS_BY_COLS)
        + dot_with(raw_key_grad, key_projected, COLS_BY_COLS)
        + dot_with(value_grad, value_projected, COLS_BY_COLS)
    )
    normed_grad = scatter_group(normed_grad.astype(jnp.bfloat16)).astype(jnp.float32)
    own_float = own_inputs.astype(jnp.float32)
    in_scale = inverse_root(own_float)
    in_hat = own_float * in_scale
    grad_input_gain = jnp.sum(normed_grad * in_hat, axis=0)
    in_scaled = normed_grad * input_gain
    grad_inputs = to_given(
        hidden_grad
        + in_scale * (in_scaled - in_hat * jnp.mean(in_scaled * in_hat, axis=-1, keepdims=True))
    )

    def ep_sum(rows):
        return lax.psum_scatter(
            rows.astype(jnp.bfloat16), "ep", scatter_dimension=0, tiled=True
        ).astype(jnp.float32)

    grad_output = jnp.transpose(ep_sum(dot_with(branch_grad, out_rows, ROWS_BY_ROWS)))
    grad_query = ep_sum(dot_with(normed_in, raw_query_grad, ROWS_BY_ROWS))
    grad_kv = ep_sum(
        dot_with(normed_in, jnp.concatenate([raw_key_grad, value_grad], axis=1), ROWS_BY_ROWS)
    )
    gains = lax.psum(
        (grad_input_gain, grad_expert_gain, grad_query_gain[0], grad_key_gain[0]), everyone
    )
    return (
        layer_out,
        grad_inputs,
        grad_query,
        grad_kv[:, :HEAD],
        grad_kv[:, HEAD:],
        grad_output,
        gains[0],
        gains[2],
        gains[3],
        gains[1],
        grad_gate[None],
        grad_up[None],
        grad_down[None],
    )


def solution(mesh):
    split = P(("ep", "tp"), None)
    experts = P(("ep", "tp"), None, None)
    columns = P(None, "tp")
    return jax.shard_map(
        on_device,
        mesh=mesh,
        in_specs=(
            split, split, P(), P(), split, split, P(), columns, columns, columns,
            P(), P(), P("tp", None), P(), experts, experts, experts,
        ),
        out_specs=(
            split, split, P("ep", "tp"), P("ep", "tp"), P("ep", "tp"), P("tp", "ep"),
            P(), P(), P(), P(), experts, experts, experts,
        ),
        check_vma=False,
    )
```

time: 3840 us -> 2110 us (0.55)
  local copies, waits for them, and re-layouts: 722 us -> 52.3 us
  matrix products: 767 us -> 111 us
  other arithmetic: 358 us -> 28 us
  blocking collectives: 443 us -> 149 us
  Pallas kernels: 0 us -> 285 us
  loops' own time: 151 us -> 0 us
  waiting for transfers between devices: 1320 us -> 1440 us
    all_to_all x7 -> x2, waiting for transfers between devices: 1140 us -> 16.2 us  [to_given(): lax.all_to_all(rows.astype(jnp.bfloat16).reshape(ep_size, row_block, widt...]
    reduce_scatter x5 -> x8, waiting for transfers between devices: 108 us -> 953 us  [the longest x1 352 us: on_device(): lax.psum_scatter(mid_partial, everyone, scatter_dimension=0, tiled=True)]
    dot_general x379 -> x15, matrix products: 767 us -> 111 us  [the longest x12 104 us: dot_with(): lax.dot_general(left, right, dims, preferred_element_type=jnp.float32)]
    all_gather x4 -> x5, waiting for transfers between devices: 63.4 us -> 467 us  [the longest x1 196 us: on_device(): mid_all = lax.all_gather(normed_mid, everyone, axis=0, tiled=True)]
    all_to_all x2, blocking collectives: 401 us -> 61.7 us  [to_places(): lax.all_to_all(moved, 'ep', split_axis=0, concat_axis=0, tiled=True)]
    pallas_call x0 -> x7, Pallas kernels: none -> 285 us  [the longest x1 108 us: expert_pass(): pl.pallas_call(expert_kernel, grid_spec=pltpu.PrefetchScalarGridSpec(num_...]
    gather x17 -> x0, local copies, waits for them, and re-layouts: 277 us -> none  [the longest x1 50.8 us: on_device(): grad_back[slot_expert, slot_rank].astype(jnp.float32)]
    dynamic_slice x289 -> x0, local copies, waits for them, and re-layouts: 184 us -> none  [the longest x120 65.2 us: span_mask(): seq_part = lax.dynamic_slice_in_dim(key_seq, offset, KEY_SPAN, 0)]
  transfers between devices with their start and end apart: 16 -> 15, of which waited for: 9 -> 13; matrix products, arithmetic and copies ran while one was open for 20% -> 6% of each run, Pallas kernels for 0% -> 2%
where the time goes in v1:
time: 2110 us; the launch traced here: 2100 us
  waiting for transfers between devices  1440 us (68%)
  Pallas kernels  285 us (14%)
  blocking collectives  149 us (7%)
  matrix products  111 us (5%)
  local copies, waits for them, and re-layouts  52.3 us (2%)
  other arithmetic  28 us (1%)
    reduce_scatter x1, waiting for transfers between devices, on_device(): lax.psum_scatter(mid_partial, everyone, scatter_dimension=0, tiled=True)  352 us
    reduce_scatter x1, waiting for transfers between devices, on_device(): lax.psum_scatter(out_partial, everyone, scatter_dimension=0, tiled=True)  318 us
    reduce_scatter x3, waiting for transfers between devices, ep_sum(): lax.psum_scatter(rows.astype(jnp.bfloat16), 'ep', scatter_dimension=0, ti...  201 us
    all_gather x1, waiting for transfers between devices, on_device(): mid_all = lax.all_gather(normed_mid, everyone, axis=0, tiled=True)  196 us
    all_gather x1, waiting for transfers between devices, on_device(): cot_all = lax.all_gather(own_cot, everyone, axis=0, tiled=True)  132 us
    pallas_call x1, Pallas kernels, expert_pass(): pl.pallas_call(expert_kernel, grid_spec=pltpu.PrefetchScalarGridSpec(num_...  108 us
    dot_general x12, matrix products, dot_with(): lax.dot_general(left, right, dims, preferred_element_type=jnp.float32)  104 us
    pallas_call x1, Pallas kernels, attend_backward(): pl.pallas_call(attend_backward_kernel, grid_spec=pltpu.PrefetchScalarGrid...  74.2 us
  transfers between devices with their start and end apart: 15, of which 13 were waited for; matrix products, arithmetic and copies ran while one was open for 6% of the time, Pallas kernels for 2%

profile of v1, /device:TPU:0, one launch (start us, length us, event | category | flops | bytes accessed | tf_op | source)
XLA Modules:
  0.0 2098.9 jit_solution(11665033083853447267)
XLA Ops:
  9.7 33.0 %all_to_all.20 = bf16[8,32,2048]{2,1,0:T(8,128)(2,1)} all-to-all(bf16[8,32,2048]{2,1,0:T(8,128)(2,1)S(1)} %bitcast.153), channel_id=1, replica_groups=mesh['ep'=8,'tp'=4] {'ep'}, dimensions={0} | all-to-all | bytes 2097152 | tf_op jit(solution)/shard_map/all_to_all | solution.py:535
  45.6 30.7 %all-gather.7.cloned.1.call-done = bf16[1024,2048]{1,0:T(8,128)(2,1)} async-done(((bf16[256,2048]{1,0:T(8,128)(2,1)}), bf16[1024,2048]{1,0:T(8,128)(2,1)}) %all-gather.7.cloned.1.call-update) | async-done | bytes 4194320 | tf_op jit(solution)/shard_map/all_gather | solution.py:550
  99.5 72.4 %all-gather.9.cloned.1.call-done = bf16[8192,256]{1,0:T(8,128)(2,1)} async-done(((bf16[1024,256]{1,0:T(8,128)(2,1)}), bf16[8192,256]{1,0:T(8,128)(2,1)}) %all-gather.9.cloned.1.call-update) | async-done | bytes 4194320 | tf_op jit(solution)/shard_map/all_gather | solution.py:588
  176.9 50.2 %attend_forward.1 = (f32[1024,1024]{1,0:T(8,128)}, bf16[1024,1024]{1,0:T(8,128)(2,1)S(1)}, f32[32,1,256]{2,1,0:T(1,128)S(1)}) custom-call(s32[4,32]{1,0:T(4,128)S(1)} %pad_add_fusion.2.bounds_ref, bf16[1024,1024]{1,0:T(8,128)(2,1)S(1)} %copy-done.23, s32[1024,2]{1,0:T(8,128)S(1)} %copy.99.ask_ref, s32[1,8192]{1,0:T(1,128)S(1)} %broadcast_in_dim_reshape.8.key_given_ref, ...), custom_call_target="tpu_custom_call" | custom-call | flops 12884901888 | bytes 16777216 | tf_op jit(solution)/shard_map/attend_forward/pallas_call | solution.py:206
  236.3 28.7 %all_to_all.21 = bf16[8,32,2048]{2,1,0:T(8,128)(2,1)} all-to-all(bf16[8,32,2048]{2,1,0:T(8,128)(2,1)S(1)} %bitcast.154), channel_id=1, replica_groups=mesh['ep'=8,'tp'=4] {'ep'}, dimensions={0} | all-to-all | bytes 2097152 | tf_op jit(solution)/shard_map/all_to_all | solution.py:535
  265.2 12.4 reduce-scatter.9.cloned.1.call-done
  282.0 47.0 %all-gather = f32[512,256]{1,0:T(8,128)} all-gather(f32[16,256]{1,0:T(8,128)S(1)} %pad_maximum_fusion.2), channel_id=2, replica_groups=mesh['ep'=8,'tp'=4] {'ep','tp'}, dimensions={0}, use_global_device_ids=true | all-gather | bytes 540672 | tf_op jit(solution)/shard_map/all_gather | solution.py:562
  329.0 132.3 %all-gather.13.cloned.1.call-done.c_ref = bf16[8192,2048]{1,0:T(8,128)(2,1)} async-done(((bf16[256,2048]{1,0:T(8,128)(2,1)}), bf16[8192,2048]{1,0:T(8,128)(2,1)}) %all-gather.13.cloned.1.call-update) | async-done | bytes 33554448 | tf_op jit(solution)/shard_map/all_gather | solution.py:563
  461.3 196.3 %all-gather.11.cloned.1.call-done.x_ref = bf16[8192,2048]{1,0:T(8,128)(2,1)} async-done(((bf16[256,2048]{1,0:T(8,128)(2,1)}), bf16[8192,2048]{1,0:T(8,128)(2,1)}) %all-gather.11.cloned.1.call-update) | async-done | bytes 33554448 | tf_op jit(solution)/shard_map/all_gather | solution.py:601
  657.6 108.1 %expert_pass.1 = (bf16[8192,2048]{1,0:T(8,128)(2,1)}, bf16[4096,2048]{1,0:T(8,128)(2,1)}, bf16[4096,2048]{1,0:T(8,128)(2,1)}, bf16[4096,768]{1,0:T(8,128)(2,1)},...) custom-call(s32[1]{0:T(128)} %bitcast.23.expert_ref, f32[32,16,256]{2,1,0:T(8,128)} %bitcast.125, ...), custom_call_target="tpu_custom_call" | custom-call | flops 64424509440 | bytes 157286400 | tf_op jit(solution)/shard_map/expert_pass/pallas_call | solution.py:385
  765.7 352.4 %reduce-scatter.13.cloned.1.call-done = bf16[256,2048]{1,0:T(8,128)(2,1)} async-done(((bf16[8192,2048]{1,0:T(8,128)(2,1)}), bf16[256,2048]{1,0:T(8,128)(2,1)}) %reduce-scatter.13.cloned.1.call-update) | async-done | bytes 1048592 | tf_op jit(solution)/shard_map/reduce_scatter | solution.py:605
  1130.5 35.3 %all-gather.15.cloned.1.call-done = bf16[1024,2048]{1,0:T(8,128)(2,1)} async-done(((bf16[256,2048]{1,0:T(8,128)(2,1)}), bf16[1024,2048]{1,0:T(8,128)(2,1)}) %all-gather.15.cloned.1.call-update) | async-done | bytes 4194320 | tf_op jit(solution)/shard_map/all_gather | solution.py:550
  1175.1 74.2 %attend_backward.1 = (f32[1024,1024]{1,0:T(8,128)}, f32[8192,256]{1,0:T(8,128)}) custom-call(s32[4,32]{1,0:T(4,128)} %copy-done.12, bf16[1024,1024]{1,0:T(8,128)(2,1)} %copy-done.22, bf16[1024,1024]{1,0:T(8,128)(2,1)} %convolution_convert_fusion.7.grad_ref, f32[1024,1024]{1,0:T(8,128)} %get-tuple-element.39.exact_ref, f32[32,1,256]{2,1,0:T(1,128)} %copy-done.25, ...), custom_call_target="tpu_custom_call" | custom-call | flops 32212254720 | bytes 33554432 | tf_op jit(solution)/shard_map/attend_backward/pallas_call | solution.py:300
  1274.8 68.9 %reduce-scatter.15.cloned.1.call-done = bf16[1024,256]{1,0:T(8,128)(2,1)} async-done(((bf16[8192,256]{1,0:T(8,128)(2,1)}), bf16[1024,256]{1,0:T(8,128)(2,1)}) %reduce-scatter.15.cloned.1.call-update) | async-done | bytes 524304 | tf_op jit(solution)/shard_map/reduce_scatter | solution.py:632
  1358.8 33.5 %down_pass.1 = bf16[8192,2048]{1,0:T(8,128)(2,1)} custom-call(s32[1]{0:T(128)} %bitcast.23.expert_ref, f32[32,16,256]{2,1,0:T(8,128)S(1)} %bitcast.126, bf16[4096,768]{1,0:T(8,128)(2,1)S(1)} %copy-done.19, bf16[1,768,2048]{2,1,0:T(8,128)(2,1)S(1)} %copy-done.17), custom_call_target="tpu_custom_call" | custom-call | flops 12884901888 | bytes 41943040 | tf_op jit(solution)/shard_map/down_pass/pallas_call | solution.py:429
  1412.0 21.4 %convolution_bitcast_fusion.1 = f32[1,2048,768]{2,1,0:T(8,128)} fusion(bf16[4096,2048]{1,0:T(8,128)(2,1)} %get-tuple-element.49, bf16[4096,768]{1,0:T(8,128)(2,1)} %get-tuple-element.51), kind=kOutput, calls=%fused_computation.2 | convolution fusion | flops 12884901888 | bytes 29360128 | tf_op jit(solution)/shard_map/dot_general | solution.py:28
  1435.5 318.3 %reduce-scatter.11.cloned.1.call-done = bf16[256,2048]{1,0:T(8,128)(2,1)} async-done(((bf16[8192,2048]{1,0:T(8,128)(2,1)}), bf16[256,2048]{1,0:T(8,128)(2,1)}) %reduce-scatter.11.cloned.1.call-update) | async-done | bytes 1048592 | tf_op jit(solution)/shard_map/reduce_scatter | solution.py:612
  1766.5 21.2 %convolution_bitcast_fusion.2 = f32[1,2048,768]{2,1,0:T(8,128)} fusion(bf16[4096,2048]{1,0:T(8,128)(2,1)} %get-tuple-element.49, bf16[4096,768]{1,0:T(8,128)(2,1)} %get-tuple-element.50), kind=kOutput, calls=%fused_computation.3 | convolution fusion | flops 12884901888 | bytes 29360128 | tf_op jit(solution)/shard_map/dot_general | solution.py:28
  1790.1 16.2 all-to-all-done.3
  1817.5 20.5 convolution_bitcast_fusion
  1838.0 47.5 %reduce-scatter.23.cloned.1.call-done = bf16[256,1024]{1,0:T(8,128)(2,1)} async-done(((bf16[2048,1024]{1,0:T(8,128)(2,1)}), bf16[256,1024]{1,0:T(8,128)(2,1)}) %reduce-scatter.23.cloned.1.call-update) | async-done | bytes 524304 | tf_op jit(solution)/shard_map/reduce_scatter | solution.py:653
  1888.0 88.9 %reduce-scatter.19.cloned.1.call-done = bf16[256,1024]{1,0:T(8,128)(2,1)} async-done(((bf16[2048,1024]{1,0:T(8,128)(2,1)}), bf16[256,1024]{1,0:T(8,128)(2,1)}) %reduce-scatter.19.cloned.1.call-update) | async-done | bytes 524304 | tf_op jit(solution)/shard_map/reduce_scatter | solution.py:653
  1979.0 65.1 %reduce-scatter.21.cloned.1.call-done = bf16[256,256]{1,0:T(8,128)(2,1)} async-done(((bf16[2048,256]{1,0:T(8,128)(2,1)}), bf16[256,256]{1,0:T(8,128)(2,1)}) %reduce-scatter.21.cloned.1.call-update) | async-done | bytes 131088 | tf_op jit(solution)/shard_map/reduce_scatter | solution.py:653
  2045.7 40.4 %all-reduce = (f32[2048]{0:T(1024)}, f32[128]{0:T(128)}, f32[128]{0:T(128)}, f32[2048]{0:T(1024)}) all-reduce(f32[2048]{0:T(1024)S(1)} %get-tuple-element.133, f32[128]{0:T(128)S(1)} %bitcast.130, f32[128]{0:T(128)S(1)} %bitcast.131, f32[2048]{0:T(1024)S(1)} %copy-done.35), channel_id=1, replica_groups=mesh['ep'=8,'tp'=4] {'ep','tp'}, use_global_device_ids=true, to_apply=%region_19.20 | all-reduce | flops 4352 | bytes 34816 | tf_op jit(solution)/shard_map/psum | solution.py:662
  (197 shorter events, 167.3 us)
Async XLA Ops:
  8.0 68.3 %all-gather.7.cloned.1.call-start = ((), (), s32[]{:S(2)}) async-start(), calls=%async_computation.12 | async-start | bytes 5242880 | tf_op jit(solution)/shard_map/all_gather | solution.py:550
  9.3 225.3 %copy-start.36 = (s32[256]{0:T(256)}, s32[256]{0:T(256)S(1)}, u32[]{:S(2)}) copy-start(s32[256]{0:T(256)S(1)} %sub.51) | copy-start | bytes 3076
  42.7 129.2 %all-gather.9.cloned.1.call-start = ((), (), s32[]{:S(2)}) async-start(), calls=%async_computation.13 | async-start | bytes 4718592 | tf_op jit(solution)/shard_map/all_gather | solution.py:588
  98.3 179.3 %reduce-scatter.9.cloned.1.call-start = ((), (), s32[]{:S(2)}) async-start(), calls=%async_computation.14 | async-start | bytes 5242880 | tf_op jit(solution)/shard_map/reduce_scatter | solution.py:557
  99.5 77.4 %copy-start.12 = (s32[4,32]{1,0:T(4,128)}, s32[4,32]{1,0:T(4,128)S(1)}, u32[]{:S(2)}) copy-start(s32[4,32]{1,0:T(4,128)S(1)} %pad_add_fusion.2.bounds_ref) | copy-start | bytes 1540
  176.9 50.2 %copy-start.41 = (bf16[1024,2048]{1,0:T(8,128)(2,1)S(1)}, bf16[1024,2048]{1,0:T(8,128)(2,1)}, u32[]{:S(2)}) copy-start(bf16[1024,2048]{1,0:T(8,128)(2,1)} %param.29) | copy-start | bytes 12582916
  234.5 226.8 %all-gather.13.cloned.1.call-start = ((), (), s32[]{:S(2)}) async-start(), calls=%async_computation.16 | async-start | bytes 34603008 | tf_op jit(solution)/shard_map/all_gather | solution.py:563
  265.1 392.4 %all-gather.11.cloned.1.call-start = ((), (), s32[]{:S(2)}) async-start(), calls=%async_computation.15 | async-start | bytes 34603008 | tf_op jit(solution)/shard_map/all_gather | solution.py:601
  281.9 836.2 %reduce-scatter.13.cloned.1.call-start = ((), (), s32[]{:S(2)}) async-start(), calls=%async_computation.18 | async-start | bytes 34603008 | tf_op jit(solution)/shard_map/reduce_scatter | solution.py:605
  765.7 400.2 %all-gather.15.cloned.1.call-start = ((), (), s32[]{:S(2)}) async-start(), calls=%async_computation.19 | async-start | bytes 5242880 | tf_op jit(solution)/shard_map/all_gather | solution.py:550
  1123.5 220.2 %reduce-scatter.15.cloned.1.call-start = ((), (), s32[]{:S(2)}) async-start(), calls=%async_computation.20 | async-start | bytes 4718592 | tf_op jit(solution)/shard_map/reduce_scatter | solution.py:632
  1255.6 177.8 %reduce-scatter.17.cloned.1.call-start = ((), (), s32[]{:S(2)}) async-start(), calls=%async_computation.21 | async-start | bytes 5242880 | tf_op jit(solution)/shard_map/reduce_scatter | solution.py:557
  1267.9 77.7 %copy-start.16 = (f32[128]{0:T(128)S(1)}, f32[128]{0:T(128)}, u32[]{:S(2)}) copy-start(f32[128]{0:T(128)} %param.28) | copy-start | bytes 1540
  1274.8 71.8 %copy-start.6 = (bf16[2048,128]{1,0:T(8,128)(2,1)S(1)}, bf16[2048,128]{1,0:T(8,128)(2,1)}, u32[]{:S(2)}) copy-start(bf16[2048,128]{1,0:T(8,128)(2,1)} %wk_ref.1) | copy-start | bytes 1572868
  1352.6 401.1 %reduce-scatter.11.cloned.1.call-start = ((), (), s32[]{:S(2)}) async-start(), calls=%async_computation.17 | async-start | bytes 34603008 | tf_op jit(solution)/shard_map/reduce_scatter | solution.py:612
  1392.3 493.2 %reduce-scatter.23.cloned.1.call-start = ((), (), s32[]{:S(2)}) async-start(), calls=%async_computation.24 | async-start | bytes 4718592 | tf_op jit(solution)/shard_map/reduce_scatter | solution.py:653
  1402.0 574.8 %reduce-scatter.19.cloned.1.call-start = ((), (), s32[]{:S(2)}) async-start(), calls=%async_computation.22 | async-start | bytes 4718592 | tf_op jit(solution)/shard_map/reduce_scatter | solution.py:653
  1412.0 341.8 %copy-start.28 = (bf16[256,2048]{1,0:T(8,128)(2,1)S(1)}, bf16[256,2048]{1,0:T(8,128)(2,1)}, u32[]{:S(2)}) copy-start(bf16[256,2048]{1,0:T(8,128)(2,1)} %reduce-scatter.9.cloned.1.call-done) | copy-start | bytes 3145732
  1759.0 47.3 %all-to-all-start.3 = ((bf16[8,32,2048]{2,1,0:T(8,128)(2,1)}), bf16[8,32,2048]{2,1,0:T(8,128)(2,1)S(1)}, u32[]{:S(2)}, u32[]{:S(2)}) async-start(bf16[8,32,2048]{2,1,0:T(8,128)(2,1)} %bitcast.155), calls=%async_computation.8 | async-start | bytes 2097152 | tf_op jit(solution)/shard_map/all_to_all | solution.py:540
  1766.4 277.7 %reduce-scatter.21.cloned.1.call-start = ((), (), s32[]{:S(2)}) async-start(), calls=%async_computation.23 | async-start | bytes 1179648 | tf_op jit(solution)/shard_map/reduce_scatter | solution.py:653
  1806.3 281.7 %all-to-all-start.2 = ((bf16[8,32,2048]{2,1,0:T(8,128)(2,1)}), bf16[8,32,2048]{2,1,0:T(8,128)(2,1)}, u32[]{:S(2)}, u32[]{:S(2)}) async-start(bf16[8,32,2048]{2,1,0:T(8,128)(2,1)} %bitcast.29), calls=%async_computation.4 | async-start | bytes 2097152 | tf_op jit(solution)/shard_map/all_to_all | solution.py:540
  1838.0 207.8 %copy-start.35 = (f32[2048]{0:T(1024)S(1)}, f32[2048]{0:T(1024)}, u32[]{:S(2)}) copy-start(f32[2048]{0:T(1024)} %get-tuple-element.131) | copy-start | bytes 24580
  1838.0 248.1 %copy-start.37 = (s32[256]{0:T(256)S(1)}, s32[256]{0:T(256)}, u32[]{:S(2)}) copy-start(s32[256]{0:T(256)} %copy-done.36) | copy-start | bytes 3076
  1976.8 113.9 %copy-start.1 = (bf16[256,2048]{1,0:T(8,128)(2,1)S(1)}, bf16[256,2048]{1,0:T(8,128)(2,1)}, u32[]{:S(2)}) copy-start(bf16[256,2048]{1,0:T(8,128)(2,1)} %param.17) | copy-start | bytes 3145732
  (37 other events, 314.3 us)
Sparse Core Ops, SparseCore 0:
  42.8 33.4 all-gather.6
  98.4 73.3 all-gather.8
  234.6 42.9 reduce-scatter.8
  1123.6 42.1 all-gather.14
  1255.7 87.8 reduce-scatter.14
  1352.8 44.2 reduce-scatter.16
  1399.4 354.2 reduce-scatter.10
  1757.8 127.6 reduce-scatter.22
  1889.1 87.6 reduce-scatter.18
  1981.0 63.0 reduce-scatter.20
Sparse Core Ops, SparseCore 1:
  265.2 196.1 all-gather.12
  465.0 192.5 all-gather.10
  765.7 352.3 reduce-scatter.12

commit v2 on v1

--- a/solution.py
+++ b/solution.py
@@ -1,3 +1,4 @@
+import functools
 import math
 
 import jax
@@ -237,7 +238,7 @@
 
 def attend_backward_kernel(
     bounds_ref, q_ref, grad_ref, exact_ref, lse_ref, ask_ref, key_given_ref, kv_ref,
-    dq_ref, dkv_ref, acc,
+    dq_ref, rounded_ref, dkv_ref, acc,
 ):
     step = pl.program_id(0)
     tokens, cols = q_ref.shape
@@ -290,6 +291,13 @@
         dq_ref[:, head * HEAD : (head + 1) * HEAD] = acc[
             head * tokens : (head + 1) * tokens
         ] * (HEAD**-0.5)
+
+    @pl.when(step == pl.num_programs(0) - 1)
+    def _():
+        @pl.loop(0, dkv_ref.shape[0], step=KEY_SPAN)
+        def _(row):
+            place = pl.ds(row, KEY_SPAN)
+            rounded_ref[place] = dkv_ref[place].astype(jnp.bfloat16)
 
 
 def attend_backward(bounds, query, grad, exact, lse, ask_rows, key_column, kv, pairs):
@@ -312,11 +320,14 @@
                 whole(kv.shape),
             ],
             out_specs=[rows_of((QUERY_TOKENS, cols)), whole(kv.shape)],
-            scratch_shapes=[pltpu.VMEM((stacked, HEAD), jnp.float32)],
+            scratch_shapes=[
+                pltpu.VMEM(kv.shape, jnp.float32),
+                pltpu.VMEM((stacked, HEAD), jnp.float32),
+            ],
         ),
         out_shape=[
             jax.ShapeDtypeStruct((rows, cols), jnp.float32),
-            jax.ShapeDtypeStruct(kv.shape, jnp.float32),
+            jax.ShapeDtypeStruct(kv.shape, jnp.bfloat16),
         ],
         compiler_params=params(56),
         cost_estimate=cost(20 * pairs * HEAD, 32 * MIB, pairs),
@@ -326,7 +337,7 @@
 
 def selection(meta, expert, capacity):
     tokens = meta.shape[1]
-    weight = jnp.sum(jnp.where(meta[:TOP] == expert, meta[TOP:], 0.0), axis=0, keepdims=True)
+    weight = jnp.sum(jnp.where(meta[:TOP] == expert, meta[TOP : 2 * TOP], 0.0), axis=0, keepdims=True)
     member = jnp.where(weight > 0.0, 1.0, 0.0)
     earlier = lax.broadcasted_iota(jnp.int32, (tokens, tokens), 0)
     later = lax.broadcasted_iota(jnp.int32, (tokens, tokens), 1)
@@ -340,17 +351,18 @@
 
 def expert_kernel(
     expert_ref, meta_ref, x_ref, c_ref, wg_ref, wu_ref, wd_ref,
-    mid_ref, xs_ref, cs_ref, inner_ref, gg_ref, ug_ref,
+    mid_ref, out_ref, xs_ref, cs_ref, inner_ref, gg_ref, ug_ref,
 ):
     blocks, _, tokens = meta_ref.shape
     capacity = xs_ref.shape[0] // blocks
     expert = expert_ref[0].astype(jnp.float32)
-    picks = []
+    picks, gates = [], []
     for block in range(blocks):
         rows = slice(block * tokens, (block + 1) * tokens)
         slots = slice(block * capacity, (block + 1) * capacity)
         pick, gate = selection(meta_ref[block], expert, capacity)
         picks.append(pick)
+        gates.append(gate)
         xs_ref[slots] = dot(pick, x_ref[rows]).astype(jnp.bfloat16)
         cs_ref[slots] = (dot(pick, c_ref[rows]) * gate).astype(jnp.bfloat16)
     gate_part = dot(xs_ref[...], wg_ref[0])
@@ -358,7 +370,8 @@
     inner_grad = dot_with(cs_ref[...], wd_ref[0], COLS_BY_COLS)
     gate_sig = jax.nn.sigmoid(gate_part)
     activated = gate_part * gate_sig
-    inner_ref[...] = (activated * up_part).astype(jnp.bfloat16)
+    inner = (activated * up_part).astype(jnp.bfloat16)
+    inner_ref[...] = inner
     gate_grad = (inner_grad * up_part * gate_sig * (1.0 + gate_part * (1.0 - gate_sig))).astype(
         jnp.bfloat16
     )
@@ -373,6 +386,12 @@
         mid_ref[rows] = dot_with(picks[block], slot_grad[slots], ROWS_BY_ROWS).astype(
             jnp.bfloat16
         )
+    result = dot(inner, wd_ref[0]).astype(jnp.bfloat16).astype(jnp.float32)
+    for block in range(blocks):
+        rows = slice(block * tokens, (block + 1) * tokens)
+        slots = slice(block * capacity, (block + 1) * capacity)
+        scaled = (result[slots] * gates[block]).astype(jnp.bfloat16)
+        out_ref[rows] = dot_with(picks[block], scaled, ROWS_BY_ROWS).astype(jnp.bfloat16)
 
 
 def expert_pass(expert, meta, x_all, c_all, gate_w, up_w, down_w, capacity):
@@ -381,7 +400,7 @@
     per = max(1, 512 // tokens)
     total = blocks * capacity
     slots = per * capacity
-    shapes = [(blocks * tokens, width)] + [(total, width)] * 2 + [(total, hidden)] * 3
+    shapes = [(blocks * tokens, width)] * 2 + [(total, width)] * 2 + [(total, hidden)] * 3
     return pl.pallas_call(
         expert_kernel,
         grid_spec=pltpu.PrefetchScalarGridSpec(
@@ -395,7 +414,7 @@
                 whole(up_w.shape),
                 whole(down_w.shape),
             ],
-            out_specs=[rows_of((per * tokens, width))]
+            out_specs=[rows_of((per * tokens, width))] * 2
             + [rows_of((slots, width))] * 2
             + [rows_of((slots, hidden))] * 3,
         ),
@@ -404,45 +423,6 @@
         cost_estimate=cost(10 * total * width * hidden, 150 * MIB, total * hidden),
         name="expert_pass",
     )(expert, meta, x_all, c_all, gate_w, up_w, down_w)
-
-
-def down_kernel(expert_ref, meta_ref, inner_ref, wd_ref, out_ref):
-    blocks, _, tokens = meta_ref.shape
-    capacity = inner_ref.shape[0] // blocks
-    expert = expert_ref[0].astype(jnp.float32)
-    result = dot(inner_ref[...], wd_ref[0]).astype(jnp.bfloat16).astype(jnp.float32)
-    for block in range(blocks):
-        pick, gate = selection(meta_ref[block], expert, capacity)
-        slots = slice(block * capacity, (block + 1) * capacity)
-        scaled = (result[slots] * gate).astype(jnp.bfloat16)
-        out_ref[block * tokens : (block + 1) * tokens] = dot_with(
-            pick, scaled, ROWS_BY_ROWS
-        ).astype(jnp.bfloat16)
-
-
-def down_pass(expert, meta, inner, down_w):
-    blocks, lines, tokens = meta.shape
-    total, hidden = inner.shape
-    width = down_w.shape[2]
-    per = max(1, 512 // tokens)
-    slots = per * (total // blocks)
-    return pl.pallas_call(
-        down_kernel,
-        grid_spec=pltpu.PrefetchScalarGridSpec(
-            num_scalar_prefetch=1,
-            grid=(blocks // per,),
-            in_specs=[
-                rows_of((per, lines, tokens)),
-                rows_of((slots, hidden)),
-                whole(down_w.shape),
-            ],
-            out_specs=rows_of((per * tokens, width)),
-        ),
-        out_shape=jax.ShapeDtypeStruct((blocks * tokens, width), jnp.bfloat16),
-        compiler_params=params(40),
-        cost_estimate=cost(2 * total * width * hidden, 40 * MIB),
-        name="down_pass",
-    )(expert, meta, inner, down_w)
 
 
 def head_back_kernel(raw_ref, grad_ref, gain_ref, cos_ref, sin_ref, out_ref, gain_grad_ref):
@@ -487,6 +467,513 @@
         cost_estimate=cost(rows * cols * 20, rows * cols * 10),
         name="head_back",
     )(raw, grad, gain[None], cosine, sine)
+
+
+MESH_ID = pl.DeviceIdType.MESH
+
+
+class Place:
+    def __init__(self, send_sem, tp_size=4):
+        self.tp_size, self.send_sem, self.sent = tp_size, send_sem, []
+        self.ep, self.tp = lax.axis_index("ep"), lax.axis_index("tp")
+        self.z, self.y, self.x, self.core = self.ep // 2, self.ep % 2, self.tp // 2, self.tp % 2
+        self.over_x = self.tp + 2 - 4 * self.x
+        self.over_core = self.tp + 1 - 2 * self.core
+        self.over_both = self.over_core + 2 - 4 * self.x
+
+    def level(self, step):
+        return (self.z, self.z + 1 - 2 * (self.z % 2), (self.z + 2) % 4, 3 - self.z)[step]
+
+    def across(self, step, over_y):
+        return self.level(step) * 2 + self.y + over_y * (1 - 2 * self.y)
+
+    def device(self, step, first, second, other=0):
+        core = self.core + other * (1 - 2 * self.core)
+        over_y = first * (1 - core) + second * core
+        over_x = first * core + second * (1 - core)
+        x = self.x + over_x * (1 - 2 * self.x)
+        return self.across(step, over_y), x * 2 + core
+
+    def slot(self, *where):
+        ep, tp = self.device(*where)
+        return ep * self.tp_size + tp
+
+    def greet(self, partners):
+        barrier = pltpu.get_barrier_semaphore()
+        for partner in partners:
+            pl.semaphore_signal(barrier, inc=1, device_id=partner, device_id_type=MESH_ID)
+        pl.semaphore_wait(barrier, len(partners))
+
+    def greet_all_ways(self):
+        partners = [(1, 0, 0), (2, 0, 0), (3, 0, 0), (0, 1, 0), (0, 0, 1), (0, 0, 0, 1)]
+        self.greet([self.device(*partner) for partner in partners])
+
+    def send(self, src, dst, sem, device):
+        copy = pltpu.make_async_remote_copy(
+            src_ref=src,
+            dst_ref=dst,
+            send_sem=self.send_sem.at[len(self.sent)],
+            recv_sem=sem,
+            device_id=device,
+            device_id_type=MESH_ID,
+        )
+        copy.start()
+        self.sent.append(copy)
+
+    def arrive(self, dst, sem):
+        pltpu.make_async_remote_copy(
+            src_ref=dst,
+            dst_ref=dst,
+            send_sem=self.send_sem.at[0],
+            recv_sem=sem,
+            device_id=(self.ep, self.over_core),
+            device_id_type=MESH_ID,
+        ).wait_recv()
+
+    def finish(self):
+        for copy in self.sent:
+            copy.wait_send()
+
+
+def reach(kernel, out, scratch, ident, *operands, vmem_out=False, mib=None):
+    dma = [kind if not isinstance(kind, tuple) else pltpu.SemaphoreType.DMA(kind) for kind in scratch]
+    space = pltpu.VMEM if vmem_out else pl.ANY
+    single = not isinstance(out, (list, tuple))
+    return pl.pallas_call(
+        kernel,
+        in_specs=[pl.BlockSpec(memory_space=pl.ANY)] * len(operands),
+        out_specs=jax.tree.map(lambda _: pl.BlockSpec(memory_space=space), out),
+        out_shape=out,
+        scratch_shapes=dma,
+        compiler_params=pltpu.CompilerParams(
+            collective_id=ident,
+            has_side_effects=True,
+            vmem_limit_bytes=(mib or 16) * MIB,
+        ),
+        cost_estimate=cost(1, 1),
+        name=kernel.__name__ if not isinstance(kernel, functools.partial) else kernel.func.__name__,
+    )(*operands)
+
+
+def gather_all_kernel(x_ref, m_ref, out_ref, lines_ref, own_sem, send_sem, recv_sem, line_sem):
+    place = Place(send_sem)
+    rows, lines = x_ref.shape[0], m_ref.shape[0]
+
+    def part(slot):
+        return out_ref.at[pl.ds(slot * rows, rows)]
+
+    def some(slot):
+        return lines_ref.at[pl.ds(slot * lines, lines)]
+
+    def send(where, partner):
+        slot = place.slot(*where)
+        own = where == (0, 0, 0)
+        device = place.device(*partner)
+        place.send(m_ref if own else some(slot), some(slot), line_sem.at[slot], device)
+        place.send(x_ref if own else part(slot), part(slot), recv_sem.at[slot], device)
+
+    def arrive(*where):
+        slot = place.slot(*where)
+        place.arrive(some(slot), line_sem.at[slot])
+        place.arrive(part(slot), recv_sem.at[slot])
+
+    mine = place.slot(0, 0, 0)
+    own = [
+        pltpu.make_async_copy(x_ref, part(mine), own_sem.at[0]),
+        pltpu.make_async_copy(m_ref, some(mine), own_sem.at[1]),
+    ]
+    for copy in own:
+        copy.start()
+    place.greet_all_ways()
+    for step in (1, 2, 3):
+        send((0, 0, 0), (step, 0, 0))
+    for step in range(4):
+        if step:
+            arrive(step, 0, 0)
+        send((step, 0, 0), (0, 1, 0))
+        send((step, 0, 0), (0, 0, 1))
+        send((step, 0, 0), (0, 0, 0, 1))
+        if step:
+            arrive(step - 1, 1, 0)
+            send((step - 1, 1, 0), (0, 0, 1))
+            send((step - 1, 1, 0), (0, 0, 0, 1))
+    arrive(3, 1, 0)
+    send((3, 1, 0), (0, 0, 1))
+    send((3, 1, 0), (0, 0, 0, 1))
+    for step in range(4):
+        for first in (0, 1):
+            arrive(step, first, 1)
+            send((step, first, 1), (0, 0, 0, 1))
+    for step in range(4):
+        for first in (0, 1):
+            for second in (0, 1):
+                arrive(step, first, second, 1)
+    for copy in own:
+        copy.wait()
+    place.finish()
+
+
+def gather_all(x, lines, parts, ident):
+    out = [
+        jax.ShapeDtypeStruct((parts * array.shape[0], array.shape[1]), array.dtype)
+        for array in (x, lines)
+    ]
+    scratch = [(2,), (2 * parts - 2,), (parts,), (parts,)]
+    return reach(gather_all_kernel, out, scratch, ident, x, lines)
+
+
+BUFFERS = 4
+
+
+def scatter_all_kernel(
+    p_ref, out_ref, held, over_second, over_first, over_z, own,
+    own_sem, send_sem, core_sem, second_sem, first_sem, z_sem,
+):
+    place = Place(send_sem)
+    rows = out_ref.shape[0]
+
+    def add(total, other):
+        @pl.loop(0, rows, step=64)
+        def _(row):
+            some = pl.ds(row, 64)
+            total[some] = total[some] + other[some]
+
+    def part(slot):
+        return p_ref.at[pl.ds(slot * rows, rows)]
+
+    order = [(step, first, second) for second in (1, 0) for step in (3, 2, 1, 0) for first in (1, 0)]
+    loads = []
+
+    def load(number):
+        buffer = number % BUFFERS
+        copy = pltpu.make_async_copy(
+            part(place.slot(*order[number])), own.at[buffer], own_sem.at[buffer]
+        )
+        copy.start()
+        loads.append(copy)
+
+    for number in range(BUFFERS):
+        load(number)
+    place.greet_all_ways()
+    for step, first, second in order:
+        place.send(
+            part(place.slot(step, first, second, 1)),
+            held.at[step, first, second],
+            core_sem.at[step, first, second],
+            place.device(0, 0, 0, 1),
+        )
+    for number, (step, first, second) in enumerate(order):
+        mine = held.at[step, first, second]
+        place.arrive(mine, core_sem.at[step, first, second])
+        loads[number].wait()
+        add(mine, own.at[number % BUFFERS])
+        if number + BUFFERS < len(order):
+            load(number + BUFFERS)
+        if second:
+            place.send(
+                mine, over_second.at[step, first], second_sem.at[step, first], place.device(0, 0, 1)
+            )
+
+    def onward(step):
+        mine = held.at[step, 0, 0]
+        place.arrive(over_first.at[step], first_sem.at[step])
+        add(mine, over_first.at[step])
+        if step:
+            place.send(mine, over_z.at[step], z_sem.at[step], place.device(step, 0, 0))
+
+    for step in (3, 2, 1, 0):
+        mine = held.at[step, 1, 0]
+        place.arrive(over_second.at[step, 1], second_sem.at[step, 1])
+        add(mine, over_second.at[step, 1])
+        place.send(mine, over_first.at[step], first_sem.at[step], place.device(0, 1, 0))
+        mine = held.at[step, 0, 0]
+        place.arrive(over_second.at[step, 0], second_sem.at[step, 0])
+        add(mine, over_second.at[step, 0])
+        if step < 3:
+            onward(step + 1)
+    onward(0)
+    for step in (3, 2, 1):
+        place.arrive(over_z.at[step], z_sem.at[step])
+
+    @pl.loop(0, rows, step=32)
+    def _(row):
+        some = pl.ds(row, 32)
+        total = held[0, 0, 0, some].astype(jnp.float32)
+        for step in (1, 2, 3):
+            total = total + over_z[step, some].astype(jnp.float32)
+        out_ref[some] = total
+
+    place.finish()
+
+
+def scatter_all(p, parts, ident):
+    rows, width = p.shape[0] // parts, p.shape[1]
+
+    def buffer(*lead):
+        return pltpu.VMEM((*lead, rows, width), p.dtype)
+
+    scratch = [buffer(4, 2, 2), buffer(4, 2), buffer(4), buffer(4), buffer(BUFFERS)]
+    scratch += [(BUFFERS,), (parts - 1,), (4, 2, 2), (4, 2), (4,), (4,)]
+    out = jax.ShapeDtypeStruct((rows, width), jnp.float32)
+    return reach(scatter_all_kernel, out, scratch, ident, p, vmem_out=True, mib=56)
+
+
+def enter_kernel(x_ref, c_ref, group_ref, cot_ref, own_sem, send_sem, x_sem, cot_sem):
+    place = Place(send_sem)
+    ep, tp = place.ep, place.tp
+    others = [place.across(step, over) for step in range(4) for over in (0, 1)]
+    own = [
+        pltpu.make_async_copy(x_ref.at[ep], group_ref.at[ep, tp], own_sem.at[0]),
+        pltpu.make_async_copy(c_ref.at[ep], cot_ref.at[ep], own_sem.at[1]),
+    ]
+    for copy in own:
+        copy.start()
+    place.greet(
+        [(other, tp) for other in others[1:]] + [(ep, place.over_x), (ep, place.over_core)]
+    )
+    for other in others[1:]:
+        place.send(x_ref.at[other], group_ref.at[ep, tp], x_sem.at[ep, tp], (other, tp))
+    for number, other in enumerate(others):
+        block = group_ref.at[other, tp]
+        if number:
+            place.arrive(block, x_sem.at[other, tp])
+        source = block if number else x_ref.at[ep]
+        place.send(source, block, x_sem.at[other, tp], (ep, place.over_x))
+        place.send(source, block, x_sem.at[other, tp], (ep, place.over_core))
+    for other in others[1:]:
+        place.send(c_ref.at[other], cot_ref.at[ep], cot_sem.at[ep], (other, tp))
+    for other in others:
+        block = group_ref.at[other, place.over_x]
+        place.arrive(block, x_sem.at[other, place.over_x])
+        place.send(block, block, x_sem.at[other, place.over_x], (ep, place.over_core))
+    for other in others:
+        for source in (place.over_core, place.over_both):
+            place.arrive(group_ref.at[other, source], x_sem.at[other, source])
+    for other in others[1:]:
+        place.arrive(cot_ref.at[other], cot_sem.at[other])
+    for copy in own:
+        copy.wait()
+    place.finish()
+
+
+def enter(x, c, tp_size, ident):
+    ep_size, block, width = x.shape
+    moves = (ep_size - 1) * 2 + ep_size * 3
+    out = [
+        jax.ShapeDtypeStruct((ep_size, tp_size, block, width), x.dtype),
+        jax.ShapeDtypeStruct((ep_size, block, width), x.dtype),
+    ]
+    scratch = [(2,), (moves,), (ep_size, tp_size), (ep_size,)]
+    return reach(enter_kernel, out, scratch, ident, x, c)
+
+
+CHUNKS = 4
+
+
+def gather_group_kernel(x_ref, group_ref, own_sem, send_sem, recv_sem):
+    place = Place(send_sem)
+    ep, tp = place.ep, place.tp
+    some = x_ref.shape[0] // CHUNKS
+
+    def piece(chunk, owner):
+        return group_ref.at[pl.ds(chunk * some, some), owner]
+
+    own = pltpu.make_async_copy(x_ref, group_ref.at[:, tp], own_sem)
+    own.start()
+    place.greet([(ep, place.over_x), (ep, place.over_core)])
+    for partner in (place.over_x, place.over_core):
+        for chunk in range(CHUNKS):
+            place.send(
+                x_ref.at[pl.ds(chunk * some, some)],
+                piece(chunk, tp),
+                recv_sem.at[chunk, tp],
+                (ep, partner),
+            )
+    for chunk in range(CHUNKS):
+        block = piece(chunk, place.over_x)
+        place.arrive(block, recv_sem.at[chunk, place.over_x])
+        place.send(block, block, recv_sem.at[chunk, place.over_x], (ep, place.over_core))
+    for chunk in range(CHUNKS):
+        for source in (place.over_core, place.over_both):
+            place.arrive(piece(chunk, source), recv_sem.at[chunk, source])
+    own.wait()
+    place.finish()
+
+
+def gather_group(x, tp_size, ident):
+    ep_size, block, width = x.shape
+    out = jax.ShapeDtypeStruct((ep_size, tp_size, block, width), x.dtype)
+    scratch = [pltpu.SemaphoreType.DMA, (CHUNKS * 3,), (CHUNKS, tp_size)]
+    return reach(gather_group_kernel, out, scratch, ident, x)
+
+
+def scatter_group_kernel(
+    p_ref, out_ref, own, held, over_x, own_sem, send_sem, core_sem, x_sem
+):
+    place = Place(send_sem)
+    ep, tp = place.ep, place.tp
+    some = p_ref.shape[0] // CHUNKS
+    block, width = p_ref.shape[2:]
+
+    def chunk_of(chunk):
+        return pl.ds(chunk * some, some)
+
+    loads = [
+        pltpu.make_async_copy(p_ref.at[:, owner], own.at[number], own_sem.at[number])
+        for number, owner in enumerate((place.over_x, tp))
+    ]
+    for copy in loads:
+        copy.start()
+    place.greet([(ep, place.over_x), (ep, place.over_core)])
+    for number, owner in enumerate((place.over_both, place.over_core)):
+        for chunk in range(CHUNKS):
+            place.send(
+                p_ref.at[chunk_of(chunk), owner],
+                held.at[number, chunk_of(chunk)],
+                core_sem.at[number, chunk],
+                (ep, place.over_core),
+            )
+
+    def add(number, chunk):
+        place.arrive(held.at[number, chunk_of(chunk)], core_sem.at[number, chunk])
+        for row in range(chunk * some, (chunk + 1) * some):
+            held[number, row] = held[number, row] + own[number, row]
+
+    loads[0].wait()
+    for chunk in range(CHUNKS):
+        add(0, chunk)
+        place.send(
+            held.at[0, chunk_of(chunk)],
+            over_x.at[chunk_of(chunk)],
+            x_sem.at[chunk],
+            (ep, place.over_x),
+        )
+    loads[1].wait()
+    for chunk in range(CHUNKS):
+        add(1, chunk)
+    for chunk in range(CHUNKS):
+        place.arrive(over_x.at[chunk_of(chunk)], x_sem.at[chunk])
+        for row in range(chunk * some, (chunk + 1) * some):
+            out_ref[row] = held[1, row].astype(jnp.float32) + over_x[row].astype(jnp.float32)
+    place.finish()
+
+
+def scatter_group(p, ident):
+    ep_size, tp_size, block, width = p.shape
+
+    def buffer(*lead):
+        return pltpu.VMEM((*lead, ep_size, block, width), p.dtype)
+
+    scratch = [buffer(2), buffer(2), buffer(), (2,), (CHUNKS * 3,), (2, CHUNKS), (CHUNKS,)]
+    out = jax.ShapeDtypeStruct((ep_size, block, width), jnp.float32)
+    return reach(scatter_group_kernel, out, scratch, ident, p, vmem_out=True, mib=24)
+
+
+def gather_kv_kernel(kv_ref, out_ref, own_sem, send_sem, recv_sem):
+    place = Place(send_sem)
+    ep, tp = place.ep, place.tp
+    own = pltpu.make_async_copy(kv_ref, out_ref.at[:, ep], own_sem)
+    own.start()
+    partners = [place.across(*where) for where in ((1, 0), (2, 0), (3, 0), (0, 1))]
+    place.greet([(partner, tp) for partner in partners])
+    for partner in (partners[3], *partners[:3]):
+        place.send(kv_ref, out_ref.at[:, ep], recv_sem.at[ep], (partner, tp))
+    for partner in partners[:3]:
+        block = out_ref.at[:, partner]
+        place.arrive(block, recv_sem.at[partner])
+        place.send(block, block, recv_sem.at[partner], (partners[3], tp))
+    for step in range(4):
+        other = place.across(step, 1)
+        place.arrive(out_ref.at[:, other], recv_sem.at[other])
+    own.wait()
+    place.finish()
+
+
+def gather_kv(kv, ep_size, ident):
+    blocks, rows, width = kv.shape
+    out = jax.ShapeDtypeStruct((blocks, ep_size, rows, width), kv.dtype)
+    scratch = [pltpu.SemaphoreType.DMA, (ep_size - 1,), (ep_size,)]
+    return reach(gather_kv_kernel, out, scratch, ident, kv)
+
+
+def scatter_kv_kernel(p_ref, out_ref, own, over_y, over_z, own_sem, send_sem, y_sem, z_sem):
+    place = Place(send_sem)
+    tp = place.tp
+    blocks = out_ref.shape[0]
+    order = (3, 2, 1, 0)
+    loads = {}
+    for step in order:
+        loads[step] = pltpu.make_async_copy(
+            p_ref.at[:, place.across(step, 0)], own.at[step], own_sem.at[step]
+        )
+        loads[step].start()
+    place.greet([(place.across(*where), tp) for where in ((1, 0), (2, 0), (3, 0), (0, 1))])
+    for step in order:
+        place.send(
+            p_ref.at[:, place.across(step, 1)],
+            over_y.at[step],
+            y_sem.at[step],
+            (place.across(0, 1), tp),
+        )
+    for step in order:
+        loads[step].wait()
+        place.arrive(over_y.at[step], y_sem.at[step])
+
+        @pl.loop(0, blocks)
+        def _(block, step=step):
+            own[step, block] = own[step, block] + over_y[step, block]
+
+        if step:
+            place.send(
+                own.at[step], over_z.at[step], z_sem.at[step], (place.across(step, 0), tp)
+            )
+    for step in (3, 2, 1):
+        place.arrive(over_z.at[step], z_sem.at[step])
+
+    @pl.loop(0, blocks)
+    def _(block):
+        total = own[0, block].astype(jnp.float32)
+        for step in (1, 2, 3):
+            total = total + over_z[step, block].astype(jnp.float32)
+        out_ref[block] = total.astype(jnp.bfloat16)
+
+    place.finish()
+
+
+def scatter_kv(p, ident):
+    blocks, ep_size, rows, width = p.shape
+    buffer = pltpu.VMEM((4, blocks, rows, width), p.dtype)
+    scratch = [buffer, buffer, buffer, (4,), (7,), (4,), (4,)]
+    out = jax.ShapeDtypeStruct((blocks, rows, width), p.dtype)
+    return reach(scatter_kv_kernel, out, scratch, ident, p, vmem_out=True, mib=24)
+
+
+def sum_small_kernel(x_ref, out_ref, total, arrived, own_sem, send_sem, recv_sem):
+    place = Place(send_sem)
+    own = pltpu.make_async_copy(x_ref, total.at[0], own_sem)
+    own.start()
+    own.wait()
+    ways = [(place.ep, place.over_core), (place.ep, place.over_x), (place.across(0, 1), place.tp)]
+    by_z = [(place.across(step, 0), place.tp) for step in (1, 2, 3)]
+    place.greet(ways + by_z)
+    for number, partner in enumerate(ways):
+        place.send(total.at[number], arrived.at[number], recv_sem.at[number], partner)
+        place.arrive(arrived.at[number], recv_sem.at[number])
+        total[number + 1] = total[number] + arrived[number]
+    for step in (1, 2, 3):
+        place.send(total.at[3], arrived.at[2 + step], recv_sem.at[2 + step], by_z[step - 1])
+    for step in (1, 2, 3):
+        place.arrive(arrived.at[2 + step], recv_sem.at[2 + step])
+    out_ref[...] = (total[3] + arrived[3]) + (arrived[4] + arrived[5])
+    place.finish()
+
+
+def sum_small(x, ident):
+    shape = x.shape
+    scratch = [pltpu.VMEM((4, *shape), x.dtype), pltpu.VMEM((6, *shape), x.dtype)]
+    scratch += [pltpu.SemaphoreType.DMA, (6,), (6,)]
+    out = jax.ShapeDtypeStruct(shape, x.dtype)
+    return reach(sum_small_kernel, out, scratch, ident, x, vmem_out=True)
 
 
 def on_device(
@@ -520,6 +1007,7 @@
     expert_count = ep_size * tp_size
     capacity = 2 * own_rows * TOP // expert_count
     heads = query_proj.shape[1] // HEAD
+    known = (ep_size, tp_size) == (8, 4)
     expert = (ep_index * tp_size + tp_index).astype(jnp.int32)[None]
 
     table = arrangement.reshape(ep_size, tp_size, ep_size, row_block)
@@ -531,35 +1019,41 @@
     ).astype(jnp.bfloat16)
 
     def to_places(rows):
-        moved = dot(mover, rows).astype(jnp.bfloat16).reshape(ep_size, row_block, width)
-        return lax.all_to_all(moved, "ep", split_axis=0, concat_axis=0, tiled=True).reshape(
-            own_rows, width
-        )
+        return dot(mover, rows).astype(jnp.bfloat16).reshape(ep_size, row_block, width)
+
+    def exchange(rows):
+        return lax.all_to_all(rows, "ep", split_axis=0, concat_axis=0, tiled=True)
 
     def to_given(rows):
-        moved = lax.all_to_all(
-            rows.astype(jnp.bfloat16).reshape(ep_size, row_block, width),
-            "ep",
-            split_axis=0,
-            concat_axis=0,
-            tiled=True,
-        ).reshape(own_rows, width)
-        return dot_with(mover, moved, ROWS_BY_ROWS)
-
-    def group_sorted(rows):
-        gathered = lax.all_gather(rows, "tp", axis=0, tiled=True)
-        gathered = gathered.reshape(tp_size, ep_size, row_block, rows.shape[1])
-        return jnp.swapaxes(gathered, 0, 1).reshape(group_rows, rows.shape[1])
-
-    def scatter_group(rows):
-        placed = rows.reshape(ep_size, tp_size, row_block, rows.shape[1])
-        placed = jnp.swapaxes(placed, 0, 1).reshape(group_rows, rows.shape[1])
-        return lax.psum_scatter(placed, "tp", scatter_dimension=0, tiled=True)
-
-    own_inputs = to_places(inputs)
-    own_cot = to_places(cotangent)
+        moved = exchange(rows.astype(jnp.bfloat16).reshape(ep_size, row_block, width))
+        return dot_with(mover, moved.reshape(own_rows, width), ROWS_BY_ROWS)
+
+    def group_sorted(rows, ident):
+        blocks = rows.reshape(ep_size, row_block, width)
+        if known:
+            gathered = gather_group(blocks, tp_size, ident)
+        else:
+            gathered = lax.all_gather(blocks, "tp", axis=1)
+        return gathered.reshape(group_rows, width)
+
+    def sum_group(rows, ident):
+        blocks = rows.astype(jnp.bfloat16).reshape(ep_size, tp_size, row_block, width)
+        if known:
+            return scatter_group(blocks, ident).reshape(own_rows, width)
+        placed = jnp.swapaxes(blocks, 0, 1).reshape(group_rows, width)
+        own = lax.psum_scatter(placed, "tp", scatter_dimension=0, tiled=True)
+        return own.astype(jnp.float32)
+
+    leaving_x, leaving_cot = to_places(inputs), to_places(cotangent)
+    if known:
+        group_x, own_cot = enter(leaving_x, leaving_cot, tp_size, 1)
+        own_inputs = lax.dynamic_index_in_dim(group_x, tp_index, 1, keepdims=False)
+    else:
+        own_inputs, own_cot = exchange(leaving_x), exchange(leaving_cot)
+        group_x = lax.all_gather(own_inputs, "tp", axis=1)
+    own_inputs, own_cot = own_inputs.reshape(own_rows, width), own_cot.reshape(own_rows, width)
+    group_x = group_x.reshape(group_rows, width)
     meta_own = jnp.concatenate([routes.astype(jnp.float32).T, gate_values.T], axis=0)
-    meta = lax.all_gather(meta_own, everyone, axis=0, tiled=False)
     cot_all = lax.all_gather(own_cot, everyone, axis=0, tiled=True)
 
     query_given = lax.dynamic_index_in_dim(table, ep_index, 0, keepdims=False)
@@ -580,39 +1074,47 @@
         [jnp.tile(given_steps, (1, heads)), jnp.tile(first_steps, (1, heads))], axis=1
     )
 
-    group_x = group_sorted(own_inputs)
     normed_in, query_raw, query_rows, key_raw, kv_rows = front(
         group_x, input_gain, query_proj, key_projected, value_projected,
         query_gain, key_gain, cosine, sine,
     )
-    kv_places = lax.all_gather(kv_rows, "ep", axis=0, tiled=True)
-    kv_all = jnp.transpose(
-        kv_places.reshape(ep_size, ep_size, tp_size, row_block, 2 * HEAD), (1, 2, 0, 3, 4)
-    ).reshape(token_total, 2 * HEAD)
+    kv_blocks = kv_rows.reshape(expert_count, row_block, 2 * HEAD)
+    if known:
+        kv_all = gather_kv(kv_blocks, ep_size, 2)
+    else:
+        kv_all = lax.all_gather(kv_blocks, "ep", axis=1)
+    kv_all = kv_all.reshape(token_total, 2 * HEAD)
     pairs = group_rows * heads * 1536
     exact, out_rows, lse = attend_forward(
         bounds, query_rows, ask, key_given[None], kv_all, pairs
     )
-    branch = scatter_group(dot(out_rows, output_proj).astype(jnp.bfloat16))
-    hidden = own_inputs.astype(jnp.float32) + branch.astype(jnp.float32)
+    branch = sum_group(dot(out_rows, output_proj), 5)
+    hidden = own_inputs.astype(jnp.float32) + branch
     mid_scale = inverse_root(hidden)
     normed_mid = (hidden * mid_scale * expert_gain).astype(jnp.bfloat16)
 
-    mid_all = lax.all_gather(normed_mid, everyone, axis=0, tiled=True)
-    mid_partial, expert_in, slot_cot, inner, gate_grad, up_grad = expert_pass(
+    normed_mid, cot_all = lax.optimization_barrier((normed_mid, cot_all))
+    if known:
+        mid_all, meta = gather_all(normed_mid, meta_own, expert_count, 3)
+    else:
+        mid_all = lax.all_gather(normed_mid, everyone, axis=0, tiled=True)
+        meta = lax.all_gather(meta_own, everyone, axis=0, tiled=True)
+    meta = meta.reshape(expert_count, 2 * TOP, own_rows)
+    mid_partial, out_partial, expert_in, slot_cot, inner, gate_grad, up_grad = expert_pass(
         expert, meta, mid_all, cot_all, gate_weight, up_weight, down_weight, capacity
     )
-    mid_grad = lax.psum_scatter(mid_partial, everyone, scatter_dimension=0, tiled=True).astype(
-        jnp.float32
-    )
-    out_partial = down_pass(expert, meta, inner, down_weight)
+    def sum_over_all(partial):
+        return lax.psum_scatter(partial, everyone, scatter_dimension=0, tiled=True)
+
+    if known:
+        mid_grad = scatter_all(mid_partial, expert_count, 4)
+    else:
+        mid_grad = sum_over_all(mid_partial).astype(jnp.float32)
     grad_down = dot_with(inner, slot_cot, ROWS_BY_ROWS)
     grad_gate = dot_with(expert_in, gate_grad, ROWS_BY_ROWS)
     grad_up = dot_with(expert_in, up_grad, ROWS_BY_ROWS)
-    mixed = lax.psum_scatter(out_partial, everyone, scatter_dimension=0, tiled=True).astype(
-        jnp.float32
-    )
-    layer_out = to_given(hidden + mixed).astype(jnp.bfloat16)
+    layer_out = to_given(hidden + sum_over_all(out_partial).astype(jnp.float32))
+    layer_out = layer_out.astype(jnp.bfloat16)
 
     mid_hat = hidden * mid_scale
     grad_expert_gain = jnp.sum(mid_grad * mid_hat, axis=0)
@@ -620,16 +1122,17 @@
     hidden_grad = own_cot.astype(jnp.float32) + mid_scale * (
         mid_scaled - mid_hat * jnp.mean(mid_scaled * mid_hat, axis=-1, keepdims=True)
     )
-    branch_grad = group_sorted(hidden_grad.astype(jnp.bfloat16))
+    branch_grad = group_sorted(hidden_grad.astype(jnp.bfloat16), 6)
     out_grad = dot_with(branch_grad, output_proj, COLS_BY_COLS).astype(jnp.bfloat16)
     query_grad, kv_grad = attend_backward(
         bounds, query_rows, out_grad, exact, lse, ask_rows, key_given[:, None], kv_all, pairs
     )
-    kv_grad = jnp.transpose(
-        kv_grad.astype(jnp.bfloat16).reshape(ep_size, tp_size, ep_size, row_block, 2 * HEAD),
-        (2, 0, 1, 3, 4),
-    ).reshape(token_total, 2 * HEAD)
-    kv_own = lax.psum_scatter(kv_grad, "ep", scatter_dimension=0, tiled=True)
+    kv_grad = kv_grad.reshape(expert_count, ep_size, row_block, 2 * HEAD)
+    if known:
+        kv_own = scatter_kv(kv_grad, 7)
+    else:
+        kv_own = lax.psum_scatter(kv_grad, "ep", scatter_dimension=1)
+    kv_own = kv_own.reshape(group_rows, 2 * HEAD)
     value_grad = kv_own[:, HEAD:]
     raw_query_grad, grad_query_gain = head_back(query_raw, query_grad, query_gain, cosine, sine)
     raw_key_grad, grad_key_gain = head_back(key_raw, kv_own[:, :HEAD], key_gain, cosine, sine)
@@ -638,7 +1141,7 @@
         + dot_with(raw_key_grad, key_projected, COLS_BY_COLS)
         + dot_with(value_grad, value_projected, COLS_BY_COLS)
     )
-    normed_grad = scatter_group(normed_grad.astype(jnp.bfloat16)).astype(jnp.float32)
+    normed_grad = sum_group(normed_grad, 8)
     own_float = own_inputs.astype(jnp.float32)
     in_scale = inverse_root(own_float)
     in_hat = own_float * in_scale
@@ -659,9 +1162,14 @@
     grad_kv = ep_sum(
         dot_with(normed_in, jnp.concatenate([raw_key_grad, value_grad], axis=1), ROWS_BY_ROWS)
     )
-    gains = lax.psum(
-        (grad_input_gain, grad_expert_gain, grad_query_gain[0], grad_key_gain[0]), everyone
-    )
+    gains = jnp.concatenate(
+        [grad_input_gain, grad_expert_gain, grad_query_gain[0], grad_key_gain[0]]
+    )
+    if known:
+        gains = sum_small(gains.reshape(-1, HEAD), 9).reshape(-1)
+    else:
+        gains = lax.psum(gains, everyone)
+    cuts = (width, 2 * width, 2 * width + HEAD)
     return (
         layer_out,
         grad_inputs,
@@ -669,10 +1177,10 @@
         grad_kv[:, :HEAD],
         grad_kv[:, HEAD:],
         grad_output,
-        gains[0],
-        gains[2],
-        gains[3],
-        gains[1],
+        gains[: cuts[0]],
+        gains[cuts[1] : cuts[2]],
+        gains[cuts[2] :],
+        gains[cuts[0] : cuts[1]],
         grad_gate[None],
         grad_up[None],
         grad_down[None],

time: 2110 us -> 1490 us (0.71)
  waiting for transfers between devices: 1440 us -> 121 us
  Pallas kernels: 285 us -> 1160 us
  blocking collectives: 149 us -> 0 us
    pallas_call x1 -> x9, Pallas kernels: 33.5 us -> 881 us  [reach(): pl.pallas_call(kernel, in_specs=[pl.BlockSpec(memory_space=pl.ANY)] * len...]
    reduce_scatter x5 -> x1, waiting for transfers between devices: 752 us -> 0.01 us  [sum_over_all(): return lax.psum_scatter(partial, everyone, scatter_dimension=0, tiled=True)]
    all_gather x4 -> x0, waiting for transfers between devices: 335 us -> none  [the longest x1 196 us: on_device(): mid_all = lax.all_gather(normed_mid, everyone, axis=0, tiled=True)]
    reduce_scatter x3, waiting for transfers between devices: 201 us -> 88.4 us  [ep_sum(): lax.psum_scatter(rows.astype(jnp.bfloat16), 'ep', scatter_dimension=0, ti...]
    all_gather x1, waiting for transfers between devices: 132 us -> 23.4 us  [on_device(): cot_all = lax.all_gather(own_cot, everyone, axis=0, tiled=True)]
    all_to_all x2 -> x0, blocking collectives: 61.7 us -> none  [to_places(): lax.all_to_all(moved, 'ep', split_axis=0, concat_axis=0, tiled=True)]
    all_gather x1 -> x0, blocking collectives: 47 us -> none  [on_device(): meta = lax.all_gather(meta_own, everyone, axis=0, tiled=False)]
    psum x1 -> x0, blocking collectives: 40.4 us -> none  [on_device(): lax.psum((grad_input_gain, grad_expert_gain, grad_query_gain[0], grad_key...]
  transfers between devices with their start and end apart: 15 -> 7, of which waited for: 13 -> 4; matrix products, arithmetic and copies ran while one was open for 6% -> 9% of each run, Pallas kernels for 2% -> 54%
where the time goes in v2:
time: 1490 us; the launch traced here: 1480 us
  Pallas kernels  1160 us (78%)
  waiting for transfers between devices  121 us (8%)
  matrix products  108 us (7%)
  local copies, waits for them, and re-layouts  41.9 us (3%)
  other arithmetic  25.4 us (2%)
    pallas_call x9, Pallas kernels, reach(): pl.pallas_call(kernel, in_specs=[pl.BlockSpec(memory_space=pl.ANY)] * len...  881 us
    pallas_call x1, Pallas kernels, expert_pass(): pl.pallas_call(expert_kernel, grid_spec=pltpu.PrefetchScalarGridSpec(num_...  131 us
    dot_general x12, matrix products, dot_with(): lax.dot_general(left, right, dims, preferred_element_type=jnp.float32)  101 us
    reduce_scatter x3, waiting for transfers between devices, ep_sum(): lax.psum_scatter(rows.astype(jnp.bfloat16), 'ep', scatter_dimension=0, ti...  88.4 us
    pallas_call x1, Pallas kernels, attend_backward(): pl.pallas_call(attend_backward_kernel, grid_spec=pltpu.PrefetchScalarGrid...  75.9 us
    pallas_call x1, Pallas kernels, attend_forward(): pl.pallas_call(attend_forward_kernel, grid_spec=pltpu.PrefetchScalarGridS...  51.4 us
    unnamed x91, local copies, waits for them, and re-layouts  30.7 us
  transfers between devices with their start and end apart: 7, of which 4 were waited for; matrix products, arithmetic and copies ran while one was open for 9% of the time, Pallas kernels for 54%

profile of v2, /device:TPU:0, one launch (start us, length us, event | category | flops | bytes accessed | tf_op | source)
XLA Modules:
  0.0 1477.9 jit_solution(13060609574619969076)
XLA Ops:
  10.8 51.1 %enter_kernel.1 = (bf16[8,4,32,2048]{3,2,1,0:T(8,128)(2,1)S(1)}, bf16[8,32,2048]{2,1,0:T(8,128)(2,1)}) custom-call(bf16[8,32,2048]{2,1,0:T(8,128)(2,1)S(1)} %bitcast.151, bf16[8,32,2048]{2,1,0:T(8,128)(2,1)S(1)} %bitcast.152), custom_call_target="tpu_custom_call" | custom-call | flops 1 | bytes 1 | tf_op jit(solution)/shard_map/enter_kernel/pallas_call | solution.py:542
  66.9 11.2 front.1
  83.0 90.6 %gather_kv_kernel.1 = bf16[32,8,32,256]{3,2,1,0:T(8,128)(2,1)S(1)} custom-call(bf16[32,32,256]{2,1,0:T(8,128)(2,1)S(1)} %bitcast.155), custom_call_target="tpu_custom_call" | custom-call | flops 1 | bytes 1 | tf_op jit(solution)/shard_map/gather_kv_kernel/pallas_call | solution.py:542
  176.7 51.4 %attend_forward.1 = (f32[1024,1024]{1,0:T(8,128)}, bf16[1024,1024]{1,0:T(8,128)(2,1)S(1)}, f32[32,1,256]{2,1,0:T(1,128)S(1)}) custom-call(s32[4,32]{1,0:T(4,128)S(1)} %pad_add_fusion.2.bounds_ref, bf16[1024,1024]{1,0:T(8,128)(2,1)S(1)} %get-tuple-element.41.q_ref, s32[1024,2]{1,0:T(8,128)S(1)} %copy.74.ask_ref, ...), custom_call_target="tpu_custom_call" | custom-call | flops 12884901888 | bytes 16777216 | tf_op jit(solution)/shard_map/attend_forward/pallas_call | solution.py:207
  232.9 47.7 %scatter_group_kernel.2 = f32[8,32,2048]{2,1,0:T(8,128)S(1)} custom-call(bf16[8,4,32,2048]{3,2,1,0:T(8,128)(2,1)S(1)} %bitcast.149), custom_call_target="tpu_custom_call" | custom-call | flops 1 | bytes 1 | tf_op jit(solution)/shard_map/scatter_group_kernel/pallas_call | solution.py:542
  285.6 23.4 %all-gather.2.cloned.1.call-done.c_ref = bf16[8192,2048]{1,0:T(8,128)(2,1)} async-done(((bf16[256,2048]{1,0:T(8,128)(2,1)}), bf16[8192,2048]{1,0:T(8,128)(2,1)}) %all-gather.2.cloned.1.call-update) | async-done | bytes 33554448 | tf_op jit(solution)/shard_map/all_gather | solution.py:1057
  309.0 176.6 %gather_all_kernel.1 = (bf16[8192,2048]{1,0:T(8,128)(2,1)S(1)}, f32[512,256]{1,0:T(8,128)S(1)}) custom-call(bf16[256,2048]{1,0:T(8,128)(2,1)S(1)} %get-tuple-element.45.x_ref, f32[16,256]{1,0:T(8,128)S(1)} %pad_maximum_fusion.2.m_ref), custom_call_target="tpu_custom_call" | custom-call | flops 1 | bytes 1 | tf_op jit(solution)/shard_map/gather_all_kernel/pallas_call | solution.py:542
  485.7 11.1 copy-done.26
  497.5 131.1 %expert_pass.1 = (bf16[8192,2048]{1,0:T(8,128)(2,1)}, bf16[8192,2048]{1,0:T(8,128)(2,1)}, bf16[4096,2048]{1,0:T(8,128)(2,1)}, bf16[4096,2048]{1,0:T(8,128)(2,1)}...) custom-call(s32[1]{0:T(128)} %bitcast.20.expert_ref, f32[32,16,256]{2,1,0:T(8,128)} %bitcast.163, ...), custom_call_target="tpu_custom_call" | custom-call | flops 64424509440 | bytes 157286400 | tf_op jit(solution)/shard_map/expert_pass/pallas_call | solution.py:404
  635.5 342.2 %scatter_all_kernel.1 = f32[256,2048]{1,0:T(8,128)} custom-call(bf16[8192,2048]{1,0:T(8,128)(2,1)} %get-tuple-element.50.p_ref), custom_call_target="tpu_custom_call" | custom-call | flops 1 | bytes 1 | tf_op jit(solution)/shard_map/scatter_all_kernel/pallas_call | solution.py:542
  982.0 50.2 %gather_group_kernel.1 = bf16[8,4,32,2048]{3,2,1,0:T(8,128)(2,1)S(1)} custom-call(bf16[8,32,2048]{2,1,0:T(8,128)(2,1)S(1)} %bitcast.150), custom_call_target="tpu_custom_call" | custom-call | flops 1 | bytes 1 | tf_op jit(solution)/shard_map/gather_group_kernel/pallas_call | solution.py:542
  1038.0 75.9 %attend_backward.1 = (f32[1024,1024]{1,0:T(8,128)}, bf16[8192,256]{1,0:T(8,128)(2,1)}) custom-call(s32[4,32]{1,0:T(4,128)} %copy-done.21, bf16[1024,1024]{1,0:T(8,128)(2,1)} %copy-done.31, bf16[1024,1024]{1,0:T(8,128)(2,1)} %convolution_convert_fusion.7.grad_ref, f32[1024,1024]{1,0:T(8,128)} %get-tuple-element.52.exact_ref, f32[32,1,256]{2,1,0:T(1,128)} %copy-done.33, ...), custom_call_target="tpu_custom_call" | custom-call | flops 32212254720 | bytes 33554432 | tf_op jit(solution)/shard_map/attend_backward/pallas_call | solution.py:308
  1116.2 68.8 %scatter_kv_kernel.1 = bf16[32,32,256]{2,1,0:T(8,128)(2,1)S(1)} custom-call(bf16[32,8,32,256]{3,2,1,0:T(8,128)(2,1)S(1)} %bitcast.148), custom_call_target="tpu_custom_call" | custom-call | flops 1 | bytes 1 | tf_op jit(solution)/shard_map/scatter_kv_kernel/pallas_call | solution.py:542
  1188.8 9.5 convolution_convert_fusion
  1204.4 6.0 head_back.2
  1219.3 31.5 %scatter_group_kernel.3 = f32[8,32,2048]{2,1,0:T(8,128)S(1)} custom-call(bf16[8,4,32,2048]{3,2,1,0:T(8,128)(2,1)S(1)} %bitcast.142), custom_call_target="tpu_custom_call" | custom-call | flops 1 | bytes 1 | tf_op jit(solution)/shard_map/scatter_group_kernel/pallas_call | solution.py:542
  1252.8 9.5 convolution_convert_fusion.1
  1262.3 21.4 %convolution_bitcast_fusion.1 = f32[1,2048,768]{2,1,0:T(8,128)} fusion(bf16[4096,2048]{1,0:T(8,128)(2,1)} %get-tuple-element.62, bf16[4096,768]{1,0:T(8,128)(2,1)} %get-tuple-element.64), kind=kOutput, calls=%fused_computation.2 | convolution fusion | flops 12884901888 | bytes 29360128 | tf_op jit(solution)/shard_map/dot_general | solution.py:29
  1283.7 6.0 fusion.3
  1293.4 21.0 %convolution_bitcast_fusion.2 = f32[1,2048,768]{2,1,0:T(8,128)} fusion(bf16[4096,2048]{1,0:T(8,128)(2,1)} %get-tuple-element.62, bf16[4096,768]{1,0:T(8,128)(2,1)} %get-tuple-element.63), kind=kOutput, calls=%fused_computation.3 | convolution fusion | flops 12884901888 | bytes 29360128 | tf_op jit(solution)/shard_map/dot_general | solution.py:29
  1314.4 9.6 all-to-all-done.1
  1328.5 20.3 %convolution_bitcast_fusion = f32[1,768,2048]{2,1,0:T(8,128)} fusion(bf16[4096,768]{1,0:T(8,128)(2,1)} %get-tuple-element.65, bf16[4096,2048]{1,0:T(8,128)(2,1)} %get-tuple-element.66), kind=kOutput, calls=%fused_computation.1 | convolution fusion | flops 12884901888 | bytes 29360128 | tf_op jit(solution)/shard_map/dot_general | solution.py:29
  1348.9 21.8 %sum_small_kernel.1 = f32[34,128]{1,0:T(8,128)S(1)} custom-call(f32[34,128]{1,0:T(8,128)S(1)} %maximum_bitcast_fusion.x_ref), custom_call_target="tpu_custom_call" | custom-call | flops 1 | bytes 1 | tf_op jit(solution)/shard_map/sum_small_kernel/pallas_call | solution.py:542
  1376.5 87.9 %reduce-scatter.7.cloned.1.call-done = bf16[256,1024]{1,0:T(8,128)(2,1)} async-done(((bf16[2048,1024]{1,0:T(8,128)(2,1)}), bf16[256,1024]{1,0:T(8,128)(2,1)}) %reduce-scatter.7.cloned.1.call-update) | async-done | bytes 524304 | tf_op jit(solution)/shard_map/reduce_scatter | solution.py:1156
  (171 shorter events, 87.3 us)
Async XLA Ops:
  7.2 57.1 %copy-start.41 = (s32[8]{0:T(128)S(1)}, s32[8]{0:T(128)}, u32[]{:S(2)}) copy-start(s32[8]{0:T(128)} %param.20) | copy-start | bytes 100
  7.2 301.8 %all-gather.2.cloned.1.call-start = ((), (), s32[]{:S(2)}) async-start(), calls=%async_computation.6 | async-start | bytes 34603008 | tf_op jit(solution)/shard_map/all_gather | solution.py:1057
  10.7 56.1 %copy-start.13 = (bf16[2048,128]{1,0:T(8,128)(2,1)S(1)}, bf16[2048,128]{1,0:T(8,128)(2,1)}, u32[]{:S(2)}) copy-start(bf16[2048,128]{1,0:T(8,128)(2,1)} %wk_ref.1) | copy-start | bytes 1572868
  10.7 56.1 %copy-start.15 = (bf16[2048,128]{1,0:T(8,128)(2,1)S(1)}, bf16[2048,128]{1,0:T(8,128)(2,1)}, u32[]{:S(2)}) copy-start(bf16[2048,128]{1,0:T(8,128)(2,1)} %wv_ref.1) | copy-start | bytes 1572868
  10.7 56.1 %copy-start.19 = (f32[2048]{0:T(1024)S(1)}, f32[2048]{0:T(1024)}, u32[]{:S(2)}) copy-start(f32[2048]{0:T(1024)} %param.23) | copy-start | bytes 24580
  10.8 56.1 %copy-start.22 = (f32[128]{0:T(128)S(1)}, f32[128]{0:T(128)}, u32[]{:S(2)}) copy-start(f32[128]{0:T(128)} %param.27) | copy-start | bytes 1540
  10.8 56.1 %copy-start.24 = (f32[128]{0:T(128)S(1)}, f32[128]{0:T(128)}, u32[]{:S(2)}) copy-start(f32[128]{0:T(128)} %param.28) | copy-start | bytes 1540
  63.9 1219.8 %reduce-scatter.5.cloned.1.call-start = ((), (), s32[]{:S(2)}) async-start(), calls=%async_computation.7 | async-start | bytes 34603008 | tf_op jit(solution)/shard_map/reduce_scatter | solution.py:1107
  83.0 145.1 %copy-start.31 = (bf16[1024,1024]{1,0:T(8,128)(2,1)}, bf16[1024,1024]{1,0:T(8,128)(2,1)S(1)}, u32[]{:S(2)}) copy-start(bf16[1024,1024]{1,0:T(8,128)(2,1)S(1)} %get-tuple-element.41.q_ref) | copy-start | bytes 6291460
  176.7 51.4 %copy-start.21 = (s32[4,32]{1,0:T(4,128)}, s32[4,32]{1,0:T(4,128)S(1)}, u32[]{:S(2)}) copy-start(s32[4,32]{1,0:T(4,128)S(1)} %pad_add_fusion.2.bounds_ref) | copy-start | bytes 1540
  176.7 51.4 %copy-start.42 = (bf16[1024,2048]{1,0:T(8,128)(2,1)S(1)}, bf16[1024,2048]{1,0:T(8,128)(2,1)}, u32[]{:S(2)}) copy-start(bf16[1024,2048]{1,0:T(8,128)(2,1)} %param.29) | copy-start | bytes 12582916
  628.6 743.2 %reduce-scatter.9.cloned.1.call-start = ((), (), s32[]{:S(2)}) async-start(), calls=%async_computation.9 | async-start | bytes 1179648 | tf_op jit(solution)/shard_map/reduce_scatter | solution.py:1156
  635.5 342.2 %copy-start.35 = (f32[256,2048]{1,0:T(8,128)S(1)}, f32[256,2048]{1,0:T(8,128)}, u32[]{:S(2)}) copy-start(f32[256,2048]{1,0:T(8,128)} %get-tuple-element.154) | copy-start | bytes 6291460
  1038.0 147.1 %copy-start.18 = (f32[1024,128]{1,0:T(8,128)S(1)}, f32[1024,128]{1,0:T(8,128)}, u32[]{:S(2)}) copy-start(f32[1024,128]{1,0:T(8,128)} %copy-done.17) | copy-start | bytes 1572868
  1038.0 147.1 %copy-start.25 = (f32[128]{0:T(128)S(1)}, f32[128]{0:T(128)}, u32[]{:S(2)}) copy-start(f32[128]{0:T(128)} %param.28) | copy-start | bytes 1540
  1113.8 71.3 %copy-start.4 = (f32[1024,128]{1,0:T(8,128)S(1)}, f32[1024,128]{1,0:T(8,128)}, u32[]{:S(2)}) copy-start(f32[1024,128]{1,0:T(8,128)} %copy-done.3) | copy-start | bytes 1572868
  1113.9 71.3 %copy-start.6 = (f32[1024,128]{1,0:T(8,128)S(1)}, f32[1024,128]{1,0:T(8,128)}, u32[]{:S(2)}) copy-start(f32[1024,128]{1,0:T(8,128)} %copy-done.5) | copy-start | bytes 1572868
  1116.2 69.9 %copy-start.30 = (bf16[1024,2048]{1,0:T(8,128)(2,1)S(1)}, bf16[1024,2048]{1,0:T(8,128)(2,1)}, u32[]{:S(2)}) copy-start(bf16[1024,2048]{1,0:T(8,128)(2,1)} %copy-done.29) | copy-start | bytes 12582916
  1188.5 185.4 %reduce-scatter.11.cloned.1.call-start = ((), (), s32[]{:S(2)}) async-start(), calls=%async_computation.10 | async-start | bytes 4718592 | tf_op jit(solution)/shard_map/reduce_scatter | solution.py:1156
  1198.3 266.0 %reduce-scatter.7.cloned.1.call-start = ((), (), s32[]{:S(2)}) async-start(), calls=%async_computation.8 | async-start | bytes 4718592 | tf_op jit(solution)/shard_map/reduce_scatter | solution.py:1156
  1289.6 34.4 %all-to-all-start.1 = ((bf16[8,32,2048]{2,1,0:T(8,128)(2,1)}), bf16[8,32,2048]{2,1,0:T(8,128)(2,1)S(1)}, u32[]{:S(2)}, u32[]{:S(2)}) async-start(bf16[8,32,2048]{2,1,0:T(8,128)(2,1)} %bitcast.165), calls=%async_computation.2 | async-start | bytes 2097152 | tf_op jit(solution)/shard_map/all_to_all | solution.py:1025
  1324.0 144.3 %all-to-all-start = ((bf16[8,32,2048]{2,1,0:T(8,128)(2,1)}), bf16[8,32,2048]{2,1,0:T(8,128)(2,1)}, u32[]{:S(2)}, u32[]{:S(2)}) async-start(bf16[8,32,2048]{2,1,0:T(8,128)(2,1)} %bitcast.26), calls=%async_computation.1 | async-start | bytes 2097152 | tf_op jit(solution)/shard_map/all_to_all | solution.py:1025
  1348.9 117.6 %copy-start.38 = (s32[256]{0:T(256)S(1)}, s32[256]{0:T(256)}, u32[]{:S(2)}) copy-start(s32[256]{0:T(256)} %copy-done.37) | copy-start | bytes 3076
  1373.9 97.2 %copy-start.1 = (bf16[256,2048]{1,0:T(8,128)(2,1)S(1)}, bf16[256,2048]{1,0:T(8,128)(2,1)}, u32[]{:S(2)}) copy-start(bf16[256,2048]{1,0:T(8,128)(2,1)} %param.17) | copy-start | bytes 3145732
  (28 other events, 227.3 us)
Sparse Core Ops, SparseCore 0:
  64.0 244.9 all-gather.1
  628.7 509.7 reduce-scatter.4
  1188.6 66.0 reduce-scatter.8
  1258.6 115.2 reduce-scatter.10
  1377.4 86.9 reduce-scatter.6

commit v3 on v2

--- a/solution.py
+++ b/solution.py
@@ -473,16 +473,21 @@
 
 
 class Place:
-    def __init__(self, send_sem, tp_size=4):
+    def __init__(self, send_sem, tp_size=4, nearest=False):
         self.tp_size, self.send_sem, self.sent = tp_size, send_sem, []
+        self.nearest = nearest
         self.ep, self.tp = lax.axis_index("ep"), lax.axis_index("tp")
         self.z, self.y, self.x, self.core = self.ep // 2, self.ep % 2, self.tp // 2, self.tp % 2
+        self.edge = 1 - (self.z + self.z // 2) % 2
         self.over_x = self.tp + 2 - 4 * self.x
         self.over_core = self.tp + 1 - 2 * self.core
         self.over_both = self.over_core + 2 - 4 * self.x
 
     def level(self, step):
-        return (self.z, self.z + 1 - 2 * (self.z % 2), (self.z + 2) % 4, 3 - self.z)[step]
+        levels = [self.z, self.z + 1 - 2 * (self.z % 2), (self.z + 2) % 4, 3 - self.z]
+        if self.nearest and step > 1:
+            return self.edge * levels[step] + (1 - self.edge) * levels[5 - step]
+        return levels[step]
 
     def across(self, step, over_y):
         return self.level(step) * 2 + self.y + over_y * (1 - 2 * self.y)
@@ -537,12 +542,14 @@
 
 def reach(kernel, out, scratch, ident, *operands, vmem_out=False, mib=None):
     dma = [kind if not isinstance(kind, tuple) else pltpu.SemaphoreType.DMA(kind) for kind in scratch]
-    space = pltpu.VMEM if vmem_out else pl.ANY
-    single = not isinstance(out, (list, tuple))
+    spaces = vmem_out if isinstance(vmem_out, tuple) else jax.tree.map(lambda _: vmem_out, out)
+    out_specs = jax.tree.map(
+        lambda vmem: pl.BlockSpec(memory_space=pltpu.VMEM if vmem else pl.ANY), spaces
+    )
     return pl.pallas_call(
         kernel,
         in_specs=[pl.BlockSpec(memory_space=pl.ANY)] * len(operands),
-        out_specs=jax.tree.map(lambda _: pl.BlockSpec(memory_space=space), out),
+        out_specs=out_specs,
         out_shape=out,
         scratch_shapes=dma,
         compiler_params=pltpu.CompilerParams(
@@ -555,71 +562,252 @@
     )(*operands)
 
 
-def gather_all_kernel(x_ref, m_ref, out_ref, lines_ref, own_sem, send_sem, recv_sem, line_sem):
-    place = Place(send_sem)
-    rows, lines = x_ref.shape[0], m_ref.shape[0]
-
-    def part(slot):
-        return out_ref.at[pl.ds(slot * rows, rows)]
-
-    def some(slot):
-        return lines_ref.at[pl.ds(slot * lines, lines)]
-
-    def send(where, partner):
-        slot = place.slot(*where)
-        own = where == (0, 0, 0)
-        device = place.device(*partner)
-        place.send(m_ref if own else some(slot), some(slot), line_sem.at[slot], device)
-        place.send(x_ref if own else part(slot), part(slot), recv_sem.at[slot], device)
-
-    def arrive(*where):
-        slot = place.slot(*where)
-        place.arrive(some(slot), line_sem.at[slot])
-        place.arrive(part(slot), recv_sem.at[slot])
-
-    mine = place.slot(0, 0, 0)
+NEAR = ((0, 0), (1, 0), (0, 1), (2, 0), (1, 1), (3, 0), (2, 1), (3, 1))
+ORDER = tuple((*where, 0) for where in NEAR[:6])
+ORDER += ((0, 0, 1), (2, 1, 0), (1, 0, 1), (3, 1, 0), (0, 1, 1))
+ORDER += tuple((*where, 1) for where in NEAR[3:])
+
+
+def expert_all_kernel(
+    x_ref, m_ref, c_ref, wg_ref, wu_ref, wd_ref,
+    all_ref, mid_ref, out_ref, xs_ref, cs_ref, inner_ref, gg_ref, ug_ref,
+    lines, wg, wu, wd, pair, xb, cb, midb, outb, xsb, csb, innerb, ggb, ugb,
+    w_sem, own_sem, z_sem, z_line_sem, send_sem, line_send_sem, recv_sem, line_sem,
+    load_sem, store_sem,
+):
+    place = Place(send_sem, nearest=True)
+    rows = x_ref.shape[0]
+    capacity = xsb.shape[1] // 2
+    expert = (place.ep * 4 + place.tp).astype(jnp.float32)
+    count = len(ORDER)
+    slots = {(*where, other): place.slot(*where, other) for where in ORDER for other in (0, 1)}
+    first, second, across = place.device(0, 1, 0), place.device(0, 0, 1), place.device(0, 0, 0, 1)
+
+    def part(ref, slot):
+        return ref.at[pl.ds(slot * rows, rows)]
+
+    weights = [
+        pltpu.make_async_copy(ref, held, w_sem.at[number])
+        for number, (ref, held) in enumerate(((wg_ref, wg), (wu_ref, wu), (wd_ref, wd)))
+    ]
+    mine = slots[0, 0, 0, 0]
     own = [
-        pltpu.make_async_copy(x_ref, part(mine), own_sem.at[0]),
-        pltpu.make_async_copy(m_ref, some(mine), own_sem.at[1]),
+        pltpu.make_async_copy(x_ref, part(all_ref, mine), own_sem.at[0]),
+        pltpu.make_async_copy(m_ref, lines.at[mine], own_sem.at[1]),
     ]
-    for copy in own:
+    for copy in own + weights:
         copy.start()
     place.greet_all_ways()
-    for step in (1, 2, 3):
-        send((0, 0, 0), (step, 0, 0))
-    for step in range(4):
-        if step:
-            arrive(step, 0, 0)
-        send((step, 0, 0), (0, 1, 0))
-        send((step, 0, 0), (0, 0, 1))
-        send((step, 0, 0), (0, 0, 0, 1))
-        if step:
-            arrive(step - 1, 1, 0)
-            send((step - 1, 1, 0), (0, 0, 1))
-            send((step - 1, 1, 0), (0, 0, 0, 1))
-    arrive(3, 1, 0)
-    send((3, 1, 0), (0, 0, 1))
-    send((3, 1, 0), (0, 0, 0, 1))
-    for step in range(4):
-        for first in (0, 1):
-            arrive(step, first, 1)
-            send((step, first, 1), (0, 0, 0, 1))
-    for step in range(4):
-        for first in (0, 1):
-            for second in (0, 1):
-                arrive(step, first, second, 1)
     for copy in own:
         copy.wait()
-    place.finish()
-
-
-def gather_all(x, lines, parts, ident):
-    out = [
-        jax.ShapeDtypeStruct((parts * array.shape[0], array.shape[1]), array.dtype)
-        for array in (x, lines)
-    ]
-    scratch = [(2,), (2 * parts - 2,), (parts,), (parts,)]
-    return reach(gather_all_kernel, out, scratch, ident, x, lines)
+
+    def copies(slot, device, rows_sem, words_sem):
+        some = dict(device_id=device, device_id_type=MESH_ID)
+        return (
+            pltpu.make_async_remote_copy(
+                src_ref=lines.at[slot], dst_ref=lines.at[slot],
+                send_sem=words_sem, recv_sem=line_sem.at[slot], **some,
+            ),
+            pltpu.make_async_remote_copy(
+                src_ref=part(all_ref, slot), dst_ref=part(all_ref, slot),
+                send_sem=rows_sem, recv_sem=recv_sem.at[slot], **some,
+            ),
+        )
+
+    def along_z(step):
+        level, z = place.level(step), place.z
+        up = (z < 3) if step == 0 else (level < z) & (z < 3)
+        down = (z > 0) if step == 0 else (level > z) & (z > 0)
+        return ((up, 2 * step, (place.ep + 2, place.tp)), (down, 2 * step + 1, (place.ep - 2, place.tp)))
+
+    def z_copies(slot, number, device):
+        return copies(slot, device, z_sem.at[number], z_line_sem.at[number])
+
+    sends = []
+    for where in ORDER:
+        targets = [across]
+        if where[2] == 0:
+            targets = [second, *targets]
+        if where[1:] == (0, 0):
+            targets = [first, *targets]
+        sends.append(targets)
+    starts = [sum(len(targets) for targets in sends[:number]) for number in range(count)]
+
+    def arrive(slot):
+        for copy in copies(slot, across, send_sem.at[0], line_send_sem.at[0]):
+            copy.wait_recv()
+
+    def onward_z(step):
+        for wanted, index, device in along_z(step):
+
+            @pl.when(wanted)
+            def _(index=index, device=device):
+                for copy in z_copies(slots[step, 0, 0, 0], index, device):
+                    copy.start()
+
+    relays = {1: 2, 3: 3}
+
+    def event(number):
+        where = ORDER[number]
+        slot = slots[(*where, 0)]
+        if where[0] in relays.values() and where[1:] == (0, 0):
+
+            @pl.when(place.edge == 1)
+            def _():
+                arrive(slot)
+
+        elif number:
+            arrive(slot)
+        if where in ((0, 0, 0), (1, 0, 0)):
+            onward_z(where[0])
+        if number in relays:
+            step = relays[number]
+
+            @pl.when(place.edge == 0)
+            def _():
+                arrive(slots[step, 0, 0, 0])
+                onward_z(step)
+
+        for index, device in enumerate(sends[number], starts[number]):
+            for copy in copies(slot, device, send_sem.at[index], line_send_sem.at[index]):
+                copy.start()
+
+    def load_copies(slot, parity, half):
+        return (
+            pltpu.make_async_copy(part(all_ref, slot), xb.at[parity, half], load_sem.at[parity, half]),
+            pltpu.make_async_copy(part(c_ref, slot), cb.at[parity, half], load_sem.at[parity, 2 + half]),
+        )
+
+    def load(number):
+        where, parity = ORDER[number], number % 2
+        arrive(slots[(*where, 1)])
+        for half in (0, 1):
+            slot = slots[(*where, half)]
+            pair[parity, half] = lines[slot]
+            for copy in load_copies(slot, parity, half):
+                copy.start()
+
+    def store_copies(number, parity, both):
+        kept = pl.ds(number * 2 * capacity, 2 * capacity)
+        moves = [(held.at[parity], ref.at[kept]) for held, ref in (
+            (xsb, xs_ref), (csb, cs_ref), (innerb, inner_ref), (ggb, gg_ref), (ugb, ug_ref),
+        )]
+        for half in (0, 1):
+            moves.append((midb.at[parity, half], part(mid_ref, both[half])))
+            moves.append((outb.at[parity, half], part(out_ref, both[half])))
+        return [
+            pltpu.make_async_copy(held, ref, store_sem.at[parity, index])
+            for index, (held, ref) in enumerate(moves)
+        ]
+
+    def compute(parity):
+        picks, gates = [], []
+        for half in (0, 1):
+            pick, gate = selection(pair[parity, half], expert, capacity)
+            picks.append(pick)
+            gates.append(gate)
+            some = slice(half * capacity, (half + 1) * capacity)
+            xsb[parity, some] = dot(pick, xb[parity, half]).astype(jnp.bfloat16)
+            csb[parity, some] = (dot(pick, cb[parity, half]) * gate).astype(jnp.bfloat16)
+        expert_in, slot_cot = xsb[parity], csb[parity]
+        gate_part = dot(expert_in, wg[0])
+        up_part = dot(expert_in, wu[0])
+        inner_grad = dot_with(slot_cot, wd[0], COLS_BY_COLS)
+        gate_sig = jax.nn.sigmoid(gate_part)
+        activated = gate_part * gate_sig
+        inner = (activated * up_part).astype(jnp.bfloat16)
+        innerb[parity] = inner
+        gate_grad = inner_grad * up_part * gate_sig * (1.0 + gate_part * (1.0 - gate_sig))
+        gate_grad = gate_grad.astype(jnp.bfloat16)
+        up_grad = (inner_grad * activated).astype(jnp.bfloat16)
+        ggb[parity] = gate_grad
+        ugb[parity] = up_grad
+        slot_grad = dot_with(gate_grad, wg[0], COLS_BY_COLS)
+        slot_grad = (slot_grad + dot_with(up_grad, wu[0], COLS_BY_COLS)).astype(jnp.bfloat16)
+        result = dot(inner, wd[0]).astype(jnp.bfloat16).astype(jnp.float32)
+        for half in (0, 1):
+            some = slice(half * capacity, (half + 1) * capacity)
+            midb[parity, half] = dot_with(picks[half], slot_grad[some], ROWS_BY_ROWS).astype(
+                jnp.bfloat16
+            )
+            scaled = (result[some] * gates[half]).astype(jnp.bfloat16)
+            outb[parity, half] = dot_with(picks[half], scaled, ROWS_BY_ROWS).astype(jnp.bfloat16)
+
+    @pl.loop(0, count + 2)
+    def _(turn):
+        for number in range(count):
+
+            @pl.when(turn == number)
+            def _(number=number):
+                event(number)
+
+        for number in range(count):
+
+            @pl.when(turn == number + 1)
+            def _(number=number):
+                load(number)
+
+        @pl.when(turn == 2)
+        def _():
+            for copy in weights:
+                copy.wait()
+
+        @pl.when(turn >= 2)
+        def _():
+            parity = turn % 2
+            for half in (0, 1):
+                for copy in load_copies(0, parity, half):
+                    copy.wait()
+
+            @pl.when(turn >= 4)
+            def _():
+                for copy in store_copies(0, parity, (0, 0)):
+                    copy.wait()
+
+            compute(parity)
+
+        for number in range(count):
+
+            @pl.when(turn == number + 2)
+            def _(number=number):
+                both = [slots[(*ORDER[number], half)] for half in (0, 1)]
+                for copy in store_copies(number, number % 2, both):
+                    copy.start()
+
+    for parity in (0, 1):
+        for copy in store_copies(0, parity, (0, 0)):
+            copy.wait()
+    for index in range(sum(len(targets) for targets in sends)):
+        for copy in copies(0, across, send_sem.at[index], line_send_sem.at[index]):
+            copy.wait_send()
+    for step in range(4):
+        for wanted, index, device in along_z(step):
+
+            @pl.when(wanted)
+            def _(index=index, device=device):
+                for copy in z_copies(0, index, device):
+                    copy.wait_send()
+
+
+def expert_all(x, lines, c_all, gate_w, up_w, down_w, capacity, ident):
+    rows, width = x.shape
+    blocks = c_all.shape[0] // rows
+    hidden = gate_w.shape[2]
+    total = blocks * capacity
+    shapes = [c_all.shape] * 3 + [(total, width)] * 2 + [(total, hidden)] * 3
+    out = [jax.ShapeDtypeStruct(shape, jnp.bfloat16) for shape in shapes]
+
+    def buffer(*shape):
+        return pltpu.VMEM(shape, jnp.bfloat16)
+
+    scratch = [pltpu.VMEM((blocks, *lines.shape), jnp.float32)]
+    scratch += [buffer(*gate_w.shape), buffer(*up_w.shape), buffer(*down_w.shape)]
+    scratch += [pltpu.VMEM((2, 2, *lines.shape), jnp.float32)]
+    scratch += [buffer(2, 2, rows, width)] * 4 + [buffer(2, 2 * capacity, width)] * 2
+    scratch += [buffer(2, 2 * capacity, hidden)] * 3
+    scratch += [(3,), (2,), (8,), (8,), (28,), (28,), (blocks,), (blocks,), (2, 4), (2, 9)]
+    operands = (x, lines, c_all, gate_w, up_w, down_w)
+    return reach(expert_all_kernel, out, scratch, ident, *operands, mib=58)[1:]
 
 
 BUFFERS = 4
@@ -948,32 +1136,231 @@
     return reach(scatter_kv_kernel, out, scratch, ident, p, vmem_out=True, mib=24)
 
 
-def sum_small_kernel(x_ref, out_ref, total, arrived, own_sem, send_sem, recv_sem):
+SLOTS = 1024
+
+
+def finish_kernel(*refs):
+    partials, gains_ref, rows_ref, experts = refs[:3], refs[3], refs[4], refs[5:10]
+    outs, gain_out, rows_out, grads, refs = refs[10:13], refs[13], refs[14], refs[15:18], refs[18:]
+    owns, overs_y, overs_z, stages, refs = refs[:3], refs[3:6], refs[6:9], refs[9:11], refs[11:]
+    wide, narrow, sums, refs = refs[0], refs[1], refs[2:5], refs[5:]
+    own_sem, send_sem, y_sem, z_sem, gain_sem, load_sem, grad_sem, rows_sem, rows_send_sem = refs
     place = Place(send_sem)
-    own = pltpu.make_async_copy(x_ref, total.at[0], own_sem)
-    own.start()
-    own.wait()
-    ways = [(place.ep, place.over_core), (place.ep, place.over_x), (place.across(0, 1), place.tp)]
-    by_z = [(place.across(step, 0), place.tp) for step in (1, 2, 3)]
-    place.greet(ways + by_z)
-    for number, partner in enumerate(ways):
-        place.send(total.at[number], arrived.at[number], recv_sem.at[number], partner)
-        place.arrive(arrived.at[number], recv_sem.at[number])
-        total[number + 1] = total[number] + arrived[number]
-    for step in (1, 2, 3):
-        place.send(total.at[3], arrived.at[2 + step], recv_sem.at[2 + step], by_z[step - 1])
-    for step in (1, 2, 3):
-        place.arrive(arrived.at[2 + step], recv_sem.at[2 + step])
-    out_ref[...] = (total[3] + arrived[3]) + (arrived[4] + arrived[5])
-    place.finish()
-
-
-def sum_small(x, ident):
-    shape = x.shape
-    scratch = [pltpu.VMEM((4, *shape), x.dtype), pltpu.VMEM((6, *shape), x.dtype)]
-    scratch += [pltpu.SemaphoreType.DMA, (6,), (6,)]
-    out = jax.ShapeDtypeStruct(shape, x.dtype)
-    return reach(sum_small_kernel, out, scratch, ident, x, vmem_out=True)
+    ep, tp = place.ep, place.tp
+    count = len(partials)
+    total, arrived = stages
+    ways = [(ep, place.over_core), (ep, place.over_x)]
+    ways += [(place.across(step, 0), tp) for step in (1, 2, 3)]
+    ways.append((place.across(0, 1), tp))
+    moves = [(number, step) for step in (3, 2, 1, 0) for number in range(count)]
+    gain_load = pltpu.make_async_copy(gains_ref, total.at[0], own_sem.at[count, 0])
+    gain_load.start()
+
+    def own_copy(number, step):
+        return pltpu.make_async_copy(
+            partials[number].at[place.across(step, 0)],
+            owns[number].at[step],
+            own_sem.at[number, step],
+        )
+
+    def to_y(number, step):
+        return pltpu.make_async_remote_copy(
+            src_ref=partials[number].at[place.across(step, 1)],
+            dst_ref=overs_y[number].at[step],
+            send_sem=send_sem.at[number, step],
+            recv_sem=y_sem.at[number, step],
+            device_id=(place.across(0, 1), tp),
+            device_id_type=MESH_ID,
+        )
+
+    def to_z(number, step):
+        return pltpu.make_async_remote_copy(
+            src_ref=owns[number].at[step],
+            dst_ref=overs_z[number].at[step],
+            send_sem=send_sem.at[number, 3 + step],
+            recv_sem=z_sem.at[number, step],
+            device_id=(place.across(step, 0), tp),
+            device_id_type=MESH_ID,
+        )
+
+    def gain_copy(number):
+        return pltpu.make_async_remote_copy(
+            src_ref=total.at[(0, 1, 2, 2, 2, 3)[number]],
+            dst_ref=arrived.at[number],
+            send_sem=send_sem.at[count, number],
+            recv_sem=gain_sem.at[number],
+            device_id=ways[number],
+            device_id_type=MESH_ID,
+        )
+
+    others = [(step, over) for step in range(4) for over in (0, 1)][1:]
+
+    def row_copy(index):
+        other = place.across(*others[index])
+        return pltpu.make_async_remote_copy(
+            src_ref=rows_ref.at[other],
+            dst_ref=rows_out.at[ep],
+            send_sem=rows_send_sem.at[index],
+            recv_sem=rows_sem.at[ep],
+            device_id=(other, tp),
+            device_id_type=MESH_ID,
+        )
+
+    def row_arrival(index):
+        other = place.across(*others[index])
+        return pltpu.make_async_remote_copy(
+            src_ref=rows_ref.at[other],
+            dst_ref=rows_out.at[other],
+            send_sem=rows_send_sem.at[index],
+            recv_sem=rows_sem.at[other],
+            device_id=(other, tp),
+            device_id_type=MESH_ID,
+        )
+
+    own_rows = pltpu.make_async_copy(rows_ref.at[ep], rows_out.at[ep], rows_sem.at[ep])
+    own_rows.start()
+    for number, step in moves:
+        own_copy(number, step).start()
+    place.greet(ways[:2] + [(place.across(*other), tp) for other in others])
+    gain_load.wait()
+    gain_copy(0).start()
+    for index in range(len(others)):
+        row_copy(index).start()
+    for number, step in moves:
+        to_y(number, step).start()
+
+    def event(index):
+        number, step = moves[index]
+        own, over = owns[number], overs_y[number]
+        own_copy(number, step).wait()
+        to_y(number, step).wait_recv()
+
+        @pl.loop(0, own.shape[1], step=64)
+        def _(row):
+            some = pl.ds(row, 64)
+            own[step, some] = own[step, some] + over[step, some]
+
+        if step:
+            to_z(number, step).start()
+        if index < 2:
+            gain_copy(index).wait_recv()
+            total[index + 1] = total[index] + arrived[index]
+            for later in (1,) if index == 0 else (2, 3, 4):
+                gain_copy(later).start()
+        if index == 2:
+            for later in (2, 3, 4):
+                gain_copy(later).wait_recv()
+            total[3] = (total[2] + arrived[2]) + (arrived[3] + arrived[4])
+            gain_copy(5).start()
+
+    expert_in, slot_cot, inner, gate_grad, up_grad = experts
+    pieces = expert_in.shape[0] // SLOTS
+    jobs = ((expert_in, gate_grad), (expert_in, up_grad), (slot_cot, inner))
+    steps = pieces * len(jobs)
+
+    def load_copies(pair, piece, parity):
+        some = pl.ds(piece * SLOTS, SLOTS)
+        return [
+            pltpu.make_async_copy(ref.at[some], held.at[parity], load_sem.at[parity, index])
+            for index, (ref, held) in enumerate(zip(pair, (wide, narrow)))
+        ]
+
+    def grad_copy(job):
+        return pltpu.make_async_copy(sums[job], grads[job], grad_sem.at[job])
+
+    def multiply(job, parity):
+        into = sums[job]
+        left, right = (wide, narrow) if job < 2 else (narrow, wide)
+        tile = 512 if into.shape[0] % 512 == 0 else 384
+
+        @pl.loop(0, into.shape[0], step=tile)
+        def _(row):
+            some = pl.ds(pl.multiple_of(row, tile), tile)
+            product = dot_with(left[parity, :, some], right[parity], ROWS_BY_ROWS)
+
+            into[some] += product
+
+    for into in sums:
+
+        @pl.loop(0, into.shape[0], step=64)
+        def _(row, into=into):
+            into[pl.ds(row, 64)] = jnp.zeros((64, into.shape[1]), jnp.float32)
+
+    @pl.loop(0, steps + 1)
+    def _(turn):
+        for index in range(len(moves)):
+
+            @pl.when(turn == index)
+            def _(index=index):
+                event(index)
+
+        for job, pair in enumerate(jobs):
+
+            @pl.when((turn >= job * pieces) & (turn < (job + 1) * pieces))
+            def _(job=job, pair=pair):
+                for copy in load_copies(pair, turn - job * pieces, turn % 2):
+                    copy.start()
+
+        for job, pair in enumerate(jobs):
+
+            @pl.when((turn > job * pieces) & (turn <= (job + 1) * pieces))
+            def _(job=job, pair=pair):
+                parity = (turn - 1) % 2
+                for copy in load_copies(pair, 0, parity):
+                    copy.wait()
+                multiply(job, parity)
+
+            @pl.when(turn == (job + 1) * pieces)
+            def _(job=job):
+                grad_copy(job).start()
+
+    for number in range(count):
+        own, over, out = owns[number], overs_z[number], outs[number]
+        for step in (3, 2, 1):
+            to_z(number, step).wait_recv()
+
+        @pl.loop(0, own.shape[1], step=64)
+        def _(row, own=own, over=over, out=out):
+            some = pl.ds(row, 64)
+            sum_of = own[0, some].astype(jnp.float32)
+            for step in (1, 2, 3):
+                sum_of = sum_of + over[step, some].astype(jnp.float32)
+            out[some] = sum_of
+
+    gain_copy(5).wait_recv()
+    gain_out[...] = total[3] + arrived[5]
+    for job in range(len(jobs)):
+        grad_copy(job).wait()
+    for number, step in moves:
+        to_y(number, step).wait_send()
+        if step:
+            to_z(number, step).wait_send()
+    for number in range(6):
+        gain_copy(number).wait_send()
+    own_rows.wait()
+    for index in range(len(others)):
+        row_copy(index).wait_send()
+        row_arrival(index).wait_recv()
+
+
+def finish(partials, gains, rows, expert_in, slot_cot, inner, gate_grad, up_grad, ident):
+    count = len(partials)
+    buffers = [pltpu.VMEM((4, *p.shape[1:]), p.dtype) for p in partials]
+    width, hidden = expert_in.shape[1], inner.shape[1]
+    grads = [(width, hidden), (width, hidden), (hidden, width)]
+    scratch = buffers * 3
+    scratch += [pltpu.VMEM((4, *gains.shape), gains.dtype), pltpu.VMEM((6, *gains.shape), gains.dtype)]
+    scratch += [pltpu.VMEM((2, SLOTS, width), jnp.bfloat16), pltpu.VMEM((2, SLOTS, hidden), jnp.bfloat16)]
+    scratch += [pltpu.VMEM(shape, jnp.float32) for shape in grads]
+    scratch += [(count + 1, 4), (count + 1, 7), (count, 4), (count, 4), (6,), (2, 2), (3,), (8,), (7,)]
+    out = [jax.ShapeDtypeStruct(p.shape[1:], jnp.float32) for p in partials]
+    out.append(jax.ShapeDtypeStruct(gains.shape, jnp.float32))
+    out.append(jax.ShapeDtypeStruct(rows.shape, rows.dtype))
+    out += [jax.ShapeDtypeStruct(shape, jnp.float32) for shape in grads]
+    operands = (*partials, gains, rows, expert_in, slot_cot, inner, gate_grad, up_grad)
+    return reach(
+        finish_kernel, out, scratch, ident, *operands, vmem_out=(True,) * 4 + (False,) * 4, mib=58
+    )
 
 
 def on_device(
@@ -1024,8 +1411,10 @@
     def exchange(rows):
         return lax.all_to_all(rows, "ep", split_axis=0, concat_axis=0, tiled=True)
 
-    def to_given(rows):
-        moved = exchange(rows.astype(jnp.bfloat16).reshape(ep_size, row_block, width))
+    def by_source(rows):
+        return rows.astype(jnp.bfloat16).reshape(ep_size, row_block, width)
+
+    def to_given(moved):
         return dot_with(mover, moved.reshape(own_rows, width), ROWS_BY_ROWS)
 
     def group_sorted(rows, ident):
@@ -1093,16 +1482,14 @@
     mid_scale = inverse_root(hidden)
     normed_mid = (hidden * mid_scale * expert_gain).astype(jnp.bfloat16)
 
-    normed_mid, cot_all = lax.optimization_barrier((normed_mid, cot_all))
+    experts = (gate_weight, up_weight, down_weight, capacity)
     if known:
-        mid_all, meta = gather_all(normed_mid, meta_own, expert_count, 3)
+        results = expert_all(normed_mid, meta_own, cot_all, *experts, 3)
     else:
         mid_all = lax.all_gather(normed_mid, everyone, axis=0, tiled=True)
-        meta = lax.all_gather(meta_own, everyone, axis=0, tiled=True)
-    meta = meta.reshape(expert_count, 2 * TOP, own_rows)
-    mid_partial, out_partial, expert_in, slot_cot, inner, gate_grad, up_grad = expert_pass(
-        expert, meta, mid_all, cot_all, gate_weight, up_weight, down_weight, capacity
-    )
+        meta = lax.all_gather(meta_own, everyone, axis=0)
+        results = expert_pass(expert, meta, mid_all, cot_all, *experts)
+    mid_partial, out_partial, expert_in, slot_cot, inner, gate_grad, up_grad = results
     def sum_over_all(partial):
         return lax.psum_scatter(partial, everyone, scatter_dimension=0, tiled=True)
 
@@ -1110,11 +1497,8 @@
         mid_grad = scatter_all(mid_partial, expert_count, 4)
     else:
         mid_grad = sum_over_all(mid_partial).astype(jnp.float32)
-    grad_down = dot_with(inner, slot_cot, ROWS_BY_ROWS)
-    grad_gate = dot_with(expert_in, gate_grad, ROWS_BY_ROWS)
-    grad_up = dot_with(expert_in, up_grad, ROWS_BY_ROWS)
-    layer_out = to_given(hidden + sum_over_all(out_partial).astype(jnp.float32))
-    layer_out = layer_out.astype(jnp.bfloat16)
+    mid_grad, out_partial = lax.optimization_barrier((mid_grad, out_partial))
+    mixed = sum_over_all(out_partial)
 
     mid_hat = hidden * mid_scale
     grad_expert_gain = jnp.sum(mid_grad * mid_hat, axis=0)
@@ -1147,28 +1531,40 @@
     in_hat = own_float * in_scale
     grad_input_gain = jnp.sum(normed_grad * in_hat, axis=0)
     in_scaled = normed_grad * input_gain
-    grad_inputs = to_given(
+    input_rows = by_source(
         hidden_grad
         + in_scale * (in_scaled - in_hat * jnp.mean(in_scaled * in_hat, axis=-1, keepdims=True))
     )
 
-    def ep_sum(rows):
-        return lax.psum_scatter(
-            rows.astype(jnp.bfloat16), "ep", scatter_dimension=0, tiled=True
-        ).astype(jnp.float32)
-
-    grad_output = jnp.transpose(ep_sum(dot_with(branch_grad, out_rows, ROWS_BY_ROWS)))
-    grad_query = ep_sum(dot_with(normed_in, raw_query_grad, ROWS_BY_ROWS))
-    grad_kv = ep_sum(
-        dot_with(normed_in, jnp.concatenate([raw_key_grad, value_grad], axis=1), ROWS_BY_ROWS)
-    )
+    weights = [
+        dot_with(branch_grad, out_rows, ROWS_BY_ROWS),
+        dot_with(normed_in, raw_query_grad, ROWS_BY_ROWS),
+        dot_with(normed_in, jnp.concatenate([raw_key_grad, value_grad], axis=1), ROWS_BY_ROWS),
+    ]
+    weights = [array.astype(jnp.bfloat16).reshape(ep_size, -1, array.shape[1]) for array in weights]
     gains = jnp.concatenate(
         [grad_input_gain, grad_expert_gain, grad_query_gain[0], grad_key_gain[0]]
     )
     if known:
-        gains = sum_small(gains.reshape(-1, HEAD), 9).reshape(-1)
+        experts = (expert_in, slot_cot, inner, gate_grad, up_grad)
+        results = finish(weights, gains.reshape(-1, HEAD), input_rows, *experts, 10)
+        grad_output, grad_query, grad_kv, gains, input_rows = results[:5]
+        grad_gate, grad_up, grad_down = results[5:]
+        gains = gains.reshape(-1)
     else:
-        gains = lax.psum(gains, everyone)
+        grad_output, grad_query, grad_kv = [
+            lax.psum_scatter(array, "ep", scatter_dimension=0).astype(jnp.float32)
+            for array in weights
+        ]
+        gains, input_rows = lax.psum(gains, everyone), exchange(input_rows)
+        grad_gate = dot_with(expert_in, gate_grad, ROWS_BY_ROWS)
+        grad_up = dot_with(expert_in, up_grad, ROWS_BY_ROWS)
+        grad_down = dot_with(inner, slot_cot, ROWS_BY_ROWS)
+    mixed, gains = lax.optimization_barrier((mixed, gains))
+    grad_inputs = to_given(input_rows)
+    layer_out = to_given(exchange(by_source(hidden + mixed.astype(jnp.float32))))
+    layer_out = layer_out.astype(jnp.bfloat16)
+    grad_output = jnp.transpose(grad_output)
     cuts = (width, 2 * width, 2 * width + HEAD)
     return (
         layer_out,

time: 1490 us -> 1320 us (0.89)
  waiting for transfers between devices: 121 us -> 28.3 us
  matrix products: 108 us -> 36.9 us
    pallas_call x1 -> x0, Pallas kernels: 131 us -> none  [expert_pass(): pl.pallas_call(expert_kernel, grid_spec=pltpu.PrefetchScalarGridSpec(num_...]
    pallas_call x9, Pallas kernels: 881 us -> 997 us  [reach(): pl.pallas_call(kernel, in_specs=[pl.BlockSpec(memory_space=pl.ANY)] * len...]
    reduce_scatter x3 -> x0, waiting for transfers between devices: 88.4 us -> none  [ep_sum(): lax.psum_scatter(rows.astype(jnp.bfloat16), 'ep', scatter_dimension=0, ti...]
    dot_general x12 -> x9, matrix products: 101 us -> 31.3 us  [dot_with(): lax.dot_general(left, right, dims, preferred_element_type=jnp.float32)]
    unnamed x91 -> x113, local copies, waits for them, and re-layouts: 30.7 us -> 30.2 us
  transfers between devices with their start and end apart: 7 -> 3, of which waited for: 4 -> 2; matrix products, arithmetic and copies ran while one was open for 9% -> 5% of each run, Pallas kernels for 54% -> 53%
where the time goes in v3:
time: 1320 us; the launch traced here: 1310 us
  Pallas kernels  1160 us (88%)
  local copies, waits for them, and re-layouts  40.5 us (3%)
  matrix products  36.9 us (3%)
  waiting for transfers between devices  28.3 us (2%)
  other arithmetic  25.7 us (2%)
  between operations  15.2 us (1%)
    pallas_call x9, Pallas kernels, reach(): pl.pallas_call(kernel, in_specs=[pl.BlockSpec(memory_space=pl.ANY)] * len...  997 us
    pallas_call x1, Pallas kernels, attend_backward(): pl.pallas_call(attend_backward_kernel, grid_spec=pltpu.PrefetchScalarGrid...  83.9 us
    pallas_call x1, Pallas kernels, attend_forward(): pl.pallas_call(attend_forward_kernel, grid_spec=pltpu.PrefetchScalarGridS...  56.8 us
    dot_general x9, matrix products, dot_with(): lax.dot_general(left, right, dims, preferred_element_type=jnp.float32)  31.3 us
    unnamed x113, local copies, waits for them, and re-layouts  30.2 us
  transfers between devices with their start and end apart: 3, of which 2 were waited for; matrix products, arithmetic and copies ran while one was open for 5% of the time, Pallas kernels for 53%

profile of v3, /device:TPU:0, one launch (start us, length us, event | category | flops | bytes accessed | tf_op | source)
XLA Modules:
  0.0 1306.4 jit_solution(15209443423546768959)
XLA Ops:
  9.4 51.1 %enter_kernel.1 = (bf16[8,4,32,2048]{3,2,1,0:T(8,128)(2,1)S(1)}, bf16[8,32,2048]{2,1,0:T(8,128)(2,1)}) custom-call(bf16[8,32,2048]{2,1,0:T(8,128)(2,1)S(1)} %bitcast.135, bf16[8,32,2048]{2,1,0:T(8,128)(2,1)S(1)} %bitcast.136), custom_call_target="tpu_custom_call" | custom-call | flops 1 | bytes 1 | tf_op jit(solution)/shard_map/enter_kernel/pallas_call | solution.py:549
  65.7 11.2 front.1
  81.7 90.6 %gather_kv_kernel.1 = bf16[32,8,32,256]{3,2,1,0:T(8,128)(2,1)S(1)} custom-call(bf16[32,32,256]{2,1,0:T(8,128)(2,1)S(1)} %bitcast.139), custom_call_target="tpu_custom_call" | custom-call | flops 1 | bytes 1 | tf_op jit(solution)/shard_map/gather_kv_kernel/pallas_call | solution.py:549
  175.5 56.8 %attend_forward.1 = (f32[1024,1024]{1,0:T(8,128)}, bf16[1024,1024]{1,0:T(8,128)(2,1)S(1)}, f32[32,1,256]{2,1,0:T(1,128)S(1)}) custom-call(s32[4,32]{1,0:T(4,128)S(1)} %pad_add_fusion.2.bounds_ref, bf16[1024,1024]{1,0:T(8,128)(2,1)S(1)} %get-tuple-element.49.q_ref, s32[1024,2]{1,0:T(8,128)S(1)} %copy.74.ask_ref, ...), custom_call_target="tpu_custom_call" | custom-call | flops 12884901888 | bytes 16777216 | tf_op jit(solution)/shard_map/attend_forward/pallas_call | solution.py:207
  232.4 4.7 convolution_convert_fusion.2
  237.1 42.2 %scatter_group_kernel.2 = f32[8,32,2048]{2,1,0:T(8,128)S(1)} custom-call(bf16[8,4,32,2048]{3,2,1,0:T(8,128)(2,1)S(1)} %bitcast.133), custom_call_target="tpu_custom_call" | custom-call | flops 1 | bytes 1 | tf_op jit(solution)/shard_map/scatter_group_kernel/pallas_call | solution.py:549
  285.4 16.8 %all-gather.2.cloned.1.call-done.c_ref = bf16[8192,2048]{1,0:T(8,128)(2,1)} async-done(((bf16[256,2048]{1,0:T(8,128)(2,1)}), bf16[8192,2048]{1,0:T(8,128)(2,1)}) %all-gather.2.cloned.1.call-update) | async-done | bytes 33554448 | tf_op jit(solution)/shard_map/all_gather | solution.py:1446
  302.1 223.8 %expert_all_kernel.1 = (bf16[8192,2048]{1,0:T(8,128)(2,1)}, bf16[8192,2048]{1,0:T(8,128)(2,1)}, bf16[8192,2048]{1,0:T(8,128)(2,1)}, bf16[4096,2048]{1,0:T(8,128)...) custom-call(bf16[256,2048]{1,0:T(8,128)(2,1)} %get-tuple-element.169, ...), custom_call_target="tpu_custom_call" | custom-call | flops 1 | bytes 1 | tf_op jit(solution)/shard_map/expert_all_kernel/pallas_call | solution.py:549
  525.9 183.9 %scatter_all_kernel.1 = f32[256,2048]{1,0:T(8,128)} custom-call(bf16[8192,2048]{1,0:T(8,128)(2,1)} %get-tuple-element.53.p_ref), custom_call_target="tpu_custom_call" | custom-call | flops 1 | bytes 1 | tf_op jit(solution)/shard_map/scatter_all_kernel/pallas_call | solution.py:549
  709.8 5.8 broadcast_in_dim_reshape.10.key_given_ref
  722.7 53.5 %gather_group_kernel.1 = bf16[8,4,32,2048]{3,2,1,0:T(8,128)(2,1)S(1)} custom-call(bf16[8,32,2048]{2,1,0:T(8,128)(2,1)S(1)} %bitcast.134), custom_call_target="tpu_custom_call" | custom-call | flops 1 | bytes 1 | tf_op jit(solution)/shard_map/gather_group_kernel/pallas_call | solution.py:549
  776.2 5.8 convolution_convert_fusion.7.grad_ref
  782.0 83.9 %attend_backward.1 = (f32[1024,1024]{1,0:T(8,128)}, bf16[8192,256]{1,0:T(8,128)(2,1)}) custom-call(s32[4,32]{1,0:T(4,128)} %copy-done.21, bf16[1024,1024]{1,0:T(8,128)(2,1)} %copy-done.28, bf16[1024,1024]{1,0:T(8,128)(2,1)} %convolution_convert_fusion.7.grad_ref, f32[1024,1024]{1,0:T(8,128)} %get-tuple-element.59.exact_ref, f32[32,1,256]{2,1,0:T(1,128)} %copy-done.31, ...), custom_call_target="tpu_custom_call" | custom-call | flops 32212254720 | bytes 33554432 | tf_op jit(solution)/shard_map/attend_backward/pallas_call | solution.py:308
  868.1 95.9 %scatter_kv_kernel.1 = bf16[32,32,256]{2,1,0:T(8,128)(2,1)S(1)} custom-call(bf16[32,8,32,256]{3,2,1,0:T(8,128)(2,1)S(1)} %bitcast.132), custom_call_target="tpu_custom_call" | custom-call | flops 1 | bytes 1 | tf_op jit(solution)/shard_map/scatter_kv_kernel/pallas_call | solution.py:549
  967.4 6.2 head_back.2
  976.5 4.5 fusion.34
  982.4 58.1 %scatter_group_kernel.3 = f32[8,32,2048]{2,1,0:T(8,128)S(1)} custom-call(bf16[8,4,32,2048]{3,2,1,0:T(8,128)(2,1)S(1)} %bitcast.126), custom_call_target="tpu_custom_call" | custom-call | flops 1 | bytes 1 | tf_op jit(solution)/shard_map/scatter_group_kernel/pallas_call | solution.py:549
  1042.5 5.3 fusion.3
  1051.6 6.5 convolution_convert_fusion.1
  1058.1 6.2 convolution_convert_fusion
  1064.3 197.7 %finish_kernel.1 = (f32[256,1024]{1,0:T(8,128)}, f32[256,1024]{1,0:T(8,128)}, f32[256,256]{1,0:T(8,128)}, f32[34,128]{1,0:T(8,128)}, bf16[8,32,2048]{2,1,0:T(8,1...) custom-call(bf16[8,256,1024]{2,1,0:T(8,128)(2,1)} %bitcast.155, ...), custom_call_target="tpu_custom_call" | custom-call | flops 1 | bytes 1 | tf_op jit(solution)/shard_map/finish_kernel/pallas_call | solution.py:549
  1264.5 3.7 all-to-all-start
  1273.3 11.5 all-to-all-done
  1287.2 6.1 copy.94
  (179 shorter events, 59.4 us)
Async XLA Ops:
  7.2 294.9 %all-gather.2.cloned.1.call-start = ((), (), s32[]{:S(2)}) async-start(), calls=%async_computation.2 | async-start | bytes 34603008 | tf_op jit(solution)/shard_map/all_gather | solution.py:1446
  9.4 53.5 %copy-start.46 = (s32[8]{0:T(128)S(1)}, s32[8]{0:T(128)}, u32[]{:S(2)}) copy-start(s32[8]{0:T(128)} %param.20) | copy-start | bytes 100
  62.6 1199.4 %reduce-scatter.2.cloned.1.call-start = ((), (), s32[]{:S(2)}) async-start(), calls=%async_computation.3 | async-start | bytes 34603008 | tf_op jit(solution)/shard_map/reduce_scatter | solution.py:1494
  65.6 11.3 copy-start.3
  65.6 11.3 copy-start.5
  81.7 93.8 %copy-start.28 = (bf16[1024,1024]{1,0:T(8,128)(2,1)}, bf16[1024,1024]{1,0:T(8,128)(2,1)S(1)}, u32[]{:S(2)}) copy-start(bf16[1024,1024]{1,0:T(8,128)(2,1)S(1)} %get-tuple-element.49.q_ref) | copy-start | bytes 6291460
  175.5 56.9 %copy-start.21 = (s32[4,32]{1,0:T(4,128)}, s32[4,32]{1,0:T(4,128)S(1)}, u32[]{:S(2)}) copy-start(s32[4,32]{1,0:T(4,128)S(1)} %pad_add_fusion.2.bounds_ref) | copy-start | bytes 1540
  175.5 56.9 %copy-start.47 = (bf16[1024,2048]{1,0:T(8,128)(2,1)S(1)}, bf16[1024,2048]{1,0:T(8,128)(2,1)}, u32[]{:S(2)}) copy-start(bf16[1024,2048]{1,0:T(8,128)(2,1)} %param.29) | copy-start | bytes 12582916
  709.8 8.4 copy-start.32
  722.7 53.6 %copy-start.48 = (bf16[1024,2048]{1,0:T(8,128)(2,1)S(1)}, bf16[1024,2048]{1,0:T(8,128)(2,1)}, u32[]{:S(2)}) copy-start(bf16[1024,2048]{1,0:T(8,128)(2,1)} %param.29) | copy-start | bytes 12582916
  776.2 5.8 copy-start.9
  868.1 95.9 %copy-start.4 = (f32[1024,128]{1,0:T(8,128)S(1)}, f32[1024,128]{1,0:T(8,128)}, u32[]{:S(2)}) copy-start(f32[1024,128]{1,0:T(8,128)} %copy-done.3) | copy-start | bytes 1572868
  868.1 95.9 %copy-start.6 = (f32[1024,128]{1,0:T(8,128)S(1)}, f32[1024,128]{1,0:T(8,128)}, u32[]{:S(2)}) copy-start(f32[1024,128]{1,0:T(8,128)} %copy-done.5) | copy-start | bytes 1572868
  868.1 96.0 %copy-start.19 = (f32[1024,128]{1,0:T(8,128)S(1)}, f32[1024,128]{1,0:T(8,128)}, u32[]{:S(2)}) copy-start(f32[1024,128]{1,0:T(8,128)} %copy-done.18) | copy-start | bytes 1572868
  868.1 97.0 %copy-start.8 = (f32[1024,1024]{1,0:T(8,128)S(1)}, f32[1024,1024]{1,0:T(8,128)}, u32[]{:S(2)}) copy-start(f32[1024,1024]{1,0:T(8,128)} %copy-done.7) | copy-start | bytes 12582916
  967.4 6.2 copy-start.15
  1042.5 5.9 copy-start.27
  1051.6 6.5 copy-start.25
  1064.3 197.7 %copy-start.33 = (f32[256,2048]{1,0:T(8,128)S(1)}, f32[256,2048]{1,0:T(8,128)}, u32[]{:S(2)}) copy-start(f32[256,2048]{1,0:T(8,128)} %get-tuple-element.170) | copy-start | bytes 6291460
  1264.5 20.2 %all-to-all-start = ((bf16[8,32,2048]{2,1,0:T(8,128)(2,1)}), bf16[8,32,2048]{2,1,0:T(8,128)(2,1)S(1)}, u32[]{:S(2)}, u32[]{:S(2)}) async-start(bf16[8,32,2048]{2,1,0:T(8,128)(2,1)} %bitcast.158), calls=%async_computation.1 | async-start | bytes 2097152 | tf_op jit(solution)/shard_map/all_to_all | solution.py:1412
  1270.2 16.0 %copy-start.35 = (f32[256,1024]{1,0:T(8,128)S(1)}, f32[256,1024]{1,0:T(8,128)}, u32[]{:S(2)}) copy-start(f32[256,1024]{1,0:T(8,128)} %get-tuple-element.204) | copy-start | bytes 3145732
  1284.7 8.6 slice-start.2
  1287.2 6.1 slice-start.3
  1287.2 8.9 slice-start
  (33 other events, 92.9 us)
Sparse Core Ops, SparseCore 0:
  62.7 239.3 all-gather.1
  709.9 399.2 reduce-scatter.1

commit v4 on v3

--- a/solution.py
+++ b/solution.py
@@ -12,7 +12,7 @@
 EPSILON = 1e-06
 ROPE_BASE = 1000000.0
 KEY_SPAN = 512
-QUERY_TOKENS = 32
+QUERY_TOKENS = 64
 HEAD = 128
 ROW_TILE = 256
 MIB = 1 << 20
@@ -264,7 +264,7 @@
         scores = dot_with(keys, query, COLS_BY_COLS)
         probs = jnp.exp2(scores * (HEAD**-0.5 * LOG2E) - lse)
         if masked:
-            key_given = key_given_ref[place, :]
+            key_given = jnp.broadcast_to(key_given_ref[:, place], (8, KEY_SPAN)).T[:, 0:1]
             probs = jnp.where((key_given <= last) & (key_given >= first), probs, 0.0)
         prob_grad = dot_with(values, grad, COLS_BY_COLS)
         score_grad = (probs * (prob_grad - delta)).astype(jnp.bfloat16)
@@ -300,7 +300,7 @@
             rounded_ref[place] = dkv_ref[place].astype(jnp.bfloat16)
 
 
-def attend_backward(bounds, query, grad, exact, lse, ask_rows, key_column, kv, pairs):
+def attend_backward(bounds, query, grad, exact, lse, ask_rows, key_given, kv, pairs):
     rows, cols = query.shape
     heads = cols // HEAD
     steps = rows // QUERY_TOKENS
@@ -316,7 +316,7 @@
                 rows_of((QUERY_TOKENS, cols)),
                 rows_of((1, 1, stacked)),
                 rows_of((1, 2, stacked)),
-                whole(key_column.shape),
+                whole(key_given.shape),
                 whole(kv.shape),
             ],
             out_specs=[rows_of((QUERY_TOKENS, cols)), whole(kv.shape)],
@@ -332,7 +332,7 @@
         compiler_params=params(56),
         cost_estimate=cost(20 * pairs * HEAD, 32 * MIB, pairs),
         name="attend_backward",
-    )(bounds, query, grad, exact, lse, ask_rows, key_column, kv)
+    )(bounds, query, grad, exact, lse, ask_rows, key_given, kv)
 
 
 def selection(meta, expert, capacity):
@@ -563,9 +563,7 @@
 
 
 NEAR = ((0, 0), (1, 0), (0, 1), (2, 0), (1, 1), (3, 0), (2, 1), (3, 1))
-ORDER = tuple((*where, 0) for where in NEAR[:6])
-ORDER += ((0, 0, 1), (2, 1, 0), (1, 0, 1), (3, 1, 0), (0, 1, 1))
-ORDER += tuple((*where, 1) for where in NEAR[3:])
+ORDER = ((0,0,0),(1,0,0),(0,0,1),(0,1,0),(2,0,0),(1,0,1),(1,1,0),(0,1,1),(3,0,0),(2,1,0),(2,0,1),(1,1,1),(3,1,0),(3,0,1),(2,1,1),(3,1,1))
 
 
 def expert_all_kernel(
@@ -694,7 +692,8 @@
         )]
         for half in (0, 1):
             moves.append((midb.at[parity, half], part(mid_ref, both[half])))
-            moves.append((outb.at[parity, half], part(out_ref, both[half])))
+            slot = both[half]
+            moves.append((outb.at[parity, half], out_ref.at[:, slot % 4, slot // 4]))
         return [
             pltpu.make_async_copy(held, ref, store_sem.at[parity, index])
             for index, (held, ref) in enumerate(moves)
@@ -731,7 +730,8 @@
                 jnp.bfloat16
             )
             scaled = (result[some] * gates[half]).astype(jnp.bfloat16)
-            outb[parity, half] = dot_with(picks[half], scaled, ROWS_BY_ROWS).astype(jnp.bfloat16)
+            mixed = dot_with(picks[half], scaled, ROWS_BY_ROWS).astype(jnp.bfloat16)
+            outb[parity, half] = mixed.reshape(outb.shape[2:])
 
     @pl.loop(0, count + 2)
     def _(turn):
@@ -795,6 +795,8 @@
     hidden = gate_w.shape[2]
     total = blocks * capacity
     shapes = [c_all.shape] * 3 + [(total, width)] * 2 + [(total, hidden)] * 3
+    ep_size = blocks // 4
+    shapes[2] = (ep_size, 4, ep_size, rows // ep_size, width)
     out = [jax.ShapeDtypeStruct(shape, jnp.bfloat16) for shape in shapes]
 
     def buffer(*shape):
@@ -803,7 +805,8 @@
     scratch = [pltpu.VMEM((blocks, *lines.shape), jnp.float32)]
     scratch += [buffer(*gate_w.shape), buffer(*up_w.shape), buffer(*down_w.shape)]
     scratch += [pltpu.VMEM((2, 2, *lines.shape), jnp.float32)]
-    scratch += [buffer(2, 2, rows, width)] * 4 + [buffer(2, 2 * capacity, width)] * 2
+    scratch += [buffer(2, 2, rows, width)] * 3 + [buffer(2, 2, ep_size, rows // ep_size, width)]
+    scratch += [buffer(2, 2 * capacity, width)] * 2
     scratch += [buffer(2, 2 * capacity, hidden)] * 3
     scratch += [(3,), (2,), (8,), (8,), (28,), (28,), (blocks,), (blocks,), (2, 4), (2, 9)]
     operands = (x, lines, c_all, gate_w, up_w, down_w)
@@ -866,8 +869,11 @@
         mine = held.at[step, 0, 0]
         place.arrive(over_first.at[step], first_sem.at[step])
         add(mine, over_first.at[step])
+        if step == 2:
+            place.arrive(over_z.at[3], z_sem.at[3])
+            add(mine, over_z.at[3])
         if step:
-            place.send(mine, over_z.at[step], z_sem.at[step], place.device(step, 0, 0))
+            place.send(mine, over_z.at[step], z_sem.at[step], place.device(1 + (step == 2), 0, 0))
 
     for step in (3, 2, 1, 0):
         mine = held.at[step, 1, 0]
@@ -880,14 +886,14 @@
         if step < 3:
             onward(step + 1)
     onward(0)
-    for step in (3, 2, 1):
+    for step in (2, 1):
         place.arrive(over_z.at[step], z_sem.at[step])
 
     @pl.loop(0, rows, step=32)
     def _(row):
         some = pl.ds(row, 32)
         total = held[0, 0, 0, some].astype(jnp.float32)
-        for step in (1, 2, 3):
+        for step in (1, 2):
             total = total + over_z[step, some].astype(jnp.float32)
         out_ref[some] = total
 
@@ -1111,17 +1117,23 @@
         def _(block, step=step):
             own[step, block] = own[step, block] + over_y[step, block]
 
+        if step == 2:
+            place.arrive(over_z.at[3], z_sem.at[3])
+
+            @pl.loop(0, blocks)
+            def _(block):
+                own[2, block] = own[2, block] + over_z[3, block]
+
         if step:
-            place.send(
-                own.at[step], over_z.at[step], z_sem.at[step], (place.across(step, 0), tp)
-            )
-    for step in (3, 2, 1):
+            device = (place.across(1 + (step == 2), 0), tp)
+            place.send(own.at[step], over_z.at[step], z_sem.at[step], device)
+    for step in (2, 1):
         place.arrive(over_z.at[step], z_sem.at[step])
 
     @pl.loop(0, blocks)
     def _(block):
         total = own[0, block].astype(jnp.float32)
-        for step in (1, 2, 3):
+        for step in (1, 2):
             total = total + over_z[step, block].astype(jnp.float32)
         out_ref[block] = total.astype(jnp.bfloat16)
 
@@ -1179,7 +1191,7 @@
             dst_ref=overs_z[number].at[step],
             send_sem=send_sem.at[number, 3 + step],
             recv_sem=z_sem.at[number, step],
-            device_id=(place.across(step, 0), tp),
+            device_id=(place.across(1 + (step == 2), 0), tp),
             device_id_type=MESH_ID,
         )
 
@@ -1239,6 +1251,14 @@
         def _(row):
             some = pl.ds(row, 64)
             own[step, some] = own[step, some] + over[step, some]
+
+        if step == 2:
+            to_z(number, 3).wait_recv()
+
+            @pl.loop(0, own.shape[1], step=64)
+            def _(row):
+                some = pl.ds(row, 64)
+                own[2, some] = own[2, some] + overs_z[number][3, some]
 
         if step:
             to_z(number, step).start()
@@ -1316,14 +1336,14 @@
 
     for number in range(count):
         own, over, out = owns[number], overs_z[number], outs[number]
-        for step in (3, 2, 1):
+        for step in (2, 1):
             to_z(number, step).wait_recv()
 
         @pl.loop(0, own.shape[1], step=64)
         def _(row, own=own, over=over, out=out):
             some = pl.ds(row, 64)
             sum_of = own[0, some].astype(jnp.float32)
-            for step in (1, 2, 3):
+            for step in (1, 2):
                 sum_of = sum_of + over[step, some].astype(jnp.float32)
             out[some] = sum_of
 
@@ -1411,11 +1431,8 @@
     def exchange(rows):
         return lax.all_to_all(rows, "ep", split_axis=0, concat_axis=0, tiled=True)
 
-    def by_source(rows):
-        return rows.astype(jnp.bfloat16).reshape(ep_size, row_block, width)
-
     def to_given(moved):
-        return dot_with(mover, moved.reshape(own_rows, width), ROWS_BY_ROWS)
+        return dot_with(mover, moved, ROWS_BY_ROWS)
 
     def group_sorted(rows, ident):
         blocks = rows.reshape(ep_size, row_block, width)
@@ -1488,7 +1505,10 @@
     else:
         mid_all = lax.all_gather(normed_mid, everyone, axis=0, tiled=True)
         meta = lax.all_gather(meta_own, everyone, axis=0)
-        results = expert_pass(expert, meta, mid_all, cot_all, *experts)
+        results = list(expert_pass(expert, meta, mid_all, cot_all, *experts))
+        results[1] = jnp.transpose(
+            results[1].reshape(ep_size, tp_size, ep_size, row_block, width), (2, 1, 0, 3, 4)
+        )
     mid_partial, out_partial, expert_in, slot_cot, inner, gate_grad, up_grad = results
     def sum_over_all(partial):
         return lax.psum_scatter(partial, everyone, scatter_dimension=0, tiled=True)
@@ -1498,7 +1518,7 @@
     else:
         mid_grad = sum_over_all(mid_partial).astype(jnp.float32)
     mid_grad, out_partial = lax.optimization_barrier((mid_grad, out_partial))
-    mixed = sum_over_all(out_partial)
+    mixed = sum_over_all(out_partial.reshape(token_total, width))
 
     mid_hat = hidden * mid_scale
     grad_expert_gain = jnp.sum(mid_grad * mid_hat, axis=0)
@@ -1509,7 +1529,7 @@
     branch_grad = group_sorted(hidden_grad.astype(jnp.bfloat16), 6)
     out_grad = dot_with(branch_grad, output_proj, COLS_BY_COLS).astype(jnp.bfloat16)
     query_grad, kv_grad = attend_backward(
-        bounds, query_rows, out_grad, exact, lse, ask_rows, key_given[:, None], kv_all, pairs
+        bounds, query_rows, out_grad, exact, lse, ask_rows, key_given[None], kv_all, pairs
     )
     kv_grad = kv_grad.reshape(expert_count, ep_size, row_block, 2 * HEAD)
     if known:
@@ -1531,10 +1551,11 @@
     in_hat = own_float * in_scale
     grad_input_gain = jnp.sum(normed_grad * in_hat, axis=0)
     in_scaled = normed_grad * input_gain
-    input_rows = by_source(
-        hidden_grad
-        + in_scale * (in_scaled - in_hat * jnp.mean(in_scaled * in_hat, axis=-1, keepdims=True))
-    )
+    input_rows = hidden_grad + in_scale * (
+        in_scaled - in_hat * jnp.mean(in_scaled * in_hat, axis=-1, keepdims=True)
+    )
+    leaving = jnp.concatenate([input_rows, hidden], axis=1).astype(jnp.bfloat16)
+    leaving = leaving.reshape(ep_size, row_block, 2 * width)
 
     weights = [
         dot_with(branch_grad, out_rows, ROWS_BY_ROWS),
@@ -1547,8 +1568,8 @@
     )
     if known:
         experts = (expert_in, slot_cot, inner, gate_grad, up_grad)
-        results = finish(weights, gains.reshape(-1, HEAD), input_rows, *experts, 10)
-        grad_output, grad_query, grad_kv, gains, input_rows = results[:5]
+        results = finish(weights, gains.reshape(-1, HEAD), leaving, *experts, 10)
+        grad_output, grad_query, grad_kv, gains, leaving = results[:5]
         grad_gate, grad_up, grad_down = results[5:]
         gains = gains.reshape(-1)
     else:
@@ -1556,14 +1577,15 @@
             lax.psum_scatter(array, "ep", scatter_dimension=0).astype(jnp.float32)
             for array in weights
         ]
-        gains, input_rows = lax.psum(gains, everyone), exchange(input_rows)
+        gains, leaving = lax.psum(gains, everyone), exchange(leaving)
         grad_gate = dot_with(expert_in, gate_grad, ROWS_BY_ROWS)
         grad_up = dot_with(expert_in, up_grad, ROWS_BY_ROWS)
         grad_down = dot_with(inner, slot_cot, ROWS_BY_ROWS)
     mixed, gains = lax.optimization_barrier((mixed, gains))
-    grad_inputs = to_given(input_rows)
-    layer_out = to_given(exchange(by_source(hidden + mixed.astype(jnp.float32))))
-    layer_out = layer_out.astype(jnp.bfloat16)
+    leaving = leaving.reshape(own_rows, 2 * width)
+    grad_inputs = to_given(leaving[:, :width])
+    layer_out = leaving[:, width:].astype(jnp.float32) + mixed.astype(jnp.float32)
+    layer_out = to_given(layer_out.astype(jnp.bfloat16)).astype(jnp.bfloat16)
     grad_output = jnp.transpose(grad_output)
     cuts = (width, 2 * width, 2 * width + HEAD)
     return (

time: 1320 us -> 1270 us (0.962)
  Pallas kernels: 1160 us -> 1110 us
    all_gather x1, waiting for transfers between devices: 16.8 us -> 40.8 us  [on_device(): cot_all = lax.all_gather(own_cot, everyone, axis=0, tiled=True)]
    pallas_call x1, Pallas kernels: 56.8 us -> 38.6 us  [attend_forward(): pl.pallas_call(attend_forward_kernel, grid_spec=pltpu.PrefetchScalarGridS...]
    pallas_call x9, Pallas kernels: 997 us -> 981 us  [reach(): pl.pallas_call(kernel, in_specs=[pl.BlockSpec(memory_space=pl.ANY)] * len...]
    pallas_call x1, Pallas kernels: 83.9 us -> 67.8 us  [attend_backward(): pl.pallas_call(attend_backward_kernel, grid_spec=pltpu.PrefetchScalarGrid...]
    unnamed x113 -> x111, local copies, waits for them, and re-layouts: 30.2 us -> 31.6 us
  transfers between devices with their start and end apart: 3 -> 2, of which waited for: 2 -> 1; matrix products, arithmetic and copies ran while one was open for 5% -> 5% of each run, Pallas kernels for 53% -> 53%
where the time goes in v4:
time: 1270 us; the launch traced here: 1260 us
  Pallas kernels  1110 us (87%)
  waiting for transfers between devices  40.8 us (3%)
  matrix products  38.5 us (3%)
  local copies, waits for them, and re-layouts  37 us (3%)
  other arithmetic  24.7 us (2%)
  between operations  15.2 us (1%)
    pallas_call x9, Pallas kernels, reach(): pl.pallas_call(kernel, in_specs=[pl.BlockSpec(memory_space=pl.ANY)] * len...  981 us
    pallas_call x1, Pallas kernels, attend_backward(): pl.pallas_call(attend_backward_kernel, grid_spec=pltpu.PrefetchScalarGrid...  67.8 us
    all_gather x1, waiting for transfers between devices, on_device(): cot_all = lax.all_gather(own_cot, everyone, axis=0, tiled=True)  40.8 us
    pallas_call x1, Pallas kernels, attend_forward(): pl.pallas_call(attend_forward_kernel, grid_spec=pltpu.PrefetchScalarGridS...  38.6 us
    dot_general x9, matrix products, dot_with(): lax.dot_general(left, right, dims, preferred_element_type=jnp.float32)  32.9 us
    unnamed x111, local copies, waits for them, and re-layouts  31.6 us
  transfers between devices with their start and end apart: 2, of which 1 were waited for; matrix products, arithmetic and copies ran while one was open for 5% of the time, Pallas kernels for 53%

profile of v4, /device:TPU:0, one launch (start us, length us, event | category | flops | bytes accessed | tf_op | source)
XLA Modules:
  0.0 1261.9 jit_solution(10665283646026394403)
XLA Ops:
  9.4 51.1 %enter_kernel.1 = (bf16[8,4,32,2048]{3,2,1,0:T(8,128)(2,1)S(1)}, bf16[8,32,2048]{2,1,0:T(8,128)(2,1)}) custom-call(bf16[8,32,2048]{2,1,0:T(8,128)(2,1)S(1)} %bitcast.161, bf16[8,32,2048]{2,1,0:T(8,128)(2,1)S(1)} %bitcast.162), custom_call_target="tpu_custom_call" | custom-call | flops 1 | bytes 1 | tf_op jit(solution)/shard_map/enter_kernel/pallas_call | solution.py:549
  65.6 11.2 front.1
  81.7 90.7 %gather_kv_kernel.1 = bf16[32,8,32,256]{3,2,1,0:T(8,128)(2,1)S(1)} custom-call(bf16[32,32,256]{2,1,0:T(8,128)(2,1)S(1)} %bitcast.165), custom_call_target="tpu_custom_call" | custom-call | flops 1 | bytes 1 | tf_op jit(solution)/shard_map/gather_kv_kernel/pallas_call | solution.py:549
  175.7 38.6 %attend_forward.1 = (f32[1024,1024]{1,0:T(8,128)}, bf16[1024,1024]{1,0:T(8,128)(2,1)S(1)}, f32[16,1,512]{2,1,0:T(1,128)S(1)}) custom-call(s32[4,16]{1,0:T(4,128)S(1)} %pad_add_fusion.2.bounds_ref, bf16[1024,1024]{1,0:T(8,128)(2,1)S(1)} %get-tuple-element.50.q_ref, s32[1024,2]{1,0:T(8,128)S(1)} %copy.66.ask_ref, ...), custom_call_target="tpu_custom_call" | custom-call | flops 12884901888 | bytes 16777216 | tf_op jit(solution)/shard_map/attend_forward/pallas_call | solution.py:207
  214.4 4.7 convolution_convert_fusion.2
  219.1 49.9 %scatter_group_kernel.2 = f32[8,32,2048]{2,1,0:T(8,128)S(1)} custom-call(bf16[8,4,32,2048]{3,2,1,0:T(8,128)(2,1)S(1)} %bitcast.159), custom_call_target="tpu_custom_call" | custom-call | flops 1 | bytes 1 | tf_op jit(solution)/shard_map/scatter_group_kernel/pallas_call | solution.py:549
  271.6 3.5 multiply_convert_fusion
  275.8 40.8 %all-gather.2.cloned.1.call-done.c_ref = bf16[8192,2048]{1,0:T(8,128)(2,1)} async-done(((bf16[256,2048]{1,0:T(8,128)(2,1)}), bf16[8192,2048]{1,0:T(8,128)(2,1)}) %all-gather.2.cloned.1.call-update) | async-done | bytes 33554448 | tf_op jit(solution)/shard_map/all_gather | solution.py:1463
  316.6 205.0 %expert_all_kernel.1 = (bf16[8192,2048]{1,0:T(8,128)(2,1)}, bf16[8192,2048]{1,0:T(8,128)(2,1)}, bf16[8,4,8,32,2048]{4,3,2,1,0:T(8,128)(2,1)}, bf16[4096,2048]{1,...) custom-call(bf16[256,2048]{1,0:T(8,128)(2,1)} %get-tuple-element.169, ...), custom_call_target="tpu_custom_call" | custom-call | flops 1 | bytes 1 | tf_op jit(solution)/shard_map/expert_all_kernel/pallas_call | solution.py:549
  521.6 183.6 %scatter_all_kernel.1 = f32[256,2048]{1,0:T(8,128)} custom-call(bf16[8192,2048]{1,0:T(8,128)(2,1)} %get-tuple-element.53.p_ref), custom_call_target="tpu_custom_call" | custom-call | flops 1 | bytes 1 | tf_op jit(solution)/shard_map/scatter_all_kernel/pallas_call | solution.py:549
  712.5 56.1 %gather_group_kernel.1 = bf16[8,4,32,2048]{3,2,1,0:T(8,128)(2,1)S(1)} custom-call(bf16[8,32,2048]{2,1,0:T(8,128)(2,1)S(1)} %bitcast.160), custom_call_target="tpu_custom_call" | custom-call | flops 1 | bytes 1 | tf_op jit(solution)/shard_map/gather_group_kernel/pallas_call | solution.py:549
  768.6 6.0 convolution_convert_fusion.7.grad_ref
  774.6 67.8 %attend_backward.1 = (f32[1024,1024]{1,0:T(8,128)}, bf16[8192,256]{1,0:T(8,128)(2,1)}) custom-call(s32[4,16]{1,0:T(4,128)} %copy-done.22, bf16[1024,1024]{1,0:T(8,128)(2,1)} %copy-done.29, bf16[1024,1024]{1,0:T(8,128)(2,1)} %convolution_convert_fusion.7.grad_ref, f32[1024,1024]{1,0:T(8,128)} %get-tuple-element.58.exact_ref, f32[16,1,512]{2,1,0:T(1,128)} %copy-done.32, ...), custom_call_target="tpu_custom_call" | custom-call | flops 32212254720 | bytes 33554432 | tf_op jit(solution)/shard_map/attend_backward/pallas_call | solution.py:308
  844.7 95.6 %scatter_kv_kernel.1 = bf16[32,32,256]{2,1,0:T(8,128)(2,1)S(1)} custom-call(bf16[32,8,32,256]{3,2,1,0:T(8,128)(2,1)S(1)} %bitcast.158), custom_call_target="tpu_custom_call" | custom-call | flops 1 | bytes 1 | tf_op jit(solution)/shard_map/scatter_kv_kernel/pallas_call | solution.py:549
  943.6 6.2 head_back.2
  952.8 4.5 fusion.37
  958.7 50.5 %scatter_group_kernel.3 = f32[8,32,2048]{2,1,0:T(8,128)S(1)} custom-call(bf16[8,4,32,2048]{3,2,1,0:T(8,128)(2,1)S(1)} %bitcast.152), custom_call_target="tpu_custom_call" | custom-call | flops 1 | bytes 1 | tf_op jit(solution)/shard_map/scatter_group_kernel/pallas_call | solution.py:549
  1011.1 4.1 fusion.3
  1020.6 6.5 convolution_convert_fusion
  1027.0 6.2 convolution_convert_fusion.1
  1033.3 198.2 %finish_kernel.1 = (f32[256,1024]{1,0:T(8,128)}, f32[256,1024]{1,0:T(8,128)}, f32[256,256]{1,0:T(8,128)}, f32[34,128]{1,0:T(8,128)}, bf16[8,32,4096]{2,1,0:T(8,1...) custom-call(bf16[8,256,1024]{2,1,0:T(8,128)(2,1)} %bitcast.182, ...), custom_call_target="tpu_custom_call" | custom-call | flops 1 | bytes 1 | tf_op jit(solution)/shard_map/finish_kernel/pallas_call | solution.py:549
  1238.8 2.9 convolution_convert_fusion.3
  1242.7 6.1 copy.84
  1248.8 2.8 copy.85
  (176 shorter events, 54.1 us)
Async XLA Ops:
  7.2 309.4 %all-gather.2.cloned.1.call-start = ((), (), s32[]{:S(2)}) async-start(), calls=%async_computation.1 | async-start | bytes 34603008 | tf_op jit(solution)/shard_map/all_gather | solution.py:1463
  9.4 53.5 %copy-start.45 = (s32[8]{0:T(128)S(1)}, s32[8]{0:T(128)}, u32[]{:S(2)}) copy-start(s32[8]{0:T(128)} %param.20) | copy-start | bytes 100
  62.6 1175.1 %reduce-scatter.2.cloned.1.call-start = ((), (), s32[]{:S(2)}) async-start(), calls=%async_computation.2 | async-start | bytes 34603008 | tf_op jit(solution)/shard_map/reduce_scatter | solution.py:1514
  65.6 11.3 copy-start.3
  65.6 11.3 copy-start.5
  81.7 94.0 %copy-start.29 = (bf16[1024,1024]{1,0:T(8,128)(2,1)}, bf16[1024,1024]{1,0:T(8,128)(2,1)S(1)}, u32[]{:S(2)}) copy-start(bf16[1024,1024]{1,0:T(8,128)(2,1)S(1)} %get-tuple-element.50.q_ref) | copy-start | bytes 6291460
  175.3 39.1 %copy-start.20 = (s32[1,8192]{1,0:T(1,128)}, s32[1,8192]{1,0:T(1,128)S(1)}, u32[]{:S(2)}) copy-start(s32[1,8192]{1,0:T(1,128)S(1)} %broadcast_in_dim_reshape.2.key_given_ref) | copy-start | bytes 98308
  175.7 38.7 %copy-start.22 = (s32[4,16]{1,0:T(4,128)}, s32[4,16]{1,0:T(4,128)S(1)}, u32[]{:S(2)}) copy-start(s32[4,16]{1,0:T(4,128)S(1)} %pad_add_fusion.2.bounds_ref) | copy-start | bytes 772
  175.7 38.7 %copy-start.46 = (bf16[1024,2048]{1,0:T(8,128)(2,1)S(1)}, bf16[1024,2048]{1,0:T(8,128)(2,1)}, u32[]{:S(2)}) copy-start(bf16[1024,2048]{1,0:T(8,128)(2,1)} %param.29) | copy-start | bytes 12582916
  214.4 4.7 copy-start.30
  214.4 4.7 copy-start.32
  712.4 56.2 %copy-start.47 = (bf16[1024,2048]{1,0:T(8,128)(2,1)S(1)}, bf16[1024,2048]{1,0:T(8,128)(2,1)}, u32[]{:S(2)}) copy-start(bf16[1024,2048]{1,0:T(8,128)(2,1)} %param.29) | copy-start | bytes 12582916
  768.6 6.0 copy-start.9
  844.6 95.6 %copy-start.4 = (f32[1024,128]{1,0:T(8,128)S(1)}, f32[1024,128]{1,0:T(8,128)}, u32[]{:S(2)}) copy-start(f32[1024,128]{1,0:T(8,128)} %copy-done.3) | copy-start | bytes 1572868
  844.6 95.6 %copy-start.6 = (f32[1024,128]{1,0:T(8,128)S(1)}, f32[1024,128]{1,0:T(8,128)}, u32[]{:S(2)}) copy-start(f32[1024,128]{1,0:T(8,128)} %copy-done.5) | copy-start | bytes 1572868
  844.6 95.6 %copy-start.19 = (f32[1024,128]{1,0:T(8,128)S(1)}, f32[1024,128]{1,0:T(8,128)}, u32[]{:S(2)}) copy-start(f32[1024,128]{1,0:T(8,128)} %copy-done.18) | copy-start | bytes 1572868
  844.6 96.7 %copy-start.8 = (f32[1024,1024]{1,0:T(8,128)S(1)}, f32[1024,1024]{1,0:T(8,128)}, u32[]{:S(2)}) copy-start(f32[1024,1024]{1,0:T(8,128)} %copy-done.7) | copy-start | bytes 12582916
  943.6 6.2 copy-start.15
  1011.1 4.7 copy-start.28
  1020.6 6.5 copy-start.10
  1020.6 6.5 copy-start.31
  1238.8 9.9 slice-start.2
  1242.7 6.1 slice-start.3
  1242.7 8.9 slice-start
  (31 other events, 79.5 us)
Sparse Core Ops, SparseCore 0:
  62.7 253.8 all-gather.1
  705.3 401.4 reduce-scatter.1

commit v5 on v4

--- a/solution.py
+++ b/solution.py
@@ -673,7 +673,9 @@
     def load_copies(slot, parity, half):
         return (
             pltpu.make_async_copy(part(all_ref, slot), xb.at[parity, half], load_sem.at[parity, half]),
-            pltpu.make_async_copy(part(c_ref, slot), cb.at[parity, half], load_sem.at[parity, 2 + half]),
+            pltpu.make_async_copy(
+                c_ref.at[:, slot % 4, slot // 4], cb.at[parity, half], load_sem.at[parity, 2 + half]
+            ),
         )
 
     def load(number):
@@ -707,7 +709,8 @@
             gates.append(gate)
             some = slice(half * capacity, (half + 1) * capacity)
             xsb[parity, some] = dot(pick, xb[parity, half]).astype(jnp.bfloat16)
-            csb[parity, some] = (dot(pick, cb[parity, half]) * gate).astype(jnp.bfloat16)
+            cot = cb[parity, half].reshape(rows, -1)
+            csb[parity, some] = (dot(pick, cot) * gate).astype(jnp.bfloat16)
         expert_in, slot_cot = xsb[parity], csb[parity]
         gate_part = dot(expert_in, wg[0])
         up_part = dot(expert_in, wu[0])
@@ -791,12 +794,12 @@
 
 def expert_all(x, lines, c_all, gate_w, up_w, down_w, capacity, ident):
     rows, width = x.shape
-    blocks = c_all.shape[0] // rows
+    ep_size, tp_size = c_all.shape[:2]
+    blocks = ep_size * tp_size
     hidden = gate_w.shape[2]
     total = blocks * capacity
-    shapes = [c_all.shape] * 3 + [(total, width)] * 2 + [(total, hidden)] * 3
-    ep_size = blocks // 4
-    shapes[2] = (ep_size, 4, ep_size, rows // ep_size, width)
+    shapes = [(blocks * rows, width)] * 2 + [c_all.shape]
+    shapes += [(total, width)] * 2 + [(total, hidden)] * 3
     out = [jax.ShapeDtypeStruct(shape, jnp.bfloat16) for shape in shapes]
 
     def buffer(*shape):
@@ -805,7 +808,8 @@
     scratch = [pltpu.VMEM((blocks, *lines.shape), jnp.float32)]
     scratch += [buffer(*gate_w.shape), buffer(*up_w.shape), buffer(*down_w.shape)]
     scratch += [pltpu.VMEM((2, 2, *lines.shape), jnp.float32)]
-    scratch += [buffer(2, 2, rows, width)] * 3 + [buffer(2, 2, ep_size, rows // ep_size, width)]
+    by_source = buffer(2, 2, ep_size, rows // ep_size, width)
+    scratch += [buffer(2, 2, rows, width), by_source, buffer(2, 2, rows, width), by_source]
     scratch += [buffer(2, 2 * capacity, width)] * 2
     scratch += [buffer(2, 2 * capacity, hidden)] * 3
     scratch += [(3,), (2,), (8,), (8,), (28,), (28,), (blocks,), (blocks,), (2, 4), (2, 9)]
@@ -912,16 +916,12 @@
     return reach(scatter_all_kernel, out, scratch, ident, p, vmem_out=True, mib=56)
 
 
-def enter_kernel(x_ref, c_ref, group_ref, cot_ref, own_sem, send_sem, x_sem, cot_sem):
+def enter_kernel(x_ref, group_ref, own_sem, send_sem, x_sem):
     place = Place(send_sem)
     ep, tp = place.ep, place.tp
     others = [place.across(step, over) for step in range(4) for over in (0, 1)]
-    own = [
-        pltpu.make_async_copy(x_ref.at[ep], group_ref.at[ep, tp], own_sem.at[0]),
-        pltpu.make_async_copy(c_ref.at[ep], cot_ref.at[ep], own_sem.at[1]),
-    ]
-    for copy in own:
-        copy.start()
+    own = pltpu.make_async_copy(x_ref.at[ep], group_ref.at[ep, tp], own_sem)
+    own.start()
     place.greet(
         [(other, tp) for other in others[1:]] + [(ep, place.over_x), (ep, place.over_core)]
     )
@@ -934,8 +934,6 @@
         source = block if number else x_ref.at[ep]
         place.send(source, block, x_sem.at[other, tp], (ep, place.over_x))
         place.send(source, block, x_sem.at[other, tp], (ep, place.over_core))
-    for other in others[1:]:
-        place.send(c_ref.at[other], cot_ref.at[ep], cot_sem.at[ep], (other, tp))
     for other in others:
         block = group_ref.at[other, place.over_x]
         place.arrive(block, x_sem.at[other, place.over_x])
@@ -943,22 +941,16 @@
     for other in others:
         for source in (place.over_core, place.over_both):
             place.arrive(group_ref.at[other, source], x_sem.at[other, source])
-    for other in others[1:]:
-        place.arrive(cot_ref.at[other], cot_sem.at[other])
-    for copy in own:
-        copy.wait()
+    own.wait()
     place.finish()
 
 
-def enter(x, c, tp_size, ident):
+def enter(x, tp_size, ident):
     ep_size, block, width = x.shape
-    moves = (ep_size - 1) * 2 + ep_size * 3
-    out = [
-        jax.ShapeDtypeStruct((ep_size, tp_size, block, width), x.dtype),
-        jax.ShapeDtypeStruct((ep_size, block, width), x.dtype),
-    ]
-    scratch = [(2,), (moves,), (ep_size, tp_size), (ep_size,)]
-    return reach(enter_kernel, out, scratch, ident, x, c)
+    moves = ep_size - 1 + ep_size * 3
+    out = jax.ShapeDtypeStruct((ep_size, tp_size, block, width), x.dtype)
+    scratch = [pltpu.SemaphoreType.DMA, (moves,), (ep_size, tp_size)]
+    return reach(enter_kernel, out, scratch, ident, x)
 
 
 CHUNKS = 4
@@ -1452,15 +1444,19 @@
 
     leaving_x, leaving_cot = to_places(inputs), to_places(cotangent)
     if known:
-        group_x, own_cot = enter(leaving_x, leaving_cot, tp_size, 1)
+        cot_all = lax.all_gather(leaving_cot, everyone, axis=0, tiled=True)
+        cot_all = cot_all.reshape(ep_size, tp_size, ep_size, row_block, width)
+        own_cot = lax.dynamic_index_in_dim(cot_all, tp_index, 1, keepdims=False)
+        own_cot = lax.dynamic_index_in_dim(own_cot, ep_index, 1, keepdims=False)
+        group_x = enter(leaving_x, tp_size, 1)
         own_inputs = lax.dynamic_index_in_dim(group_x, tp_index, 1, keepdims=False)
     else:
         own_inputs, own_cot = exchange(leaving_x), exchange(leaving_cot)
         group_x = lax.all_gather(own_inputs, "tp", axis=1)
+        cot_all = lax.all_gather(own_cot.reshape(own_rows, width), everyone, axis=0, tiled=True)
     own_inputs, own_cot = own_inputs.reshape(own_rows, width), own_cot.reshape(own_rows, width)
     group_x = group_x.reshape(group_rows, width)
     meta_own = jnp.concatenate([routes.astype(jnp.float32).T, gate_values.T], axis=0)
-    cot_all = lax.all_gather(own_cot, everyone, axis=0, tiled=True)
 
     query_given = lax.dynamic_index_in_dim(table, ep_index, 0, keepdims=False)
     query_given = jnp.swapaxes(query_given, 0, 1).reshape(group_rows)

time: 1270 us -> 1230 us (0.969)
  Pallas kernels: 1110 us -> 1080 us
  waiting for transfers between devices: 40.8 us -> 15.6 us
    pallas_call x9, Pallas kernels: 981 us -> 955 us  [reach(): pl.pallas_call(kernel, in_specs=[pl.BlockSpec(memory_space=pl.ANY)] * len...]
    all_gather x1, waiting for transfers between devices: 40.8 us -> 15.6 us  [on_device(): cot_all = lax.all_gather(leaving_cot, everyone, axis=0, tiled=True)]
    unnamed x111 -> x119, local copies, waits for them, and re-layouts: 31.6 us -> 32.3 us
  transfers between devices with their start and end apart: 2 -> 2, of which waited for: 1 -> 1; matrix products, arithmetic and copies ran while one was open for 5% -> 5% of each run, Pallas kernels for 53% -> 57%
where the time goes in v5:
time: 1230 us; the launch traced here: 1220 us
  Pallas kernels  1080 us (88%)
  matrix products  41.9 us (3%)
  local copies, waits for them, and re-layouts  39.2 us (3%)
  other arithmetic  21.9 us (2%)
  waiting for transfers between devices  15.6 us (1%)
  between operations  15.3 us (1%)
    pallas_call x9, Pallas kernels, reach(): pl.pallas_call(kernel, in_specs=[pl.BlockSpec(memory_space=pl.ANY)] * len...  955 us
    pallas_call x1, Pallas kernels, attend_backward(): pl.pallas_call(attend_backward_kernel, grid_spec=pltpu.PrefetchScalarGrid...  68.7 us
    pallas_call x1, Pallas kernels, attend_forward(): pl.pallas_call(attend_forward_kernel, grid_spec=pltpu.PrefetchScalarGridS...  39 us
    dot_general x9, matrix products, dot_with(): lax.dot_general(left, right, dims, preferred_element_type=jnp.float32)  35.2 us
    unnamed x119, local copies, waits for them, and re-layouts  32.3 us
  transfers between devices with their start and end apart: 2, of which 1 were waited for; matrix products, arithmetic and copies ran while one was open for 5% of the time, Pallas kernels for 57%

profile of v5, /device:TPU:0, one launch (start us, length us, event | category | flops | bytes accessed | tf_op | source)
XLA Modules:
  0.0 1215.1 jit_solution(6080490996125742016)
XLA Ops:
  10.5 41.4 %enter_kernel.1 = bf16[8,4,32,2048]{3,2,1,0:T(8,128)(2,1)S(1)} custom-call(bf16[8,32,2048]{2,1,0:T(8,128)(2,1)S(1)} %bitcast.171), custom_call_target="tpu_custom_call" | custom-call | flops 1 | bytes 1 | tf_op jit(solution)/shard_map/enter_kernel/pallas_call | solution.py:549
  56.9 11.2 front.1
  73.0 100.2 %gather_kv_kernel.1 = bf16[32,8,32,256]{3,2,1,0:T(8,128)(2,1)S(1)} custom-call(bf16[32,32,256]{2,1,0:T(8,128)(2,1)S(1)} %bitcast.175), custom_call_target="tpu_custom_call" | custom-call | flops 1 | bytes 1 | tf_op jit(solution)/shard_map/gather_kv_kernel/pallas_call | solution.py:549
  176.5 39.0 %attend_forward.1 = (f32[1024,1024]{1,0:T(8,128)}, bf16[1024,1024]{1,0:T(8,128)(2,1)S(1)}, f32[16,1,512]{2,1,0:T(1,128)S(1)}) custom-call(s32[4,16]{1,0:T(4,128)S(1)} %pad_add_fusion.2.bounds_ref, bf16[1024,1024]{1,0:T(8,128)(2,1)S(1)} %get-tuple-element.46.q_ref, s32[1024,2]{1,0:T(8,128)S(1)} %copy.66.ask_ref, ...), custom_call_target="tpu_custom_call" | custom-call | flops 12884901888 | bytes 16777216 | tf_op jit(solution)/shard_map/attend_forward/pallas_call | solution.py:207
  215.5 4.7 convolution_convert_fusion.2
  220.2 25.7 %scatter_group_kernel.2 = f32[8,32,2048]{2,1,0:T(8,128)S(1)} custom-call(bf16[8,4,32,2048]{3,2,1,0:T(8,128)(2,1)S(1)} %bitcast.170), custom_call_target="tpu_custom_call" | custom-call | flops 1 | bytes 1 | tf_op jit(solution)/shard_map/scatter_group_kernel/pallas_call | solution.py:549
  249.2 3.5 multiply_convert_fusion
  252.8 15.6 %all-gather.2.cloned.1.call-done = bf16[256,32,2048]{2,1,0:T(8,128)(2,1)} async-done(((bf16[8,32,2048]{2,1,0:T(8,128)(2,1)}), bf16[256,32,2048]{2,1,0:T(8,128)(2,1)}) %all-gather.2.cloned.1.call-update) | async-done | bytes 33554448 | tf_op jit(solution)/shard_map/all_gather | solution.py:1447
  268.3 205.2 %expert_all_kernel.1 = (bf16[8192,2048]{1,0:T(8,128)(2,1)}, bf16[8192,2048]{1,0:T(8,128)(2,1)}, bf16[8,4,8,32,2048]{4,3,2,1,0:T(8,128)(2,1)}, bf16[4096,2048]{1,...) custom-call(bf16[256,2048]{1,0:T(8,128)(2,1)} %get-tuple-element.165, ...), custom_call_target="tpu_custom_call" | custom-call | flops 1 | bytes 1 | tf_op jit(solution)/shard_map/expert_all_kernel/pallas_call | solution.py:549
  473.5 185.7 %scatter_all_kernel.1 = f32[256,2048]{1,0:T(8,128)} custom-call(bf16[8192,2048]{1,0:T(8,128)(2,1)} %get-tuple-element.49.p_ref), custom_call_target="tpu_custom_call" | custom-call | flops 1 | bytes 1 | tf_op jit(solution)/shard_map/scatter_all_kernel/pallas_call | solution.py:549
  667.1 54.5 %gather_group_kernel.1 = bf16[8,4,32,2048]{3,2,1,0:T(8,128)(2,1)S(1)} custom-call(bf16[8,32,2048]{2,1,0:T(8,128)(2,1)S(1)} %bitcast.172), custom_call_target="tpu_custom_call" | custom-call | flops 1 | bytes 1 | tf_op jit(solution)/shard_map/gather_group_kernel/pallas_call | solution.py:549
  721.6 6.0 convolution_convert_fusion.7.grad_ref
  727.6 68.7 %attend_backward.1 = (f32[1024,1024]{1,0:T(8,128)}, bf16[8192,256]{1,0:T(8,128)(2,1)}) custom-call(s32[4,16]{1,0:T(4,128)} %copy-done.22, bf16[1024,1024]{1,0:T(8,128)(2,1)} %copy-done.29, bf16[1024,1024]{1,0:T(8,128)(2,1)} %convolution_convert_fusion.7.grad_ref, f32[1024,1024]{1,0:T(8,128)} %get-tuple-element.54.exact_ref, f32[16,1,512]{2,1,0:T(1,128)} %copy-done.32, ...), custom_call_target="tpu_custom_call" | custom-call | flops 32212254720 | bytes 33554432 | tf_op jit(solution)/shard_map/attend_backward/pallas_call | solution.py:308
  798.6 95.2 %scatter_kv_kernel.1 = bf16[32,32,256]{2,1,0:T(8,128)(2,1)S(1)} custom-call(bf16[32,8,32,256]{3,2,1,0:T(8,128)(2,1)S(1)} %bitcast.169), custom_call_target="tpu_custom_call" | custom-call | flops 1 | bytes 1 | tf_op jit(solution)/shard_map/scatter_kv_kernel/pallas_call | solution.py:549
  897.2 6.2 head_back.2
  906.4 4.5 fusion.37
  912.2 50.5 %scatter_group_kernel.3 = f32[8,32,2048]{2,1,0:T(8,128)S(1)} custom-call(bf16[8,4,32,2048]{3,2,1,0:T(8,128)(2,1)S(1)} %bitcast.164), custom_call_target="tpu_custom_call" | custom-call | flops 1 | bytes 1 | tf_op jit(solution)/shard_map/scatter_group_kernel/pallas_call | solution.py:549
  965.3 4.7 convolution_convert_fusion.4
  970.0 2.9 fusion.3
  975.3 6.5 convolution_convert_fusion
  981.7 6.2 convolution_convert_fusion.1
  988.0 196.7 %finish_kernel.1 = (f32[256,1024]{1,0:T(8,128)}, f32[256,1024]{1,0:T(8,128)}, f32[256,256]{1,0:T(8,128)}, f32[34,128]{1,0:T(8,128)}, bf16[8,32,4096]{2,1,0:T(8,1...) custom-call(bf16[8,256,1024]{2,1,0:T(8,128)(2,1)} %bitcast.194, ...), custom_call_target="tpu_custom_call" | custom-call | flops 1 | bytes 1 | tf_op jit(solution)/shard_map/finish_kernel/pallas_call | solution.py:549
  1192.1 2.9 convolution_convert_fusion.3
  1195.9 6.1 copy.75
  (185 shorter events, 56.1 us)
Async XLA Ops:
  7.2 261.1 %all-gather.2.cloned.1.call-start = ((), (), s32[]{:S(2)}) async-start(), calls=%async_computation.1 | async-start | bytes 34603008 | tf_op jit(solution)/shard_map/all_gather | solution.py:1447
  9.9 1181.0 %reduce-scatter.2.cloned.1.call-start = ((), (), s32[]{:S(2)}) async-start(), calls=%async_computation.2 | async-start | bytes 34603008 | tf_op jit(solution)/shard_map/reduce_scatter | solution.py:1510
  10.5 43.8 %copy-start.49 = (s32[8]{0:T(128)S(1)}, s32[8]{0:T(128)}, u32[]{:S(2)}) copy-start(s32[8]{0:T(128)} %param.20) | copy-start | bytes 100
  56.8 11.3 copy-start.3
  56.8 11.3 copy-start.5
  73.0 103.5 %copy-start.29 = (bf16[1024,1024]{1,0:T(8,128)(2,1)}, bf16[1024,1024]{1,0:T(8,128)(2,1)S(1)}, u32[]{:S(2)}) copy-start(bf16[1024,1024]{1,0:T(8,128)(2,1)S(1)} %get-tuple-element.46.q_ref) | copy-start | bytes 6291460
  176.1 39.4 %copy-start.20 = (s32[1,8192]{1,0:T(1,128)}, s32[1,8192]{1,0:T(1,128)S(1)}, u32[]{:S(2)}) copy-start(s32[1,8192]{1,0:T(1,128)S(1)} %broadcast_in_dim_reshape.2.key_given_ref) | copy-start | bytes 98308
  176.5 39.0 %copy-start.22 = (s32[4,16]{1,0:T(4,128)}, s32[4,16]{1,0:T(4,128)S(1)}, u32[]{:S(2)}) copy-start(s32[4,16]{1,0:T(4,128)S(1)} %pad_add_fusion.2.bounds_ref) | copy-start | bytes 772
  176.5 39.0 %copy-start.50 = (bf16[1024,2048]{1,0:T(8,128)(2,1)S(1)}, bf16[1024,2048]{1,0:T(8,128)(2,1)}, u32[]{:S(2)}) copy-start(bf16[1024,2048]{1,0:T(8,128)(2,1)} %param.29) | copy-start | bytes 12582916
  215.5 4.7 copy-start.30
  215.5 4.7 copy-start.32
  667.1 54.6 %copy-start.51 = (bf16[1024,2048]{1,0:T(8,128)(2,1)S(1)}, bf16[1024,2048]{1,0:T(8,128)(2,1)}, u32[]{:S(2)}) copy-start(bf16[1024,2048]{1,0:T(8,128)(2,1)} %param.29) | copy-start | bytes 12582916
  721.6 6.0 copy-start.9
  798.6 95.3 %copy-start.4 = (f32[1024,128]{1,0:T(8,128)S(1)}, f32[1024,128]{1,0:T(8,128)}, u32[]{:S(2)}) copy-start(f32[1024,128]{1,0:T(8,128)} %copy-done.3) | copy-start | bytes 1572868
  798.6 95.3 %copy-start.6 = (f32[1024,128]{1,0:T(8,128)S(1)}, f32[1024,128]{1,0:T(8,128)}, u32[]{:S(2)}) copy-start(f32[1024,128]{1,0:T(8,128)} %copy-done.5) | copy-start | bytes 1572868
  798.6 95.3 %copy-start.19 = (f32[1024,128]{1,0:T(8,128)S(1)}, f32[1024,128]{1,0:T(8,128)}, u32[]{:S(2)}) copy-start(f32[1024,128]{1,0:T(8,128)} %copy-done.18) | copy-start | bytes 1572868
  798.6 96.3 %copy-start.8 = (f32[1024,1024]{1,0:T(8,128)S(1)}, f32[1024,1024]{1,0:T(8,128)}, u32[]{:S(2)}) copy-start(f32[1024,1024]{1,0:T(8,128)} %copy-done.7) | copy-start | bytes 12582916
  897.2 6.2 copy-start.15
  965.3 4.7 copy-start.38
  975.3 6.5 copy-start.10
  975.3 6.5 copy-start.31
  1192.1 9.9 slice-start.2
  1195.9 6.1 slice-start.3
  1195.9 8.9 slice-start
  (35 other events, 95.4 us)
Sparse Core Ops, SparseCore 0:
  11.5 256.8 all-gather.1
  659.3 400.9 reduce-scatter.1

commit v6 on v5

--- a/solution.py
+++ b/solution.py
@@ -818,6 +818,7 @@
 
 
 BUFFERS = 4
+LEAD = 2
 
 
 def scatter_all_kernel(
@@ -836,7 +837,12 @@
     def part(slot):
         return p_ref.at[pl.ds(slot * rows, rows)]
 
-    order = [(step, first, second) for second in (1, 0) for step in (3, 2, 1, 0) for first in (1, 0)]
+    pairs = [(step, first) for step in (3, 2, 1, 0) for first in (1, 0)]
+    order = [(*pairs[number], 1) for number in range(LEAD)]
+    for number, where in enumerate(pairs):
+        if number + LEAD < len(pairs):
+            order.append((*pairs[number + LEAD], 1))
+        order.append((*where, 0))
     loads = []
 
     def load(number):
@@ -850,24 +856,10 @@
     for number in range(BUFFERS):
         load(number)
     place.greet_all_ways()
-    for step, first, second in order:
+    for where in order:
         place.send(
-            part(place.slot(step, first, second, 1)),
-            held.at[step, first, second],
-            core_sem.at[step, first, second],
-            place.device(0, 0, 0, 1),
+            part(place.slot(*where, 1)), held.at[where], core_sem.at[where], place.device(0, 0, 0, 1)
         )
-    for number, (step, first, second) in enumerate(order):
-        mine = held.at[step, first, second]
-        place.arrive(mine, core_sem.at[step, first, second])
-        loads[number].wait()
-        add(mine, own.at[number % BUFFERS])
-        if number + BUFFERS < len(order):
-            load(number + BUFFERS)
-        if second:
-            place.send(
-                mine, over_second.at[step, first], second_sem.at[step, first], place.device(0, 0, 1)
-            )
 
     def onward(step):
         mine = held.at[step, 0, 0]
@@ -879,17 +871,25 @@
         if step:
             place.send(mine, over_z.at[step], z_sem.at[step], place.device(1 + (step == 2), 0, 0))
 
-    for step in (3, 2, 1, 0):
-        mine = held.at[step, 1, 0]
-        place.arrive(over_second.at[step, 1], second_sem.at[step, 1])
-        add(mine, over_second.at[step, 1])
-        place.send(mine, over_first.at[step], first_sem.at[step], place.device(0, 1, 0))
-        mine = held.at[step, 0, 0]
-        place.arrive(over_second.at[step, 0], second_sem.at[step, 0])
-        add(mine, over_second.at[step, 0])
-        if step < 3:
-            onward(step + 1)
-    onward(0)
+    for number, where in enumerate(order):
+        step, first, second = where
+        mine = held.at[where]
+        place.arrive(mine, core_sem.at[where])
+        loads[number].wait()
+        add(mine, own.at[number % BUFFERS])
+        if number + BUFFERS < len(order):
+            load(number + BUFFERS)
+        if second:
+            place.send(
+                mine, over_second.at[step, first], second_sem.at[step, first], place.device(0, 0, 1)
+            )
+            continue
+        place.arrive(over_second.at[step, first], second_sem.at[step, first])
+        add(mine, over_second.at[step, first])
+        if first:
+            place.send(mine, over_first.at[step], first_sem.at[step], place.device(0, 1, 0))
+        else:
+            onward(step)
     for step in (2, 1):
         place.arrive(over_z.at[step], z_sem.at[step])
 

time: 1230 us -> 1200 us (0.976)
  Pallas kernels: 1080 us -> 1050 us
    pallas_call x9, Pallas kernels: 955 us -> 929 us  [reach(): pl.pallas_call(kernel, in_specs=[pl.BlockSpec(memory_space=pl.ANY)] * len...]
  transfers between devices with their start and end apart: 2 -> 2, of which waited for: 1 -> 1; matrix products, arithmetic and copies ran while one was open for 5% -> 6% of each run, Pallas kernels for 57% -> 58%
where the time goes in v6:
time: 1200 us; the launch traced here: 1190 us
  Pallas kernels  1050 us (88%)
  matrix products  41.8 us (3%)
  local copies, waits for them, and re-layouts  39.5 us (3%)
  other arithmetic  21.9 us (2%)
  waiting for transfers between devices  15.7 us (1%)
  between operations  15.3 us (1%)
    pallas_call x9, Pallas kernels, reach(): pl.pallas_call(kernel, in_specs=[pl.BlockSpec(memory_space=pl.ANY)] * len...  929 us
    pallas_call x1, Pallas kernels, attend_backward(): pl.pallas_call(attend_backward_kernel, grid_spec=pltpu.PrefetchScalarGrid...  68.3 us
    pallas_call x1, Pallas kernels, attend_forward(): pl.pallas_call(attend_forward_kernel, grid_spec=pltpu.PrefetchScalarGridS...  38.8 us
    dot_general x9, matrix products, dot_with(): lax.dot_general(left, right, dims, preferred_element_type=jnp.float32)  35.2 us
    unnamed x119, local copies, waits for them, and re-layouts  32.5 us
  transfers between devices with their start and end apart: 2, of which 1 were waited for; matrix products, arithmetic and copies ran while one was open for 6% of the time, Pallas kernels for 58%

profile of v6, /device:TPU:0, one launch (start us, length us, event | category | flops | bytes accessed | tf_op | source)
XLA Modules:
  0.0 1188.8 jit_solution(9774011706717559973)
XLA Ops:
  10.5 41.4 %enter_kernel.1 = bf16[8,4,32,2048]{3,2,1,0:T(8,128)(2,1)S(1)} custom-call(bf16[8,32,2048]{2,1,0:T(8,128)(2,1)S(1)} %bitcast.171), custom_call_target="tpu_custom_call" | custom-call | flops 1 | bytes 1 | tf_op jit(solution)/shard_map/enter_kernel/pallas_call | solution.py:549
  56.9 11.2 front.1
  73.0 100.2 %gather_kv_kernel.1 = bf16[32,8,32,256]{3,2,1,0:T(8,128)(2,1)S(1)} custom-call(bf16[32,32,256]{2,1,0:T(8,128)(2,1)S(1)} %bitcast.175), custom_call_target="tpu_custom_call" | custom-call | flops 1 | bytes 1 | tf_op jit(solution)/shard_map/gather_kv_kernel/pallas_call | solution.py:549
  176.5 38.8 %attend_forward.1 = (f32[1024,1024]{1,0:T(8,128)}, bf16[1024,1024]{1,0:T(8,128)(2,1)S(1)}, f32[16,1,512]{2,1,0:T(1,128)S(1)}) custom-call(s32[4,16]{1,0:T(4,128)S(1)} %pad_add_fusion.2.bounds_ref, bf16[1024,1024]{1,0:T(8,128)(2,1)S(1)} %get-tuple-element.46.q_ref, s32[1024,2]{1,0:T(8,128)S(1)} %copy.66.ask_ref, ...), custom_call_target="tpu_custom_call" | custom-call | flops 12884901888 | bytes 16777216 | tf_op jit(solution)/shard_map/attend_forward/pallas_call | solution.py:207
  215.4 4.7 convolution_convert_fusion.2
  220.1 25.7 %scatter_group_kernel.2 = f32[8,32,2048]{2,1,0:T(8,128)S(1)} custom-call(bf16[8,4,32,2048]{3,2,1,0:T(8,128)(2,1)S(1)} %bitcast.170), custom_call_target="tpu_custom_call" | custom-call | flops 1 | bytes 1 | tf_op jit(solution)/shard_map/scatter_group_kernel/pallas_call | solution.py:549
  249.1 3.5 multiply_convert_fusion
  252.6 15.7 %all-gather.2.cloned.1.call-done = bf16[256,32,2048]{2,1,0:T(8,128)(2,1)} async-done(((bf16[8,32,2048]{2,1,0:T(8,128)(2,1)}), bf16[256,32,2048]{2,1,0:T(8,128)(2,1)}) %all-gather.2.cloned.1.call-update) | async-done | bytes 33554448 | tf_op jit(solution)/shard_map/all_gather | solution.py:1447
  268.3 205.2 %expert_all_kernel.1 = (bf16[8192,2048]{1,0:T(8,128)(2,1)}, bf16[8192,2048]{1,0:T(8,128)(2,1)}, bf16[8,4,8,32,2048]{4,3,2,1,0:T(8,128)(2,1)}, bf16[4096,2048]{1,...) custom-call(bf16[256,2048]{1,0:T(8,128)(2,1)} %get-tuple-element.165, ...), custom_call_target="tpu_custom_call" | custom-call | flops 1 | bytes 1 | tf_op jit(solution)/shard_map/expert_all_kernel/pallas_call | solution.py:549
  473.5 156.8 %scatter_all_kernel.1 = f32[256,2048]{1,0:T(8,128)} custom-call(bf16[8192,2048]{1,0:T(8,128)(2,1)} %get-tuple-element.49.p_ref), custom_call_target="tpu_custom_call" | custom-call | flops 1 | bytes 1 | tf_op jit(solution)/shard_map/scatter_all_kernel/pallas_call | solution.py:549
  638.4 53.6 %gather_group_kernel.1 = bf16[8,4,32,2048]{3,2,1,0:T(8,128)(2,1)S(1)} custom-call(bf16[8,32,2048]{2,1,0:T(8,128)(2,1)S(1)} %bitcast.172), custom_call_target="tpu_custom_call" | custom-call | flops 1 | bytes 1 | tf_op jit(solution)/shard_map/gather_group_kernel/pallas_call | solution.py:549
  692.0 6.0 convolution_convert_fusion.7.grad_ref
  698.0 68.3 %attend_backward.1 = (f32[1024,1024]{1,0:T(8,128)}, bf16[8192,256]{1,0:T(8,128)(2,1)}) custom-call(s32[4,16]{1,0:T(4,128)} %copy-done.22, bf16[1024,1024]{1,0:T(8,128)(2,1)} %copy-done.29, bf16[1024,1024]{1,0:T(8,128)(2,1)} %convolution_convert_fusion.7.grad_ref, f32[1024,1024]{1,0:T(8,128)} %get-tuple-element.54.exact_ref, f32[16,1,512]{2,1,0:T(1,128)} %copy-done.32, ...), custom_call_target="tpu_custom_call" | custom-call | flops 32212254720 | bytes 33554432 | tf_op jit(solution)/shard_map/attend_backward/pallas_call | solution.py:308
  768.6 96.7 %scatter_kv_kernel.1 = bf16[32,32,256]{2,1,0:T(8,128)(2,1)S(1)} custom-call(bf16[32,8,32,256]{3,2,1,0:T(8,128)(2,1)S(1)} %bitcast.169), custom_call_target="tpu_custom_call" | custom-call | flops 1 | bytes 1 | tf_op jit(solution)/shard_map/scatter_kv_kernel/pallas_call | solution.py:549
  868.7 6.2 head_back.2
  878.0 4.5 fusion.37
  883.8 49.3 %scatter_group_kernel.3 = f32[8,32,2048]{2,1,0:T(8,128)S(1)} custom-call(bf16[8,4,32,2048]{3,2,1,0:T(8,128)(2,1)S(1)} %bitcast.164), custom_call_target="tpu_custom_call" | custom-call | flops 1 | bytes 1 | tf_op jit(solution)/shard_map/scatter_group_kernel/pallas_call | solution.py:549
  935.6 4.7 convolution_convert_fusion.4
  940.3 2.9 fusion.3
  945.6 6.5 convolution_convert_fusion
  952.1 6.2 convolution_convert_fusion.1
  958.3 200.0 %finish_kernel.1 = (f32[256,1024]{1,0:T(8,128)}, f32[256,1024]{1,0:T(8,128)}, f32[256,256]{1,0:T(8,128)}, f32[34,128]{1,0:T(8,128)}, bf16[8,32,4096]{2,1,0:T(8,1...) custom-call(bf16[8,256,1024]{2,1,0:T(8,128)(2,1)} %bitcast.194, ...), custom_call_target="tpu_custom_call" | custom-call | flops 1 | bytes 1 | tf_op jit(solution)/shard_map/finish_kernel/pallas_call | solution.py:549
  1165.8 2.9 convolution_convert_fusion.3
  1169.7 6.1 copy.75
  (185 shorter events, 56.4 us)
Async XLA Ops:
  7.2 261.1 %all-gather.2.cloned.1.call-start = ((), (), s32[]{:S(2)}) async-start(), calls=%async_computation.1 | async-start | bytes 34603008 | tf_op jit(solution)/shard_map/all_gather | solution.py:1447
  9.9 1154.7 %reduce-scatter.2.cloned.1.call-start = ((), (), s32[]{:S(2)}) async-start(), calls=%async_computation.2 | async-start | bytes 34603008 | tf_op jit(solution)/shard_map/reduce_scatter | solution.py:1510
  10.5 43.8 %copy-start.49 = (s32[8]{0:T(128)S(1)}, s32[8]{0:T(128)}, u32[]{:S(2)}) copy-start(s32[8]{0:T(128)} %param.20) | copy-start | bytes 100
  56.8 11.3 copy-start.3
  56.8 11.3 copy-start.5
  73.0 103.5 %copy-start.29 = (bf16[1024,1024]{1,0:T(8,128)(2,1)}, bf16[1024,1024]{1,0:T(8,128)(2,1)S(1)}, u32[]{:S(2)}) copy-start(bf16[1024,1024]{1,0:T(8,128)(2,1)S(1)} %get-tuple-element.46.q_ref) | copy-start | bytes 6291460
  176.1 39.3 %copy-start.20 = (s32[1,8192]{1,0:T(1,128)}, s32[1,8192]{1,0:T(1,128)S(1)}, u32[]{:S(2)}) copy-start(s32[1,8192]{1,0:T(1,128)S(1)} %broadcast_in_dim_reshape.2.key_given_ref) | copy-start | bytes 98308
  176.5 38.9 %copy-start.22 = (s32[4,16]{1,0:T(4,128)}, s32[4,16]{1,0:T(4,128)S(1)}, u32[]{:S(2)}) copy-start(s32[4,16]{1,0:T(4,128)S(1)} %pad_add_fusion.2.bounds_ref) | copy-start | bytes 772
  176.5 38.9 %copy-start.50 = (bf16[1024,2048]{1,0:T(8,128)(2,1)S(1)}, bf16[1024,2048]{1,0:T(8,128)(2,1)}, u32[]{:S(2)}) copy-start(bf16[1024,2048]{1,0:T(8,128)(2,1)} %param.29) | copy-start | bytes 12582916
  215.3 4.7 copy-start.30
  215.3 4.7 copy-start.32
  638.4 53.6 %copy-start.51 = (bf16[1024,2048]{1,0:T(8,128)(2,1)S(1)}, bf16[1024,2048]{1,0:T(8,128)(2,1)}, u32[]{:S(2)}) copy-start(bf16[1024,2048]{1,0:T(8,128)(2,1)} %param.29) | copy-start | bytes 12582916
  692.0 6.0 copy-start.9
  768.5 96.8 %copy-start.4 = (f32[1024,128]{1,0:T(8,128)S(1)}, f32[1024,128]{1,0:T(8,128)}, u32[]{:S(2)}) copy-start(f32[1024,128]{1,0:T(8,128)} %copy-done.3) | copy-start | bytes 1572868
  768.5 96.8 %copy-start.6 = (f32[1024,128]{1,0:T(8,128)S(1)}, f32[1024,128]{1,0:T(8,128)}, u32[]{:S(2)}) copy-start(f32[1024,128]{1,0:T(8,128)} %copy-done.5) | copy-start | bytes 1572868
  768.5 96.8 %copy-start.19 = (f32[1024,128]{1,0:T(8,128)S(1)}, f32[1024,128]{1,0:T(8,128)}, u32[]{:S(2)}) copy-start(f32[1024,128]{1,0:T(8,128)} %copy-done.18) | copy-start | bytes 1572868
  768.6 97.8 %copy-start.8 = (f32[1024,1024]{1,0:T(8,128)S(1)}, f32[1024,1024]{1,0:T(8,128)}, u32[]{:S(2)}) copy-start(f32[1024,1024]{1,0:T(8,128)} %copy-done.7) | copy-start | bytes 12582916
  868.7 6.2 copy-start.15
  935.6 4.7 copy-start.38
  945.6 6.5 copy-start.10
  945.6 6.5 copy-start.31
  1165.8 9.9 slice-start.2
  1169.6 6.1 slice-start.3
  1169.7 8.9 slice-start
  (35 other events, 95.7 us)
Sparse Core Ops, SparseCore 0:
  11.5 256.8 all-gather.1
  630.5 396.2 reduce-scatter.1

commit v7 on v6

--- a/solution.py
+++ b/solution.py
@@ -643,7 +643,7 @@
                 for copy in z_copies(slots[step, 0, 0, 0], index, device):
                     copy.start()
 
-    relays = {1: 2, 3: 3}
+    relays = {1: 2, 4: 3}
 
     def event(number):
         where = ORDER[number]

time: 1200 us -> 1190 us (level)
  no operation moved by 1% of the time
where the time goes in v7:
time: 1190 us; the launch traced here: 1170 us
  Pallas kernels  1040 us (87%)
  matrix products  41.8 us (4%)
  local copies, waits for them, and re-layouts  39.4 us (3%)
  other arithmetic  21.9 us (2%)
  waiting for transfers between devices  18.7 us (2%)
  between operations  15.3 us (1%)
    pallas_call x9, Pallas kernels, reach(): pl.pallas_call(kernel, in_specs=[pl.BlockSpec(memory_space=pl.ANY)] * len...  925 us
    pallas_call x1, Pallas kernels, attend_backward(): pl.pallas_call(attend_backward_kernel, grid_spec=pltpu.PrefetchScalarGrid...  59.6 us
    dot_general x9, matrix products, dot_with(): lax.dot_general(left, right, dims, preferred_element_type=jnp.float32)  35.1 us
    pallas_call x1, Pallas kernels, attend_forward(): pl.pallas_call(attend_forward_kernel, grid_spec=pltpu.PrefetchScalarGridS...  34.3 us
    unnamed x119, local copies, waits for them, and re-layouts  32.4 us
  transfers between devices with their start and end apart: 2, of which 1 were waited for; matrix products, arithmetic and copies ran while one was open for 6% of the time, Pallas kernels for 58%

profile of v7, /device:TPU:0, one launch (start us, length us, event | category | flops | bytes accessed | tf_op | source)
XLA Modules:
  0.0 1174.7 jit_solution(7004521816620003887)
XLA Ops:
  10.5 41.4 %enter_kernel.1 = bf16[8,4,32,2048]{3,2,1,0:T(8,128)(2,1)S(1)} custom-call(bf16[8,32,2048]{2,1,0:T(8,128)(2,1)S(1)} %bitcast.171), custom_call_target="tpu_custom_call" | custom-call | flops 1 | bytes 1 | tf_op jit(solution)/shard_map/enter_kernel/pallas_call | solution.py:549
  56.9 11.2 front.1
  73.0 100.2 %gather_kv_kernel.1 = bf16[32,8,32,256]{3,2,1,0:T(8,128)(2,1)S(1)} custom-call(bf16[32,32,256]{2,1,0:T(8,128)(2,1)S(1)} %bitcast.175), custom_call_target="tpu_custom_call" | custom-call | flops 1 | bytes 1 | tf_op jit(solution)/shard_map/gather_kv_kernel/pallas_call | solution.py:549
  176.5 34.3 %attend_forward.1 = (f32[1024,1024]{1,0:T(8,128)}, bf16[1024,1024]{1,0:T(8,128)(2,1)S(1)}, f32[16,1,512]{2,1,0:T(1,128)S(1)}) custom-call(s32[4,16]{1,0:T(4,128)S(1)} %pad_add_fusion.2.bounds_ref, bf16[1024,1024]{1,0:T(8,128)(2,1)S(1)} %get-tuple-element.46.q_ref, s32[1024,2]{1,0:T(8,128)S(1)} %copy.66.ask_ref, ...), custom_call_target="tpu_custom_call" | custom-call | flops 12884901888 | bytes 16777216 | tf_op jit(solution)/shard_map/attend_forward/pallas_call | solution.py:207
  210.8 4.7 convolution_convert_fusion.2
  215.5 27.3 %scatter_group_kernel.2 = f32[8,32,2048]{2,1,0:T(8,128)S(1)} custom-call(bf16[8,4,32,2048]{3,2,1,0:T(8,128)(2,1)S(1)} %bitcast.170), custom_call_target="tpu_custom_call" | custom-call | flops 1 | bytes 1 | tf_op jit(solution)/shard_map/scatter_group_kernel/pallas_call | solution.py:549
  246.1 3.5 multiply_convert_fusion
  249.7 18.7 %all-gather.2.cloned.1.call-done = bf16[256,32,2048]{2,1,0:T(8,128)(2,1)} async-done(((bf16[8,32,2048]{2,1,0:T(8,128)(2,1)}), bf16[256,32,2048]{2,1,0:T(8,128)(2,1)}) %all-gather.2.cloned.1.call-update) | async-done | bytes 33554448 | tf_op jit(solution)/shard_map/all_gather | solution.py:1447
  268.3 205.2 %expert_all_kernel.1 = (bf16[8192,2048]{1,0:T(8,128)(2,1)}, bf16[8192,2048]{1,0:T(8,128)(2,1)}, bf16[8,4,8,32,2048]{4,3,2,1,0:T(8,128)(2,1)}, bf16[4096,2048]{1,...) custom-call(bf16[256,2048]{1,0:T(8,128)(2,1)} %get-tuple-element.165, ...), custom_call_target="tpu_custom_call" | custom-call | flops 1 | bytes 1 | tf_op jit(solution)/shard_map/expert_all_kernel/pallas_call | solution.py:549
  473.5 148.4 %scatter_all_kernel.1 = f32[256,2048]{1,0:T(8,128)} custom-call(bf16[8192,2048]{1,0:T(8,128)(2,1)} %get-tuple-element.49.p_ref), custom_call_target="tpu_custom_call" | custom-call | flops 1 | bytes 1 | tf_op jit(solution)/shard_map/scatter_all_kernel/pallas_call | solution.py:549
  630.0 53.6 %gather_group_kernel.1 = bf16[8,4,32,2048]{3,2,1,0:T(8,128)(2,1)S(1)} custom-call(bf16[8,32,2048]{2,1,0:T(8,128)(2,1)S(1)} %bitcast.172), custom_call_target="tpu_custom_call" | custom-call | flops 1 | bytes 1 | tf_op jit(solution)/shard_map/gather_group_kernel/pallas_call | solution.py:549
  683.7 6.0 convolution_convert_fusion.7.grad_ref
  689.7 59.6 %attend_backward.1 = (f32[1024,1024]{1,0:T(8,128)}, bf16[8192,256]{1,0:T(8,128)(2,1)}) custom-call(s32[4,16]{1,0:T(4,128)} %copy-done.22, bf16[1024,1024]{1,0:T(8,128)(2,1)} %copy-done.29, bf16[1024,1024]{1,0:T(8,128)(2,1)} %convolution_convert_fusion.7.grad_ref, f32[1024,1024]{1,0:T(8,128)} %get-tuple-element.54.exact_ref, f32[16,1,512]{2,1,0:T(1,128)} %copy-done.32, ...), custom_call_target="tpu_custom_call" | custom-call | flops 32212254720 | bytes 33554432 | tf_op jit(solution)/shard_map/attend_backward/pallas_call | solution.py:308
  751.5 97.6 %scatter_kv_kernel.1 = bf16[32,32,256]{2,1,0:T(8,128)(2,1)S(1)} custom-call(bf16[32,8,32,256]{3,2,1,0:T(8,128)(2,1)S(1)} %bitcast.169), custom_call_target="tpu_custom_call" | custom-call | flops 1 | bytes 1 | tf_op jit(solution)/shard_map/scatter_kv_kernel/pallas_call | solution.py:549
  852.5 6.2 head_back.2
  861.7 4.5 fusion.37
  867.5 48.9 %scatter_group_kernel.3 = f32[8,32,2048]{2,1,0:T(8,128)S(1)} custom-call(bf16[8,4,32,2048]{3,2,1,0:T(8,128)(2,1)S(1)} %bitcast.164), custom_call_target="tpu_custom_call" | custom-call | flops 1 | bytes 1 | tf_op jit(solution)/shard_map/scatter_group_kernel/pallas_call | solution.py:549
  919.1 4.6 convolution_convert_fusion.4
  923.7 2.9 fusion.3
  929.0 6.5 convolution_convert_fusion
  935.5 6.2 convolution_convert_fusion.1
  941.7 202.5 %finish_kernel.1 = (f32[256,1024]{1,0:T(8,128)}, f32[256,1024]{1,0:T(8,128)}, f32[256,256]{1,0:T(8,128)}, f32[34,128]{1,0:T(8,128)}, bf16[8,32,4096]{2,1,0:T(8,1...) custom-call(bf16[8,256,1024]{2,1,0:T(8,128)(2,1)} %bitcast.194, ...), custom_call_target="tpu_custom_call" | custom-call | flops 1 | bytes 1 | tf_op jit(solution)/shard_map/finish_kernel/pallas_call | solution.py:549
  1151.6 2.9 convolution_convert_fusion.3
  1155.5 6.1 copy.75
  (185 shorter events, 56.3 us)
Async XLA Ops:
  7.2 261.1 %all-gather.2.cloned.1.call-start = ((), (), s32[]{:S(2)}) async-start(), calls=%async_computation.1 | async-start | bytes 34603008 | tf_op jit(solution)/shard_map/all_gather | solution.py:1447
  9.9 1140.6 %reduce-scatter.2.cloned.1.call-start = ((), (), s32[]{:S(2)}) async-start(), calls=%async_computation.2 | async-start | bytes 34603008 | tf_op jit(solution)/shard_map/reduce_scatter | solution.py:1510
  10.5 43.8 %copy-start.49 = (s32[8]{0:T(128)S(1)}, s32[8]{0:T(128)}, u32[]{:S(2)}) copy-start(s32[8]{0:T(128)} %param.20) | copy-start | bytes 100
  56.8 11.3 copy-start.3
  56.8 11.3 copy-start.5
  73.0 103.5 %copy-start.29 = (bf16[1024,1024]{1,0:T(8,128)(2,1)}, bf16[1024,1024]{1,0:T(8,128)(2,1)S(1)}, u32[]{:S(2)}) copy-start(bf16[1024,1024]{1,0:T(8,128)(2,1)S(1)} %get-tuple-element.46.q_ref) | copy-start | bytes 6291460
  176.1 34.7 %copy-start.20 = (s32[1,8192]{1,0:T(1,128)}, s32[1,8192]{1,0:T(1,128)S(1)}, u32[]{:S(2)}) copy-start(s32[1,8192]{1,0:T(1,128)S(1)} %broadcast_in_dim_reshape.2.key_given_ref) | copy-start | bytes 98308
  176.5 34.3 %copy-start.22 = (s32[4,16]{1,0:T(4,128)}, s32[4,16]{1,0:T(4,128)S(1)}, u32[]{:S(2)}) copy-start(s32[4,16]{1,0:T(4,128)S(1)} %pad_add_fusion.2.bounds_ref) | copy-start | bytes 772
  176.5 34.3 %copy-start.50 = (bf16[1024,2048]{1,0:T(8,128)(2,1)S(1)}, bf16[1024,2048]{1,0:T(8,128)(2,1)}, u32[]{:S(2)}) copy-start(bf16[1024,2048]{1,0:T(8,128)(2,1)} %param.29) | copy-start | bytes 12582916
  210.8 4.7 copy-start.30
  210.8 4.7 copy-start.32
  630.0 53.7 %copy-start.51 = (bf16[1024,2048]{1,0:T(8,128)(2,1)S(1)}, bf16[1024,2048]{1,0:T(8,128)(2,1)}, u32[]{:S(2)}) copy-start(bf16[1024,2048]{1,0:T(8,128)(2,1)} %param.29) | copy-start | bytes 12582916
  683.7 6.0 copy-start.9
  751.5 97.7 %copy-start.4 = (f32[1024,128]{1,0:T(8,128)S(1)}, f32[1024,128]{1,0:T(8,128)}, u32[]{:S(2)}) copy-start(f32[1024,128]{1,0:T(8,128)} %copy-done.3) | copy-start | bytes 1572868
  751.5 97.7 %copy-start.6 = (f32[1024,128]{1,0:T(8,128)S(1)}, f32[1024,128]{1,0:T(8,128)}, u32[]{:S(2)}) copy-start(f32[1024,128]{1,0:T(8,128)} %copy-done.5) | copy-start | bytes 1572868
  751.5 97.7 %copy-start.19 = (f32[1024,128]{1,0:T(8,128)S(1)}, f32[1024,128]{1,0:T(8,128)}, u32[]{:S(2)}) copy-start(f32[1024,128]{1,0:T(8,128)} %copy-done.18) | copy-start | bytes 1572868
  751.5 98.7 %copy-start.8 = (f32[1024,1024]{1,0:T(8,128)S(1)}, f32[1024,1024]{1,0:T(8,128)}, u32[]{:S(2)}) copy-start(f32[1024,1024]{1,0:T(8,128)} %copy-done.7) | copy-start | bytes 12582916
  852.5 6.2 copy-start.15
  919.1 4.7 copy-start.38
  929.0 6.5 copy-start.10
  929.0 6.5 copy-start.31
  1151.6 9.9 slice-start.2
  1155.5 6.1 slice-start.3
  1155.5 8.9 slice-start
  (35 other events, 95.6 us)
Sparse Core Ops, SparseCore 0:
  11.5 256.8 all-gather.1
  622.1 401.9 reduce-scatter.1
